TPU v7x, 256 devices: a whole 4x4x8 slice. The times are simulated.
256 devices in a mesh: grp: 16 (over y, z_lo), tp: 16 (over x, z_hi, core).
Axes of the slice: x: 4, y: 4, z: 8 (z_hi: 2, z_lo: 4; z = z_hi * 4 + z_lo), core: 2. Of those that a mesh axis runs over, the one named last changes fastest.
Arguments:
- teacher_rows: bfloat16 [32768, 8192], P(('grp', 'tp')), may hold values from -6 to 6
- student_rows: bfloat16 [32768, 2048], P(('grp', 'tp')), may hold values from -24 to 24
- proj: bfloat16 [2048, 8192], P(None, 'tp'), may hold values from -0.125 to 0.125
Outputs:
- grad_proj: float32 [2048, 8192], P('grp', 'tp')
- grad_student: bfloat16 [32768, 2048], P(('grp', 'tp'))
All inputs are finite; a program needn't handle non-finite values.
Results may differ from a plain program's by a relative error of at most 0.019.
Values may be sent and summed in bfloat16 or wider, within the bound.
No kernel may reach another device: no remote copies, remote signals or barrier semaphores. Data moves between devices by JAX's collectives and lax.ppermute only.
A program may use at most 192 MiB of HBM per device.

v0:
```python
import math

import jax
import jax.numpy as jnp
from jax import lax
from jax.sharding import PartitionSpec as P


def body(teacher_rows, student_rows, proj):
    groups = lax.axis_size("grp")
    col_groups = lax.axis_size("tp")
    tok_dev = student_rows.shape[0]
    factor = 1.0 / math.sqrt(tok_dev * groups * col_groups)
    teacher_local = lax.all_to_all(teacher_rows, "tp", split_axis=1, concat_axis=0, tiled=True)
    local_rows = lax.all_gather(student_rows, "tp", axis=0, tiled=True)
    predicted = jnp.dot(local_rows, proj, preferred_element_type=jnp.float32)
    error = (predicted - teacher_local.astype(jnp.float32)).astype(jnp.bfloat16)
    grad_proj = (
        lax.psum_scatter(
            lax.dot_general(
                local_rows, error, (((0,), (0,)), ((), ())), preferred_element_type=jnp.float32
            ).astype(jnp.bfloat16),
            "grp",
            scatter_dimension=0,
            tiled=True,
        ).astype(jnp.float32)
        * factor
    )
    grad_student = lax.psum_scatter(
        lax.dot_general(
            error, proj, (((1,), (1,)), ((), ())), preferred_element_type=jnp.float32
        ).astype(jnp.bfloat16),
        "tp",
        scatter_dimension=0,
        tiled=True,
    )
    return (grad_proj, grad_student)


def solution(mesh):
    placed = (P(("grp", "tp"), None), P(("grp", "tp"), None), P(None, "tp"))
    return jax.shard_map(
        body,
        mesh=mesh,
        in_specs=placed,
        out_specs=(P("grp", "tp"), P(("grp", "tp"), None)),
        check_vma=False,
    )
```

profile of v0, /device:TPU:32, one launch (start us, length us, event | category | flops | bytes accessed | tf_op | source)
XLA Modules:
  0.0 404.3 jit_solution(12627949948478922832)
XLA Ops:
  7.2 0.0 copy-start
  7.2 0.0 all-gather.2.cloned.1.call-start
  7.2 0.7 all-gather.2.cloned.1.call-update
  7.9 0.0 reduce-scatter.7.cloned.1.call-start
  8.0 1.8 copy.13
  9.8 75.3 %all_to_all.13 = bf16[128,16,512]{2,0,1:T(8,128)(2,1)} all-to-all(bf16[128,16,512]{2,0,1:T(8,128)(2,1)S(1)} %bitcast.19), channel_id=1, replica_groups=mesh['grp'=16,'tp'=16] {'tp'}, dimensions={1} | all-to-all | bytes 4194304 | tf_op jit(solution)/shard_map/all_to_all | solution.py:14
  85.1 61.6 %all-gather.2.cloned.1.call-done = bf16[2048,2048]{1,0:T(8,128)(2,1)} async-done(((bf16[128,2048]{1,0:T(8,128)(2,1)}), bf16[2048,2048]{1,0:T(8,128)(2,1)}) %all-gather.2.cloned.1.call-update) | async-done | bytes 8388624 | tf_op jit(solution)/shard_map/all_gather | solution.py:15
  146.7 0.0 copy-done
  146.7 0.0 copy-start.1
  146.7 8.6 %fusion = bf16[2048,512]{1,0:T(8,128)(2,1)S(1)} fusion(bf16[2048,2048]{1,0:T(8,128)(2,1)} %all-gather.2.cloned.1.call-done, bf16[2048,512]{1,0:T(8,128)(2,1)S(1)} %copy-done, bf16[128,16,512]{2,0,1:T(8,128)(2,1)} %all_to_all.13), kind=kOutput, calls=%fused_computation.2 | convolution fusion | flops 4298113024 | bytes 14680064 | tf_op jit(solution)/shard_map/dot_general | solution.py:16
  155.3 0.0 copy-start.2
  155.3 1.3 copy-done.2
  156.7 0.0 copy-done.1
  156.7 5.7 %fusion.1 = bf16[2048,512]{0,1:T(8,128)(2,1)} fusion(bf16[2048,512]{1,0:T(8,128)(2,1)S(1)} %fusion, bf16[2048,2048]{1,0:T(8,128)(2,1)S(1)} %copy-done.1), kind=kOutput, calls=%fused_computation.4 | convolution fusion | flops 4296015872 | bytes 12582912 | tf_op jit(solution)/shard_map/dot_general | solution.py:20
  162.4 3.9 copy.9
  166.3 0.0 reduce-scatter.7.cloned.1.call-update
  166.4 0.0 reduce-scatter.5.cloned.1.call-start
  166.4 8.4 %convolution_convert_fusion = bf16[2048,2048]{1,0:T(8,128)(2,1)} fusion(bf16[2048,512]{1,0:T(8,128)(2,1)} %copy-done.2, bf16[2048,512]{1,0:T(8,128)(2,1)S(1)} %copy-done), kind=kOutput, calls=%fused_computation | convolution fusion | flops 4299161600 | bytes 12582912 | tf_op jit(solution)/shard_map/dot_general | solution.py:30
  174.8 0.0 reduce-scatter.5.cloned.1.call-update
  174.8 74.7 %reduce-scatter.7.cloned.1.call-done = bf16[128,512]{1,0:T(8,128)(2,1)} async-done(((bf16[2048,512]{1,0:T(8,128)(2,1)}), bf16[128,512]{1,0:T(8,128)(2,1)}) %reduce-scatter.7.cloned.1.call-update) | async-done | bytes 131088
  249.5 1.0 copy.10
  250.5 0.8 copy.8
  251.4 146.4 %reduce-scatter.5.cloned.1.call-done = bf16[128,2048]{1,0:T(8,128)(2,1)} async-done(((bf16[2048,2048]{1,0:T(8,128)(2,1)}), bf16[128,2048]{1,0:T(8,128)(2,1)}) %reduce-scatter.5.cloned.1.call-update) | async-done | bytes 524304 | tf_op jit(solution)/shard_map/reduce_scatter | solution.py:29
  (1 shorter events, 0.0 us)
Async XLA Ops:
  7.2 139.5 %copy-start = (bf16[2048,512]{1,0:T(8,128)(2,1)S(1)}, bf16[2048,512]{1,0:T(8,128)(2,1)}, u32[]{:S(2)}) copy-start(bf16[2048,512]{1,0:T(8,128)(2,1)} %param.5) | copy-start | bytes 6291460
  7.2 139.5 %all-gather.2.cloned.1.call-start = ((), (), s32[]{:S(2)}) async-start(), calls=%async_computation.3 | async-start | bytes 8912896 | tf_op jit(solution)/shard_map/all_gather | solution.py:15
  7.9 241.6 %reduce-scatter.7.cloned.1.call-start = ((), (), s32[]{:S(2)}) async-start(), calls=%async_computation.5 | async-start | bytes 2228224
  146.7 10.0 %copy-start.1 = (bf16[2048,2048]{1,0:T(8,128)(2,1)S(1)}, bf16[2048,2048]{1,0:T(8,128)(2,1)}, u32[]{:S(2)}) copy-start(bf16[2048,2048]{1,0:T(8,128)(2,1)} %all-gather.2.cloned.1.call-done) | copy-start | bytes 25165828
  155.3 1.4 copy-start.2
  166.4 231.4 %reduce-scatter.5.cloned.1.call-start = ((), (), s32[]{:S(2)}) async-start(), calls=%async_computation.4 | async-start | bytes 8912896 | tf_op jit(solution)/shard_map/reduce_scatter | solution.py:29
Sparse Core Ops, SparseCore 0:
  10.7 135.9 all-gather.1
  166.5 82.9 reduce-scatter.6
  254.7 142.9 reduce-scatter.4
where the time goes:
time: 406 us; the launch traced here: 404 us
  waiting for transfers between devices  283 us (70%)
  blocking collectives  75.3 us (19%)
  matrix products  22.7 us (6%)
  between operations  13.8 us (3%)
  local copies, waits for them, and re-layouts  8.96 us (2%)
    reduce_scatter x1, waiting for transfers between devices, body(): lax.psum_scatter(lax.dot_general(error, proj, (((1,), (1,)), ((), ())), p...  146 us
    unnamed x4, waiting for transfers between devices  75.4 us
    all_to_all x1, blocking collectives, body(): lax.all_to_all(teacher_rows, 'tp', split_axis=1, concat_axis=0, tiled=True)  75.3 us
    all_gather x1, waiting for transfers between devices, body(): local_rows = lax.all_gather(student_rows, 'tp', axis=0, tiled=True)  61.6 us
    dot_general x1, matrix products, body(): predicted = jnp.dot(local_rows, proj, preferred_element_type=jnp.float32)  8.61 us
    dot_general x1, matrix products, body(): lax.dot_general(error, proj, (((1,), (1,)), ((), ())), preferred_element_...  8.41 us
  transfers between devices with their start and end apart: 3, of which 3 were waited for; matrix products, arithmetic and copies ran while one was open for 3% of the time, Pallas kernels for 0%

commit v1 on v0

v1 whole, which is shorter than its diff:
```python
import functools
import math

import jax
import jax.numpy as jnp
from jax import lax
from jax.experimental import pallas as pl
from jax.experimental.pallas import tpu as pltpu
from jax.sharding import Mesh
from jax.sharding import PartitionSpec as P

F32 = jnp.float32
BF16 = jnp.bfloat16
ALL = ("y", "zl", "x", "zh", "c")
ANY = pl.BlockSpec(memory_space=pl.ANY)
VMEM = pl.BlockSpec(memory_space=pltpu.VMEM)
N = 4
TOK, DS, WIDTH = 128, 2048, 512
BLOCK = DS // N
ROWS = BLOCK // N
BIG = 10**11


def shift(array, axis, by):
    n = lax.axis_size(axis)
    return lax.ppermute(array, axis, [(i, (i + by) % n) for i in range(n)])


def after(value, *done):
    return lax.optimization_barrier((value, *done))[0]


def index(axis):
    return lax.axis_index(axis)


def columns(x_at, zh_at, c_at):
    return pl.ds(pl.multiple_of(((x_at * 2 + zh_at) * 2 + c_at) * WIDTH, WIDTH), WIDTH)


def place(at, size):
    return pl.ds(pl.multiple_of(at * size, size), size)


def pieces(zh, c):
    return ((zh, c), (zh, 1 - c), (1 - zh, c), (1 - zh, 1 - c))


def dot(a, b, da, db):
    return lax.dot_general(a, b, (((da,), (db,)), ((), ())), preferred_element_type=F32)


def call(kernel, ins, out_shapes, scratch, mib, flops=1, out_specs=None, in_specs=None):
    return pl.pallas_call(
        kernel,
        in_specs=in_specs or [ANY] * len(ins),
        out_specs=out_specs or [ANY] * len(out_shapes),
        out_shape=[jax.ShapeDtypeStruct(s, t) for s, t in out_shapes],
        scratch_shapes=scratch,
        cost_estimate=pl.CostEstimate(flops=flops, bytes_accessed=1, transcendentals=0),
        compiler_params=pltpu.CompilerParams(vmem_limit_bytes=mib * 2**20),
    )(*ins)


def run(pairs, sems, first=0):
    copies = [
        pltpu.make_async_copy(src, dst, sems.at[first + i]) for i, (src, dst) in enumerate(pairs)
    ]
    for copy in copies:
        copy.start()
    return copies


def cut_kernel(proj, part, sem):
    copy = pltpu.make_async_copy(proj.at[place(index("y"), BLOCK), :], part, sem)
    copy.start()
    copy.wait()


def cut(proj):
    return call(
        cut_kernel,
        (proj,),
        [((BLOCK, WIDTH), BF16)],
        [pltpu.SemaphoreType.DMA],
        4,
        out_specs=[VMEM],
    )[0]


def split_kernel(teacher, o1, o3, o2, sems):
    x, zh, c = (index(a) for a in ("x", "zh", "c"))
    pairs = []
    for s, out in ((1, o1), (3, o3), (2, o2)):
        for j, (zh_at, c_at) in enumerate(pieces(zh, c)):
            pairs.append(
                (
                    teacher.at[:, columns((x + s) % N, zh_at, c_at)],
                    out.at[:, pl.ds(j * WIDTH, WIDTH)],
                )
            )
    for copy in run(pairs, sems):
        copy.wait()


def split(teacher):
    return call(
        split_kernel,
        (teacher,),
        [((TOK, 4 * WIDTH), BF16)] * 3,
        [pltpu.SemaphoreType.DMA((12,))],
        8,
        BIG,
        out_specs=[VMEM] * 3,
    )


def join_kernel(own, p1, p2, p3, out, sems):
    y = index("y")
    pairs = [
        (ref, out.at[place((y + N - s) % N, BLOCK), :]) for s, ref in enumerate((own, p1, p2, p3))
    ]
    for copy in run(pairs, sems):
        copy.wait()


def join(parts):
    return call(
        join_kernel,
        parts,
        [((DS, WIDTH), BF16)],
        [pltpu.SemaphoreType.DMA((4,))],
        8,
        out_specs=[VMEM],
    )[0]


def error_kernel(half, s0, s1, s2, s3, w_own, w_other, teacher, t1, t2, t3, *rest):
    error, grad, students, weights, targets, errors, grads, sems, out_sems = rest
    x, zh, c = (index(a) for a in ("x", "zh", "c"))
    zh_at = zh if half == 0 else 1 - zh
    spots = [place((x + N - s) % N, TOK) for s in range(N)]
    first = run(
        [(ref, students.at[spot, :]) for ref, spot in zip((s0, s1, s2, s3), spots)]
        + [(w_other, weights.at[1])],
        sems,
    )
    second = run(
        [
            (ref.at[:, pl.ds(half * 2 * WIDTH, 2 * WIDTH)], targets.at[spot, :])
            for ref, spot in zip((t1, t2, t3), spots[1:])
        ]
        + [
            (
                teacher.at[:, columns(x, zh_at, c_at)],
                targets.at[spots[0], pl.ds(j * WIDTH, WIDTH)],
            )
            for j, c_at in enumerate((c, 1 - c))
        ]
        + [(w_own, weights.at[0])],
        sems,
        5,
    )
    for copy in first + second[:-1]:
        copy.wait()

    def one(j):
        for n in range(2):
            cols = pl.ds(j * WIDTH + n * 256, 256)
            predicted = dot(students[...], weights[j, :, pl.ds(n * 256, 256)], 1, 0)
            errors[:, cols] = (predicted - targets[:, cols].astype(F32)).astype(BF16)

    one(1)
    turned = errors[:, pl.ds(WIDTH, WIDTH)].T
    for n in range(N):
        cols = pl.ds(n * BLOCK, BLOCK)
        grads[:, cols] = dot(turned, students[:, cols], 1, 0).astype(BF16)
    out = run([(grads, grad)], out_sems)
    second[-1].wait()
    one(0)
    out += run([(errors, error)], out_sems, 1)
    for copy in out:
        copy.wait()


def error_and_other(half, students, w_own, w_other, teacher, targets):
    n_tok = N * TOK
    return call(
        functools.partial(error_kernel, half),
        (*students, w_own, w_other, teacher, *targets),
        [((n_tok, 2 * WIDTH), BF16), ((WIDTH, DS), BF16)],
        [
            pltpu.VMEM((n_tok, DS), BF16),
            pltpu.VMEM((2, DS, WIDTH), BF16),
            pltpu.VMEM((n_tok, 2 * WIDTH), BF16),
            pltpu.VMEM((n_tok, 2 * WIDTH), BF16),
            pltpu.VMEM((WIDTH, DS), BF16),
            pltpu.SemaphoreType.DMA((11,)),
            pltpu.SemaphoreType.DMA((2,)),
        ],
    18,
        BIG,
    )


def own_kernel(order, s0, s1, s2, s3, error, there, *rest):
    ins, rest = rest[: len(order) - 1], rest[len(order) - 1 :]
    outs, rest = rest[: 2 if order == (2,) else 3], rest[2 if order == (2,) else 3 :]
    students, errors, theirs, passed, grads, sems, there_sems, out_sems = rest
    x, y = index("x"), index("y")
    spots = [place((x + N - s) % N, TOK) for s in range(N)]
    begun = run([(error.at[:, pl.ds(0, WIDTH)], errors)], sems)
    begun += run([(ref, passed.at[i]) for i, ref in enumerate(ins)], sems, 13)
    loads = []
    for k, s in enumerate(order):
        cols = place((y + s) % N, BLOCK)
        loads.append(
            run(
                [
                    (ref.at[:, cols], students.at[k, spot, :])
                    for ref, spot in zip((s0, s1, s2, s3), spots)
                ],
                sems,
                1 + 4 * k,
            )
            + run([(there.at[:, cols], theirs.at[k])], there_sems, k)
        )
    for copy in begun:
        copy.wait()
    turned = errors[...].T
    out = []
    half = WIDTH // 2
    for k, s in enumerate(order):
        for copy in loads[k]:
            copy.wait()
        total = dot(turned, students[k], 1, 0) + theirs[k].astype(F32)
        if s == 1:
            grads[k, :half] = (total[:half] + passed[0].astype(F32)).astype(BF16)
            grads[k, half:] = total[half:].astype(BF16)
        elif s == 3:
            grads[k, :half] = total[:half].astype(BF16)
            grads[k, half:] = (total[half:] + passed[1].astype(F32)).astype(BF16)
        else:
            grads[k] = total.astype(BF16)
        if s == 2:
            out += run(
                [(grads.at[k, :half], outs[0]), (grads.at[k, half:], outs[1])], out_sems
            )
        else:
            out += run([(grads.at[k], outs[k])], out_sems, k)
    for copy in out:
        copy.wait()


def own_and_sum(order, students, error, there, ins=()):
    n_tok, n = N * TOK, len(order)
    halves = [((WIDTH // 2, BLOCK), BF16)] * 2
    return call(
        functools.partial(own_kernel, order),
        (*students, error, there, *ins),
        halves if order == (2,) else [((WIDTH, BLOCK), BF16)] * 3,
        [
            pltpu.VMEM((n, n_tok, BLOCK), BF16),
            pltpu.VMEM((n_tok, WIDTH), BF16),
            pltpu.VMEM((n, WIDTH, BLOCK), BF16),
            pltpu.VMEM((2, WIDTH // 2, BLOCK), BF16),
            pltpu.VMEM((n, WIDTH, BLOCK), BF16),
            pltpu.SemaphoreType.DMA((15,)),
            pltpu.SemaphoreType.DMA((3,)),
            pltpu.SemaphoreType.DMA((3,)),
        ],
        12,
    )


def student_kernel(near, far, wa, wb, wc, wd, o0, o1, o3, o2, *rest):
    errors, weights, grads, sems, out_sems = rest
    x = index("x")
    loads = run([(near, errors.at[0]), (far, errors.at[1])], sems)
    loads += run([(w, weights.at[i]) for i, w in enumerate((wa, wb, wc, wd))], sems, 2)
    for copy in loads:
        copy.wait()
    stores = []
    for n in range(N):
        cols = pl.ds(n * BLOCK, BLOCK)
        total = None
        for p in range(4):
            term = dot(errors[p // 2, :, pl.ds(p % 2 * WIDTH, WIDTH)], weights[p, cols, :], 1, 1)
            total = term if total is None else total + term
        grads[:, cols] = total.astype(BF16)
        stores += run(
            [
                (grads.at[place((x + s) % N, TOK), cols], out.at[:, cols])
                for s, out in enumerate((o0, o1, o2, o3))
            ],
            out_sems,
            4 * n,
        )
    for copy in stores:
        copy.wait()


def student_part(near, far, weights):
    n_tok = N * TOK
    return call(
        student_kernel,
        (near, far, *weights),
        [((TOK, DS), BF16)] * 4,
        [
            pltpu.VMEM((2, n_tok, 2 * WIDTH), BF16),
            pltpu.VMEM((4, DS, WIDTH), BF16),
            pltpu.VMEM((n_tok, DS), BF16),
            pltpu.SemaphoreType.DMA((6,)),
            pltpu.SemaphoreType.DMA((16,)),
        ],
        20,
        BIG,
    )


def y_kernel(a, b, c, *outs):
    zl = index("zl")
    for s, out in zip((0, 1, 3, 2), outs):
        cols = place((zl + s) % N, ROWS)
        total = a[:, cols].astype(F32) + b[:, cols].astype(F32) + c[:, cols].astype(F32)
        out[...] = total.astype(out.dtype)


def z_kernel(own, p1, p2, p3, out):
    total = own[...] + p1[...].astype(F32) + p2[...].astype(F32) + p3[...].astype(F32)
    out[...] = total.astype(BF16)


def final_kernel(own, p1, p2, p3, far, out):
    total = own[...] + p1[...].astype(F32) + p2[...].astype(F32) + p3[...].astype(F32)
    out[...] = (total + far[...].astype(F32)).T * (1.0 / math.sqrt(TOK * 256))


def student_sum_kernel(own, p1, p2, p3, out):
    total = own[...].astype(F32) + p1[...].astype(F32)
    out[...] = (total + p2[...].astype(F32) + p3[...].astype(F32)).astype(BF16)


def in_vmem(kernel, ins, outs):
    return call(kernel, ins, outs, [], 8, in_specs=[VMEM] * len(ins), out_specs=[VMEM] * len(outs))


def over(axis, blocks, *done):
    got = {s: shift(after(b, *done), axis, s) for s, b in zip((1, 3, 2), blocks)}
    return [got[s] for s in (1, 2, 3)]


def body(teacher, student, proj):
    students = [student] + over("x", [student] * 3)
    part = shift(cut(proj), "zh", 1)
    proj_b = shift(proj, "c", 1)
    sends = split(after(teacher, *students[1:]))
    targets = over("x", sends)

    proj_c = join([part, *over("y", [part] * 3)])
    proj_d = shift(proj_c, "c", 1)

    near, near_other = error_and_other(0, students, after(proj, proj_c), proj_b, teacher, targets)
    near_there = shift(near_other, "c", 1)
    far, far_other = error_and_other(1, students, after(proj_c, near), proj_d, teacher, targets)
    far_there = shift(far_other, "c", 1)

    blocks = own_and_sum((2,), students, near, after(near_there, far))
    near_in = [shift(blocks[0], "y", 1), shift(blocks[1], "y", 3)]
    partial = student_part(near, far, (proj, proj_b, proj_c, after(proj_d, *blocks)))
    blocks = own_and_sum((1, 3, 0), students, near, after(near_there, partial[0]), near_in)
    near_y = [blocks[2], shift(blocks[0], "y", 1), shift(blocks[1], "y", 3)]
    blocks = own_and_sum((2,), students, far, after(far_there, *blocks))
    far_in = [shift(blocks[0], "y", 1), shift(blocks[1], "y", 3)]
    back2 = shift(after(partial[3], *blocks), "x", 2)
    blocks = own_and_sum((1, 3, 0), students, far, far_there, far_in)

    def over_y(terms):
        return in_vmem(
            y_kernel, terms, [((WIDTH, ROWS), F32)] + [((WIDTH, ROWS), BF16)] * 3
        )

    near_z = over_y(near_y)
    ready = after(blocks[0], *near_z), after(blocks[1], *near_z)
    far_y = [blocks[2], shift(ready[0], "y", 1), shift(ready[1], "y", 3)]
    near_terms = [near_z[0]] + over("zl", near_z[1:])
    back1 = shift(after(partial[1], *blocks), "x", 1)
    back3 = shift(after(partial[2], *blocks), "x", 3)
    far_z = over_y([after(far_y[0], back1, back2, back3, *near_terms), *far_y[1:]])
    far_terms = [far_z[0]] + over("zl", far_z[1:])
    far_part = in_vmem(z_kernel, far_terms, [((WIDTH, ROWS), BF16)])[0]
    far_part = shift(far_part, "zh", 1)
    grad_student = in_vmem(
        student_sum_kernel, [partial[0], back1, back2, back3], [((TOK, DS), BF16)]
    )[0]
    grad_proj = in_vmem(final_kernel, [*near_terms, far_part], [((ROWS, WIDTH), F32)])[0]
    return grad_proj, grad_student


def solution(mesh):
    fine = Mesh(mesh.devices.reshape(4, 4, 4, 2, 2), ALL)
    tokens = P(ALL, None)
    return jax.shard_map(
        body,
        mesh=fine,
        in_specs=(tokens, tokens, P(None, ("x", "zh", "c"))),
        out_specs=(P(("y", "zl"), ("x", "zh", "c")), tokens),
        check_vma=False,
    )
```

time: 406 us -> 165 us (0.41)
  waiting for transfers between devices: 283 us -> 80.5 us
  blocking collectives: 75.3 us -> 0 us
  starting transfers between devices: 0.12 us -> 55.6 us
  Pallas kernels: 0 us -> 27.8 us
  matrix products: 22.7 us -> 0 us
  between operations: 13.8 us -> 0.81 us
  local copies, waits for them, and re-layouts: 8.96 us -> 0.01 us
    reduce_scatter x1 -> x0, waiting for transfers between devices: 146 us -> none  [body(): lax.psum_scatter(lax.dot_general(error, proj, (((1,), (1,)), ((), ())), p...]
    ppermute x0 -> x32, waiting for transfers between devices: none -> 80.5 us  [shift(): return lax.ppermute(array, axis, [(i, (i + by) % n) for i in range(n)])]
    unnamed x4 -> x0, waiting for transfers between devices: 75.4 us -> none
    all_to_all x1 -> x0, blocking collectives: 75.3 us -> none  [body(): lax.all_to_all(teacher_rows, 'tp', split_axis=1, concat_axis=0, tiled=True)]
    all_gather x1 -> x0, waiting for transfers between devices: 61.6 us -> none  [body(): local_rows = lax.all_gather(student_rows, 'tp', axis=0, tiled=True)]
    ppermute x0 -> x32, starting transfers between devices: none -> 55.6 us  [shift(): return lax.ppermute(array, axis, [(i, (i + by) % n) for i in range(n)])]
    pallas_call x0 -> x15, Pallas kernels: none -> 27.8 us  [call(): pl.pallas_call(kernel, in_specs=in_specs or [ANY] * len(ins), out_specs=o...]
    dot_general x3 -> x0, matrix products: 22.7 us -> none  [the longest x1 8.61 us: body(): predicted = jnp.dot(local_rows, proj, preferred_element_type=jnp.float32)]
  transfers between devices with their start and end apart: 3 -> 32, of which waited for: 3 -> 16; matrix products, arithmetic and copies ran while one was open for 3% -> 0% of each run, Pallas kernels for 0% -> 15%
where the time goes in v1:
time: 165 us
  waiting for transfers between devices  80.5 us (49%)
  starting transfers between devices  55.6 us (34%)
  Pallas kernels  27.8 us (17%)
    ppermute x32, waiting for transfers between devices, shift(): return lax.ppermute(array, axis, [(i, (i + by) % n) for i in range(n)])  80.5 us
    ppermute x32, starting transfers between devices, shift(): return lax.ppermute(array, axis, [(i, (i + by) % n) for i in range(n)])  55.6 us
    pallas_call x15, Pallas kernels, call(): pl.pallas_call(kernel, in_specs=in_specs or [ANY] * len(ins), out_specs=o...  27.8 us
  transfers between devices with their start and end apart: 32, of which 16 were waited for; matrix products, arithmetic and copies ran while one was open for 0% of the time, Pallas kernels for 15%

profile of v1, /device:TPU:32, one launch (start us, length us, event | category | flops | bytes accessed | tf_op | source)
XLA Modules:
  0.0 164.7 jit_solution(13401996168134281311)
XLA Ops:
  0.6 1.2 shard_map.50
  1.9 6.4 %collective-permute-start.3 = (bf16[512,512]{1,0:T(8,128)(2,1)S(1)}, bf16[512,512]{1,0:T(8,128)(2,1)S(1)}, u32[]{:S(2)}, u32[]{:S(2)}) collective-permute-start(bf16[512,512]{1,0:T(8,128)(2,1)S(1)} %shard_map.50), channel_id=1, source_target_pairs={{0,2},{2,0},{1,3},{3,1},{4,6},{6,4},{5,7},{7,5},{8,10},{10,8},{9,1... | collective-permute-start | bytes 1572872 | tf_op jit(solution)/shard_map/ppermute | solution.py:26
  8.2 2.8 %collective-permute-start.2 = (bf16[128,2048]{1,0:T(8,128)(2,1)S(1)}, bf16[128,2048]{1,0:T(8,128)(2,1)S(1)}, u32[]{:S(2)}, u32[]{:S(2)}) collective-permute-start(bf16[128,2048]{1,0:T(8,128)(2,1)S(1)} %copy-done), channel_id=1, source_target_pairs={{0,12},{4,0},{8,4},{12,8},{1,13},{5,1},{9,5},{13,9},{2,14},{6,2},{... | collective-permute-start | bytes 1572872 | tf_op jit(solution)/shard_map/ppermute | solution.py:26
  11.0 0.8 collective-permute-start.1
  11.8 0.9 collective-permute-start
  12.7 18.8 %collective-permute-done.3.own = bf16[512,512]{1,0:T(8,128)(2,1)S(1)} collective-permute-done((bf16[512,512]{1,0:T(8,128)(2,1)S(1)}, bf16[512,512]{1,0:T(8,128)(2,1)S(1)}, u32[]{:S(2)}, u32[]{:S(2)}) %collective-permute-start.3) | collective-permute-done | bytes 524320 | tf_op jit(solution)/shard_map/ppermute | solution.py:26
  31.5 3.0 %collective-permute-start.6 = (bf16[512,512]{1,0:T(8,128)(2,1)S(1)}, bf16[512,512]{1,0:T(8,128)(2,1)S(1)}, u32[]{:S(2)}, u32[]{:S(2)}) collective-permute-start(bf16[512,512]{1,0:T(8,128)(2,1)S(1)} %collective-permute-done.3.own), channel_id=1, source_target_pairs={{0,192},{64,0},{128,64},{192,128},{1,193},{65,1},{129,65},{193,129... | collective-permute-start | bytes 1572872 | tf_op jit(solution)/shard_map/ppermute | solution.py:26
  34.6 1.8 %collective-permute-start.5 = (bf16[512,512]{1,0:T(8,128)(2,1)S(1)}, bf16[512,512]{1,0:T(8,128)(2,1)S(1)}, u32[]{:S(2)}, u32[]{:S(2)}) collective-permute-start(bf16[512,512]{1,0:T(8,128)(2,1)S(1)} %collective-permute-done.3.own), channel_id=1, source_target_pairs={{0,128},{64,192},{128,0},{192,64},{1,129},{65,193},{129,1},{193,65... | collective-permute-start | bytes 1572872 | tf_op jit(solution)/shard_map/ppermute | solution.py:26
  36.4 0.7 collective-permute-start.4
  37.1 0.4 shard_map.52
  37.5 2.2 %collective-permute-start.9 = (bf16[128,2048]{1,0:T(8,128)(2,1)S(1)}, bf16[128,2048]{1,0:T(8,128)(2,1)S(1)}, u32[]{:S(2)}, u32[]{:S(2)}) collective-permute-start(bf16[128,2048]{1,0:T(8,128)(2,1)S(1)} %get-tuple-element.47), channel_id=1, source_target_pairs={{0,8},{4,12},{8,0},{12,4},{1,9},{5,13},{9,1},{13,5},{2,10},{6,14},... | collective-permute-start | bytes 1572872 | tf_op jit(solution)/shard_map/ppermute | solution.py:26
  39.7 16.6 %collective-permute-done.6.p3 = bf16[512,512]{1,0:T(8,128)(2,1)S(1)} collective-permute-done((bf16[512,512]{1,0:T(8,128)(2,1)S(1)}, bf16[512,512]{1,0:T(8,128)(2,1)S(1)}, u32[]{:S(2)}, u32[]{:S(2)}) %collective-permute-start.6) | collective-permute-done | bytes 524320 | tf_op jit(solution)/shard_map/ppermute | solution.py:26
  56.3 1.5 collective-permute-start.8
  57.8 1.7 %collective-permute-start.10 = (bf16[128,2048]{1,0:T(8,128)(2,1)S(1)}, bf16[128,2048]{1,0:T(8,128)(2,1)S(1)}, u32[]{:S(2)}, u32[]{:S(2)}) collective-permute-start(bf16[128,2048]{1,0:T(8,128)(2,1)S(1)} %get-tuple-element.48), channel_id=1, source_target_pairs={{0,12},{4,0},{8,4},{12,8},{1,13},{5,1},{9,5},{13,9},{2,14},{6,2},{... | collective-permute-start | bytes 1572872 | tf_op jit(solution)/shard_map/ppermute | solution.py:26
  59.5 0.5 collective-permute-done.4.p1
  60.3 6.4 %collective-permute-done.8.t1 = bf16[128,2048]{1,0:T(8,128)(2,1)S(1)} collective-permute-done((bf16[128,2048]{1,0:T(8,128)(2,1)S(1)}, bf16[128,2048]{1,0:T(8,128)(2,1)S(1)}, u32[]{:S(2)}, u32[]{:S(2)}) %collective-permute-start.8) | collective-permute-done | bytes 524320 | tf_op jit(solution)/shard_map/ppermute | solution.py:26
  67.0 4.5 %shard_map.53 = (bf16[512,1024]{1,0:T(8,128)(2,1)S(1)}, bf16[512,2048]{1,0:T(8,128)(2,1)S(1)}) custom-call(bf16[128,2048]{1,0:T(8,128)(2,1)S(1)} %copy-done, bf16[128,2048]{1,0:T(8,128)(2,1)S(1)} %collective-permute-done.s1, bf16[128,2048]{1,0:T(8,128)(2,1)S(1)} %collective-permute-done.1.s2, bf16[128,2048]{1,0:T(8,128)(2,1)S(1)} %collective-permute-done.2.s3, ...), custom_call_target="tpu_custom_call" | custom-call | flops 99999997952 | bytes 1 | tf_op jit(solution)/shard_map/pallas_call | solution.py:54
  71.7 4.6 %shard_map.54 = (bf16[512,1024]{1,0:T(8,128)(2,1)S(1)}, bf16[512,2048]{1,0:T(8,128)(2,1)S(1)}) custom-call(bf16[128,2048]{1,0:T(8,128)(2,1)S(1)} %copy-done, bf16[128,2048]{1,0:T(8,128)(2,1)S(1)} %collective-permute-done.s1, bf16[128,2048]{1,0:T(8,128)(2,1)S(1)} %collective-permute-done.1.s2, bf16[128,2048]{1,0:T(8,128)(2,1)S(1)} %collective-permute-done.2.s3, ...), custom_call_target="tpu_custom_call" | custom-call | flops 99999997952 | bytes 1 | tf_op jit(solution)/shard_map/pallas_call | solution.py:54
  76.4 0.5 collective-permute-start.20
  76.9 1.1 shard_map.55
  78.0 3.8 %collective-permute-start.13 = (bf16[256,512]{1,0:T(8,128)(2,1)S(1)}, bf16[256,512]{1,0:T(8,128)(2,1)S(1)}, u32[]{:S(2)}, u32[]{:S(2)}) collective-permute-start(bf16[256,512]{1,0:T(8,128)(2,1)S(1)} %get-tuple-element.54), channel_id=1, source_target_pairs={{0,64},{64,128},{128,192},{192,0},{1,65},{65,129},{129,193},{193,1... | collective-permute-start | bytes 786440 | tf_op jit(solution)/shard_map/ppermute | solution.py:26
  82.0 7.5 %shard_map.56 = (bf16[128,2048]{1,0:T(8,128)(2,1)S(1)}, bf16[128,2048]{1,0:T(8,128)(2,1)S(1)}, bf16[128,2048]{1,0:T(8,128)(2,1)S(1)}, bf16[128,2048]{1,0:T(8,128)(2,1)S(1)}) custom-call(bf16[512,1024]{1,0:T(8,128)(2,1)S(1)} %get-tuple-element.49.error.near, bf16[512,1024]{1,0:T(8,128)(2,1)S(1)} %get-tuple-element.52.far.error, bf16[2048,512]{1,0:T(8,128)(2,1)} %wa.1, ...), custom_call_target="tpu_custom_call" | custom-call | flops 99999997952 | bytes 1 | tf_op jit(solution)/shard_map/pallas_call | solution.py:54
  89.8 2.4 %shard_map.57 = (bf16[512,512]{1,0:T(8,128)(2,1)S(1)}, bf16[512,512]{1,0:T(8,128)(2,1)S(1)}, bf16[512,512]{1,0:T(8,128)(2,1)S(1)}) custom-call(bf16[128,2048]{1,0:T(8,128)(2,1)S(1)} %copy-done, bf16[128,2048]{1,0:T(8,128)(2,1)S(1)} %collective-permute-done.s1, bf16[128,2048]{1,0:T(8,128)(2,1)S(1)} %collective-permute-done.1.s2, ...), custom_call_target="tpu_custom_call" | custom-call | flops 1 | bytes 1 | tf_op jit(solution)/shard_map/pallas_call | solution.py:54
  92.2 1.6 collective-permute-start.15
  93.9 1.7 %collective-permute-start.16 = (bf16[512,512]{1,0:T(8,128)(2,1)S(1)}, bf16[512,512]{1,0:T(8,128)(2,1)S(1)}, u32[]{:S(2)}, u32[]{:S(2)}) collective-permute-start(bf16[512,512]{1,0:T(8,128)(2,1)S(1)} %get-tuple-element.61), channel_id=1, source_target_pairs={{0,192},{64,0},{128,64},{192,128},{1,193},{65,1},{129,65},{193,129... | collective-permute-start | bytes 1572872 | tf_op jit(solution)/shard_map/ppermute | solution.py:26
  95.6 1.1 shard_map.59
  96.6 0.7 collective-permute-start.21
  97.3 2.9 %collective-permute-start.22 = (bf16[256,512]{1,0:T(8,128)(2,1)S(1)}, bf16[256,512]{1,0:T(8,128)(2,1)S(1)}, u32[]{:S(2)}, u32[]{:S(2)}) collective-permute-start(bf16[256,512]{1,0:T(8,128)(2,1)S(1)} %get-tuple-element.69), channel_id=1, source_target_pairs={{0,192},{64,0},{128,64},{192,128},{1,193},{65,1},{129,65},{193,129... | collective-permute-start | bytes 786440 | tf_op jit(solution)/shard_map/ppermute | solution.py:26
  100.2 8.2 %collective-permute-done.15.b = bf16[512,512]{1,0:T(8,128)(2,1)S(1)} collective-permute-done((bf16[512,512]{1,0:T(8,128)(2,1)S(1)}, bf16[512,512]{1,0:T(8,128)(2,1)S(1)}, u32[]{:S(2)}, u32[]{:S(2)}) %collective-permute-start.15) | collective-permute-done | bytes 524320 | tf_op jit(solution)/shard_map/ppermute | solution.py:26
  109.0 2.9 %collective-permute-start.18 = (bf16[512,128]{1,0:T(8,128)(2,1)S(1)}, bf16[512,128]{1,0:T(8,128)(2,1)S(1)}, u32[]{:S(2)}, u32[]{:S(2)}) collective-permute-start(bf16[512,128]{1,0:T(8,128)(2,1)S(1)} %get-tuple-element.64), channel_id=1, source_target_pairs={{0,32},{16,48},{32,0},{48,16},{1,33},{17,49},{33,1},{49,17},{2,34}... | collective-permute-start | bytes 393224 | tf_op jit(solution)/shard_map/ppermute | solution.py:26
  111.9 0.6 collective-permute-done.21.rest_0_
  112.5 2.8 %collective-permute-start.24 = (bf16[128,2048]{1,0:T(8,128)(2,1)S(1)}, bf16[128,2048]{1,0:T(8,128)(2,1)S(1)}, u32[]{:S(2)}, u32[]{:S(2)}) collective-permute-start(bf16[128,2048]{1,0:T(8,128)(2,1)S(1)} %get-tuple-element.76), channel_id=1, source_target_pairs={{0,8},{4,12},{8,0},{12,4},{1,9},{5,13},{9,1},{13,5},{2,10},{6,14},... | collective-permute-start | bytes 1572872 | tf_op jit(solution)/shard_map/ppermute | solution.py:26
  115.3 2.4 %shard_map.60 = (bf16[512,512]{1,0:T(8,128)(2,1)S(1)}, bf16[512,512]{1,0:T(8,128)(2,1)S(1)}, bf16[512,512]{1,0:T(8,128)(2,1)S(1)}) custom-call(bf16[128,2048]{1,0:T(8,128)(2,1)S(1)} %copy-done, bf16[128,2048]{1,0:T(8,128)(2,1)S(1)} %collective-permute-done.s1, bf16[128,2048]{1,0:T(8,128)(2,1)S(1)} %collective-permute-done.1.s2, ...), custom_call_target="tpu_custom_call" | custom-call | flops 1 | bytes 1 | tf_op jit(solution)/shard_map/pallas_call | solution.py:54
  117.7 1.9 %collective-permute-start.23 = (bf16[128,2048]{1,0:T(8,128)(2,1)S(1)}, bf16[128,2048]{1,0:T(8,128)(2,1)S(1)}, u32[]{:S(2)}, u32[]{:S(2)}) collective-permute-start(bf16[128,2048]{1,0:T(8,128)(2,1)S(1)} %get-tuple-element.74), channel_id=1, source_target_pairs={{0,4},{4,8},{8,12},{12,0},{1,5},{5,9},{9,13},{13,1},{2,6},{6,10},{... | collective-permute-start | bytes 1572872 | tf_op jit(solution)/shard_map/ppermute | solution.py:26
  119.6 2.4 %collective-permute-start.25 = (bf16[128,2048]{1,0:T(8,128)(2,1)S(1)}, bf16[128,2048]{1,0:T(8,128)(2,1)S(1)}, u32[]{:S(2)}, u32[]{:S(2)}) collective-permute-start(bf16[128,2048]{1,0:T(8,128)(2,1)S(1)} %get-tuple-element.78), channel_id=1, source_target_pairs={{0,12},{4,0},{8,4},{12,8},{1,13},{5,1},{9,5},{13,9},{2,14},{6,2},{... | collective-permute-start | bytes 1572872 | tf_op jit(solution)/shard_map/ppermute | solution.py:26
  122.3 2.9 %collective-permute-start.27 = (bf16[512,512]{1,0:T(8,128)(2,1)S(1)}, bf16[512,512]{1,0:T(8,128)(2,1)S(1)}, u32[]{:S(2)}, u32[]{:S(2)}) collective-permute-start(bf16[512,512]{1,0:T(8,128)(2,1)S(1)} %get-tuple-element.81), channel_id=1, source_target_pairs={{0,192},{64,0},{128,64},{192,128},{1,193},{65,1},{129,65},{193,129... | collective-permute-start | bytes 1572872 | tf_op jit(solution)/shard_map/ppermute | solution.py:26
  125.2 3.7 %collective-permute-done.24.p2 = bf16[128,2048]{1,0:T(8,128)(2,1)S(1)} collective-permute-done((bf16[128,2048]{1,0:T(8,128)(2,1)S(1)}, bf16[128,2048]{1,0:T(8,128)(2,1)S(1)}, u32[]{:S(2)}, u32[]{:S(2)}) %collective-permute-start.24) | collective-permute-done | bytes 524320 | tf_op jit(solution)/shard_map/ppermute | solution.py:26
  128.9 8.8 %collective-permute-done.23.p1 = bf16[128,2048]{1,0:T(8,128)(2,1)S(1)} collective-permute-done((bf16[128,2048]{1,0:T(8,128)(2,1)S(1)}, bf16[128,2048]{1,0:T(8,128)(2,1)S(1)}, u32[]{:S(2)}, u32[]{:S(2)}) %collective-permute-start.23) | collective-permute-done | bytes 524320 | tf_op jit(solution)/shard_map/ppermute | solution.py:26
  137.7 1.1 collective-permute-done.25.p3
  139.0 1.5 collective-permute-start.28
  140.5 1.6 collective-permute-start.30
  142.0 7.4 %collective-permute-done.28.p1 = bf16[512,128]{1,0:T(8,128)(2,1)S(1)} collective-permute-done((bf16[512,128]{1,0:T(8,128)(2,1)S(1)}, bf16[512,128]{1,0:T(8,128)(2,1)S(1)}, u32[]{:S(2)}, u32[]{:S(2)}) %collective-permute-start.28) | collective-permute-done | bytes 131104 | tf_op jit(solution)/shard_map/ppermute | solution.py:26
  149.4 1.4 collective-permute-done.29.p2
  150.8 0.7 collective-permute-done.30.p3
  151.6 5.8 %collective-permute-start.31 = (bf16[512,128]{1,0:T(8,128)(2,1)S(1)}, bf16[512,128]{1,0:T(8,128)(2,1)S(1)}, u32[]{:S(2)}, u32[]{:S(2)}) collective-permute-start(bf16[512,128]{1,0:T(8,128)(2,1)S(1)} %shard_map.62), channel_id=1, source_target_pairs={{0,2},{2,0},{1,3},{3,1},{4,6},{6,4},{5,7},{7,5},{8,10},{10,8},{9,1... | collective-permute-start | bytes 393224 | tf_op jit(solution)/shard_map/ppermute | solution.py:26
  157.4 1.0 shard_map.64
  158.4 5.5 %collective-permute-done.31.far = bf16[512,128]{1,0:T(8,128)(2,1)S(1)} collective-permute-done((bf16[512,128]{1,0:T(8,128)(2,1)S(1)}, bf16[512,128]{1,0:T(8,128)(2,1)S(1)}, u32[]{:S(2)}, u32[]{:S(2)}) %collective-permute-start.31) | collective-permute-done | bytes 131104 | tf_op jit(solution)/shard_map/ppermute | solution.py:26
  163.9 0.8 shard_map.63
  (35 shorter events, 2.7 us)
Async XLA Ops:
  0.6 7.6 %copy-start = (bf16[128,2048]{1,0:T(8,128)(2,1)S(1)}, bf16[128,2048]{1,0:T(8,128)(2,1)}, u32[]{:S(2)}) copy-start(bf16[128,2048]{1,0:T(8,128)(2,1)} %s0.11) | copy-start | bytes 1572868
  0.6 36.4 %copy-start.1 = (bf16[128,8192]{1,0:T(8,128)(2,1)S(1)}, bf16[128,8192]{1,0:T(8,128)(2,1)}, u32[]{:S(2)}) copy-start(bf16[128,8192]{1,0:T(8,128)(2,1)} %teacher.4) | copy-start | bytes 6291460
  1.9 29.7 %collective-permute-start.3 = (bf16[512,512]{1,0:T(8,128)(2,1)S(1)}, bf16[512,512]{1,0:T(8,128)(2,1)S(1)}, u32[]{:S(2)}, u32[]{:S(2)}) collective-permute-start(bf16[512,512]{1,0:T(8,128)(2,1)S(1)} %shard_map.50), channel_id=1, source_target_pairs={{0,2},{2,0},{1,3},{3,1},{4,6},{6,4},{5,7},{7,5},{8,10},{10,8},{9,1... | collective-permute-start | bytes 1572872 | tf_op jit(solution)/shard_map/ppermute | solution.py:26
  8.2 26.3 %collective-permute-start.2 = (bf16[128,2048]{1,0:T(8,128)(2,1)S(1)}, bf16[128,2048]{1,0:T(8,128)(2,1)S(1)}, u32[]{:S(2)}, u32[]{:S(2)}) collective-permute-start(bf16[128,2048]{1,0:T(8,128)(2,1)S(1)} %copy-done), channel_id=1, source_target_pairs={{0,12},{4,0},{8,4},{12,8},{1,13},{5,1},{9,5},{13,9},{2,14},{6,2},{... | collective-permute-start | bytes 1572872 | tf_op jit(solution)/shard_map/ppermute | solution.py:26
  11.0 25.4 %collective-permute-start.1 = (bf16[128,2048]{1,0:T(8,128)(2,1)S(1)}, bf16[128,2048]{1,0:T(8,128)(2,1)S(1)}, u32[]{:S(2)}, u32[]{:S(2)}) collective-permute-start(bf16[128,2048]{1,0:T(8,128)(2,1)S(1)} %copy-done), channel_id=1, source_target_pairs={{0,8},{4,12},{8,0},{12,4},{1,9},{5,13},{9,1},{13,5},{2,10},{6,14},... | collective-permute-start | bytes 1572872 | tf_op jit(solution)/shard_map/ppermute | solution.py:26
  11.8 25.2 %collective-permute-start = (bf16[128,2048]{1,0:T(8,128)(2,1)S(1)}, bf16[128,2048]{1,0:T(8,128)(2,1)S(1)}, u32[]{:S(2)}, u32[]{:S(2)}) collective-permute-start(bf16[128,2048]{1,0:T(8,128)(2,1)S(1)} %copy-done), channel_id=1, source_target_pairs={{0,4},{4,8},{8,12},{12,0},{1,5},{5,9},{9,13},{13,1},{2,6},{6,10},{... | collective-permute-start | bytes 1572872 | tf_op jit(solution)/shard_map/ppermute | solution.py:26
  12.7 54.3 %collective-permute-start.7 = (bf16[2048,512]{1,0:T(8,128)(2,1)}, bf16[2048,512]{1,0:T(8,128)(2,1)S(1)}, u32[]{:S(2)}, u32[]{:S(2)}) collective-permute-start(bf16[2048,512]{1,0:T(8,128)(2,1)} %wa.1), channel_id=1, source_target_pairs={{0,1},{1,0},{2,3},{3,2},{4,5},{5,4},{6,7},{7,6},{8,9},{9,8},{10,11... | collective-permute-start | bytes 6291464 | tf_op jit(solution)/shard_map/ppermute | solution.py:26
  31.5 24.7 %collective-permute-start.6 = (bf16[512,512]{1,0:T(8,128)(2,1)S(1)}, bf16[512,512]{1,0:T(8,128)(2,1)S(1)}, u32[]{:S(2)}, u32[]{:S(2)}) collective-permute-start(bf16[512,512]{1,0:T(8,128)(2,1)S(1)} %collective-permute-done.3.own), channel_id=1, source_target_pairs={{0,192},{64,0},{128,64},{192,128},{1,193},{65,1},{129,65},{193,129... | collective-permute-start | bytes 1572872 | tf_op jit(solution)/shard_map/ppermute | solution.py:26
  34.6 23.2 %collective-permute-start.5 = (bf16[512,512]{1,0:T(8,128)(2,1)S(1)}, bf16[512,512]{1,0:T(8,128)(2,1)S(1)}, u32[]{:S(2)}, u32[]{:S(2)}) collective-permute-start(bf16[512,512]{1,0:T(8,128)(2,1)S(1)} %collective-permute-done.3.own), channel_id=1, source_target_pairs={{0,128},{64,192},{128,0},{192,64},{1,129},{65,193},{129,1},{193,65... | collective-permute-start | bytes 1572872 | tf_op jit(solution)/shard_map/ppermute | solution.py:26
  36.4 23.6 %collective-permute-start.4 = (bf16[512,512]{1,0:T(8,128)(2,1)S(1)}, bf16[512,512]{1,0:T(8,128)(2,1)S(1)}, u32[]{:S(2)}, u32[]{:S(2)}) collective-permute-start(bf16[512,512]{1,0:T(8,128)(2,1)S(1)} %collective-permute-done.3.own), channel_id=1, source_target_pairs={{0,64},{64,128},{128,192},{192,0},{1,65},{65,129},{129,193},{193,1... | collective-permute-start | bytes 1572872 | tf_op jit(solution)/shard_map/ppermute | solution.py:26
  37.5 22.8 %collective-permute-start.9 = (bf16[128,2048]{1,0:T(8,128)(2,1)S(1)}, bf16[128,2048]{1,0:T(8,128)(2,1)S(1)}, u32[]{:S(2)}, u32[]{:S(2)}) collective-permute-start(bf16[128,2048]{1,0:T(8,128)(2,1)S(1)} %get-tuple-element.47), channel_id=1, source_target_pairs={{0,8},{4,12},{8,0},{12,4},{1,9},{5,13},{9,1},{13,5},{2,10},{6,14},... | collective-permute-start | bytes 1572872 | tf_op jit(solution)/shard_map/ppermute | solution.py:26
  56.3 10.4 %collective-permute-start.8 = (bf16[128,2048]{1,0:T(8,128)(2,1)S(1)}, bf16[128,2048]{1,0:T(8,128)(2,1)S(1)}, u32[]{:S(2)}, u32[]{:S(2)}) collective-permute-start(bf16[128,2048]{1,0:T(8,128)(2,1)S(1)} %get-tuple-element.46), channel_id=1, source_target_pairs={{0,4},{4,8},{8,12},{12,0},{1,5},{5,9},{9,13},{13,1},{2,6},{6,10},{... | collective-permute-start | bytes 1572872 | tf_op jit(solution)/shard_map/ppermute | solution.py:26
  57.8 9.2 %collective-permute-start.10 = (bf16[128,2048]{1,0:T(8,128)(2,1)S(1)}, bf16[128,2048]{1,0:T(8,128)(2,1)S(1)}, u32[]{:S(2)}, u32[]{:S(2)}) collective-permute-start(bf16[128,2048]{1,0:T(8,128)(2,1)S(1)} %get-tuple-element.48), channel_id=1, source_target_pairs={{0,12},{4,0},{8,4},{12,8},{1,13},{5,1},{9,5},{13,9},{2,14},{6,2},{... | collective-permute-start | bytes 1572872 | tf_op jit(solution)/shard_map/ppermute | solution.py:26
  60.2 11.5 %collective-permute-start.12 = (bf16[2048,512]{1,0:T(8,128)(2,1)S(1)}, bf16[2048,512]{1,0:T(8,128)(2,1)S(1)}, u32[]{:S(2)}, u32[]{:S(2)}) collective-permute-start(bf16[2048,512]{1,0:T(8,128)(2,1)S(1)} %shard_map.51.w_own.wc), channel_id=1, source_target_pairs={{0,1},{1,0},{2,3},{3,2},{4,5},{5,4},{6,7},{7,6},{8,9},{9,8},{10,11... | collective-permute-start | bytes 6291464 | tf_op jit(solution)/shard_map/ppermute | solution.py:26
  71.4 5.5 %collective-permute-start.11 = (bf16[512,2048]{1,0:T(8,128)(2,1)S(1)}, bf16[512,2048]{1,0:T(8,128)(2,1)S(1)}, u32[]{:S(2)}, u32[]{:S(2)}) collective-permute-start(bf16[512,2048]{1,0:T(8,128)(2,1)S(1)} %get-tuple-element.50), channel_id=1, source_target_pairs={{0,1},{1,0},{2,3},{3,2},{4,5},{5,4},{6,7},{7,6},{8,9},{9,8},{10,11... | collective-permute-start | bytes 6291464 | tf_op jit(solution)/shard_map/ppermute | solution.py:26
  76.4 19.2 %collective-permute-start.20 = (bf16[512,2048]{1,0:T(8,128)(2,1)S(1)}, bf16[512,2048]{1,0:T(8,128)(2,1)S(1)}, u32[]{:S(2)}, u32[]{:S(2)}) collective-permute-start(bf16[512,2048]{1,0:T(8,128)(2,1)S(1)} %get-tuple-element.66), channel_id=1, source_target_pairs={{0,1},{1,0},{2,3},{3,2},{4,5},{5,4},{6,7},{7,6},{8,9},{9,8},{10,11... | collective-permute-start | bytes 6291464 | tf_op jit(solution)/shard_map/ppermute | solution.py:26
  78.0 11.5 %collective-permute-start.13 = (bf16[256,512]{1,0:T(8,128)(2,1)S(1)}, bf16[256,512]{1,0:T(8,128)(2,1)S(1)}, u32[]{:S(2)}, u32[]{:S(2)}) collective-permute-start(bf16[256,512]{1,0:T(8,128)(2,1)S(1)} %get-tuple-element.54), channel_id=1, source_target_pairs={{0,64},{64,128},{128,192},{192,0},{1,65},{65,129},{129,193},{193,1... | collective-permute-start | bytes 786440 | tf_op jit(solution)/shard_map/ppermute | solution.py:26
  81.8 8.0 %collective-permute-start.14 = (bf16[256,512]{1,0:T(8,128)(2,1)S(1)}, bf16[256,512]{1,0:T(8,128)(2,1)S(1)}, u32[]{:S(2)}, u32[]{:S(2)}) collective-permute-start(bf16[256,512]{1,0:T(8,128)(2,1)S(1)} %get-tuple-element.55), channel_id=1, source_target_pairs={{0,192},{64,0},{128,64},{192,128},{1,193},{65,1},{129,65},{193,129... | collective-permute-start | bytes 786440 | tf_op jit(solution)/shard_map/ppermute | solution.py:26
  92.2 16.1 %collective-permute-start.15 = (bf16[512,512]{1,0:T(8,128)(2,1)S(1)}, bf16[512,512]{1,0:T(8,128)(2,1)S(1)}, u32[]{:S(2)}, u32[]{:S(2)}) collective-permute-start(bf16[512,512]{1,0:T(8,128)(2,1)S(1)} %get-tuple-element.60), channel_id=1, source_target_pairs={{0,64},{64,128},{128,192},{192,0},{1,65},{65,129},{129,193},{193,1... | collective-permute-start | bytes 1572872 | tf_op jit(solution)/shard_map/ppermute | solution.py:26
  93.9 14.9 %collective-permute-start.16 = (bf16[512,512]{1,0:T(8,128)(2,1)S(1)}, bf16[512,512]{1,0:T(8,128)(2,1)S(1)}, u32[]{:S(2)}, u32[]{:S(2)}) collective-permute-start(bf16[512,512]{1,0:T(8,128)(2,1)S(1)} %get-tuple-element.61), channel_id=1, source_target_pairs={{0,192},{64,0},{128,64},{192,128},{1,193},{65,1},{129,65},{193,129... | collective-permute-start | bytes 1572872 | tf_op jit(solution)/shard_map/ppermute | solution.py:26
  96.6 15.8 %collective-permute-start.21 = (bf16[256,512]{1,0:T(8,128)(2,1)S(1)}, bf16[256,512]{1,0:T(8,128)(2,1)S(1)}, u32[]{:S(2)}, u32[]{:S(2)}) collective-permute-start(bf16[256,512]{1,0:T(8,128)(2,1)S(1)} %get-tuple-element.68), channel_id=1, source_target_pairs={{0,64},{64,128},{128,192},{192,0},{1,65},{65,129},{129,193},{193,1... | collective-permute-start | bytes 786440 | tf_op jit(solution)/shard_map/ppermute | solution.py:26
  97.3 17.9 %collective-permute-start.22 = (bf16[256,512]{1,0:T(8,128)(2,1)S(1)}, bf16[256,512]{1,0:T(8,128)(2,1)S(1)}, u32[]{:S(2)}, u32[]{:S(2)}) collective-permute-start(bf16[256,512]{1,0:T(8,128)(2,1)S(1)} %get-tuple-element.69), channel_id=1, source_target_pairs={{0,192},{64,0},{128,64},{192,128},{1,193},{65,1},{129,65},{193,129... | collective-permute-start | bytes 786440 | tf_op jit(solution)/shard_map/ppermute | solution.py:26
  109.0 10.6 %collective-permute-start.19 = (bf16[512,128]{1,0:T(8,128)(2,1)S(1)}, bf16[512,128]{1,0:T(8,128)(2,1)S(1)}, u32[]{:S(2)}, u32[]{:S(2)}) collective-permute-start(bf16[512,128]{1,0:T(8,128)(2,1)S(1)} %get-tuple-element.65), channel_id=1, source_target_pairs={{0,48},{16,0},{32,16},{48,32},{1,49},{17,1},{33,17},{49,33},{2,50}... | collective-permute-start | bytes 393224 | tf_op jit(solution)/shard_map/ppermute | solution.py:26
  109.0 12.9 %collective-permute-start.18 = (bf16[512,128]{1,0:T(8,128)(2,1)S(1)}, bf16[512,128]{1,0:T(8,128)(2,1)S(1)}, u32[]{:S(2)}, u32[]{:S(2)}) collective-permute-start(bf16[512,128]{1,0:T(8,128)(2,1)S(1)} %get-tuple-element.64), channel_id=1, source_target_pairs={{0,32},{16,48},{32,0},{48,16},{1,33},{17,49},{33,1},{49,17},{2,34}... | collective-permute-start | bytes 393224 | tf_op jit(solution)/shard_map/ppermute | solution.py:26
  111.9 10.4 %collective-permute-start.17 = (bf16[512,128]{1,0:T(8,128)(2,1)S(1)}, bf16[512,128]{1,0:T(8,128)(2,1)S(1)}, u32[]{:S(2)}, u32[]{:S(2)}) collective-permute-start(bf16[512,128]{1,0:T(8,128)(2,1)S(1)} %get-tuple-element.63), channel_id=1, source_target_pairs={{0,16},{16,32},{32,48},{48,0},{1,17},{17,33},{33,49},{49,1},{2,18}... | collective-permute-start | bytes 393224 | tf_op jit(solution)/shard_map/ppermute | solution.py:26
  112.5 16.4 %collective-permute-start.24 = (bf16[128,2048]{1,0:T(8,128)(2,1)S(1)}, bf16[128,2048]{1,0:T(8,128)(2,1)S(1)}, u32[]{:S(2)}, u32[]{:S(2)}) collective-permute-start(bf16[128,2048]{1,0:T(8,128)(2,1)S(1)} %get-tuple-element.76), channel_id=1, source_target_pairs={{0,8},{4,12},{8,0},{12,4},{1,9},{5,13},{9,1},{13,5},{2,10},{6,14},... | collective-permute-start | bytes 1572872 | tf_op jit(solution)/shard_map/ppermute | solution.py:26
  117.7 20.0 %collective-permute-start.23 = (bf16[128,2048]{1,0:T(8,128)(2,1)S(1)}, bf16[128,2048]{1,0:T(8,128)(2,1)S(1)}, u32[]{:S(2)}, u32[]{:S(2)}) collective-permute-start(bf16[128,2048]{1,0:T(8,128)(2,1)S(1)} %get-tuple-element.74), channel_id=1, source_target_pairs={{0,4},{4,8},{8,12},{12,0},{1,5},{5,9},{9,13},{13,1},{2,6},{6,10},{... | collective-permute-start | bytes 1572872 | tf_op jit(solution)/shard_map/ppermute | solution.py:26
  119.6 19.2 %collective-permute-start.25 = (bf16[128,2048]{1,0:T(8,128)(2,1)S(1)}, bf16[128,2048]{1,0:T(8,128)(2,1)S(1)}, u32[]{:S(2)}, u32[]{:S(2)}) collective-permute-start(bf16[128,2048]{1,0:T(8,128)(2,1)S(1)} %get-tuple-element.78), channel_id=1, source_target_pairs={{0,12},{4,0},{8,4},{12,8},{1,13},{5,1},{9,5},{13,9},{2,14},{6,2},{... | collective-permute-start | bytes 1572872 | tf_op jit(solution)/shard_map/ppermute | solution.py:26
  122.0 16.8 %collective-permute-start.26 = (bf16[512,512]{1,0:T(8,128)(2,1)S(1)}, bf16[512,512]{1,0:T(8,128)(2,1)S(1)}, u32[]{:S(2)}, u32[]{:S(2)}) collective-permute-start(bf16[512,512]{1,0:T(8,128)(2,1)S(1)} %get-tuple-element.80), channel_id=1, source_target_pairs={{0,64},{64,128},{128,192},{192,0},{1,65},{65,129},{129,193},{193,1... | collective-permute-start | bytes 1572872 | tf_op jit(solution)/shard_map/ppermute | solution.py:26
  122.3 16.4 %collective-permute-start.27 = (bf16[512,512]{1,0:T(8,128)(2,1)S(1)}, bf16[512,512]{1,0:T(8,128)(2,1)S(1)}, u32[]{:S(2)}, u32[]{:S(2)}) collective-permute-start(bf16[512,512]{1,0:T(8,128)(2,1)S(1)} %get-tuple-element.81), channel_id=1, source_target_pairs={{0,192},{64,0},{128,64},{192,128},{1,193},{65,1},{129,65},{193,129... | collective-permute-start | bytes 1572872 | tf_op jit(solution)/shard_map/ppermute | solution.py:26
  139.0 10.4 %collective-permute-start.28 = (bf16[512,128]{1,0:T(8,128)(2,1)S(1)}, bf16[512,128]{1,0:T(8,128)(2,1)S(1)}, u32[]{:S(2)}, u32[]{:S(2)}) collective-permute-start(bf16[512,128]{1,0:T(8,128)(2,1)S(1)} %get-tuple-element.83), channel_id=1, source_target_pairs={{0,16},{16,32},{32,48},{48,0},{1,17},{17,33},{33,49},{49,1},{2,18}... | collective-permute-start | bytes 393224 | tf_op jit(solution)/shard_map/ppermute | solution.py:26
  140.5 10.3 %collective-permute-start.29 = (bf16[512,128]{1,0:T(8,128)(2,1)S(1)}, bf16[512,128]{1,0:T(8,128)(2,1)S(1)}, u32[]{:S(2)}, u32[]{:S(2)}) collective-permute-start(bf16[512,128]{1,0:T(8,128)(2,1)S(1)} %get-tuple-element.84), channel_id=1, source_target_pairs={{0,32},{16,48},{32,0},{48,16},{1,33},{17,49},{33,1},{49,17},{2,34}... | collective-permute-start | bytes 393224 | tf_op jit(solution)/shard_map/ppermute | solution.py:26
  140.5 11.1 %collective-permute-start.30 = (bf16[512,128]{1,0:T(8,128)(2,1)S(1)}, bf16[512,128]{1,0:T(8,128)(2,1)S(1)}, u32[]{:S(2)}, u32[]{:S(2)}) collective-permute-start(bf16[512,128]{1,0:T(8,128)(2,1)S(1)} %get-tuple-element.85), channel_id=1, source_target_pairs={{0,48},{16,0},{32,16},{48,32},{1,49},{17,1},{33,17},{49,33},{2,50}... | collective-permute-start | bytes 393224 | tf_op jit(solution)/shard_map/ppermute | solution.py:26
  151.6 12.3 %collective-permute-start.31 = (bf16[512,128]{1,0:T(8,128)(2,1)S(1)}, bf16[512,128]{1,0:T(8,128)(2,1)S(1)}, u32[]{:S(2)}, u32[]{:S(2)}) collective-permute-start(bf16[512,128]{1,0:T(8,128)(2,1)S(1)} %shard_map.62), channel_id=1, source_target_pairs={{0,2},{2,0},{1,3},{3,1},{4,6},{6,4},{5,7},{7,5},{8,10},{10,8},{9,1... | collective-permute-start | bytes 393224 | tf_op jit(solution)/shard_map/ppermute | solution.py:26

commit v2 on v1

--- a/solution.py
+++ b/solution.py
@@ -19,6 +19,7 @@
 BLOCK = DS // N
 ROWS = BLOCK // N
 BIG = 10**11
+SMALL = 3 * 10**8
 
 
 def shift(array, axis, by):
@@ -115,10 +116,16 @@
     )
 
 
-def join_kernel(own, p1, p2, p3, out, sems):
+def join_kernel(own, p1, p3, lower, upper, _, out, sems):
     y = index("y")
+    spots = [place((y + N - s) % N, BLOCK) for s in range(N)]
+    across = pl.multiple_of((y + 2) % N * BLOCK, BLOCK)
     pairs = [
-        (ref, out.at[place((y + N - s) % N, BLOCK), :]) for s, ref in enumerate((own, p1, p2, p3))
+        (own, out.at[spots[0], :]),
+        (p1, out.at[spots[1], :]),
+        (p3, out.at[spots[3], :]),
+        (lower, out.at[pl.ds(across, BLOCK // 2), :]),
+        (upper, out.at[pl.ds(across + BLOCK // 2, BLOCK // 2), :]),
     ]
     for copy in run(pairs, sems):
         copy.wait()
@@ -129,10 +136,18 @@
         join_kernel,
         parts,
         [((DS, WIDTH), BF16)],
-        [pltpu.SemaphoreType.DMA((4,))],
+        [pltpu.SemaphoreType.DMA((5,))],
         8,
         out_specs=[VMEM],
     )[0]
+
+
+def mark_kernel(*refs):
+    refs[-1][...] = jnp.zeros_like(refs[-1])
+
+
+def mark(values, flops):
+    return call(mark_kernel, values, [((8, 128), F32)], [], 1, flops, out_specs=[VMEM])[0]
 
 
 def error_kernel(half, s0, s1, s2, s3, w_own, w_other, teacher, t1, t2, t3, *rest):
@@ -165,16 +180,21 @@
         copy.wait()
 
     def one(j):
-        for n in range(2):
-            cols = pl.ds(j * WIDTH + n * 256, 256)
-            predicted = dot(students[...], weights[j, :, pl.ds(n * 256, 256)], 1, 0)
+        def step(i, _):
+            cols = pl.ds(pl.multiple_of(j * WIDTH + i * 256, 256), 256)
+            predicted = dot(students[...], weights[j, :, place(i, 256)], 1, 0)
             errors[:, cols] = (predicted - targets[:, cols].astype(F32)).astype(BF16)
+
+        lax.fori_loop(0, 2, step, None)
 
     one(1)
     turned = errors[:, pl.ds(WIDTH, WIDTH)].T
-    for n in range(N):
-        cols = pl.ds(n * BLOCK, BLOCK)
+
+    def step(n, _):
+        cols = place(n, BLOCK)
         grads[:, cols] = dot(turned, students[:, cols], 1, 0).astype(BF16)
+
+    lax.fori_loop(0, N, step, None)
     out = run([(grads, grad)], out_sems)
     second[-1].wait()
     one(0)
@@ -280,22 +300,23 @@
     loads += run([(w, weights.at[i]) for i, w in enumerate((wa, wb, wc, wd))], sems, 2)
     for copy in loads:
         copy.wait()
-    stores = []
-    for n in range(N):
-        cols = pl.ds(n * BLOCK, BLOCK)
+
+    def step(n, _):
+        cols = place(n, BLOCK)
         total = None
         for p in range(4):
             term = dot(errors[p // 2, :, pl.ds(p % 2 * WIDTH, WIDTH)], weights[p, cols, :], 1, 1)
             total = term if total is None else total + term
         grads[:, cols] = total.astype(BF16)
-        stores += run(
-            [
-                (grads.at[place((x + s) % N, TOK), cols], out.at[:, cols])
-                for s, out in enumerate((o0, o1, o2, o3))
-            ],
-            out_sems,
-            4 * n,
-        )
+
+    lax.fori_loop(0, N, step, None)
+    stores = run(
+        [
+            (grads.at[place((x + s) % N, TOK), :], out)
+            for s, out in enumerate((o0, o1, o2, o3))
+        ],
+        out_sems,
+    )
     for copy in stores:
         copy.wait()
 
@@ -311,7 +332,7 @@
             pltpu.VMEM((4, DS, WIDTH), BF16),
             pltpu.VMEM((n_tok, DS), BF16),
             pltpu.SemaphoreType.DMA((6,)),
-            pltpu.SemaphoreType.DMA((16,)),
+            pltpu.SemaphoreType.DMA((4,)),
         ],
         20,
         BIG,
@@ -341,8 +362,8 @@
     out[...] = (total + p2[...].astype(F32) + p3[...].astype(F32)).astype(BF16)
 
 
-def in_vmem(kernel, ins, outs):
-    return call(kernel, ins, outs, [], 8, in_specs=[VMEM] * len(ins), out_specs=[VMEM] * len(outs))
+def in_vmem(kernel, ins, outs, flops=1):
+    return call(kernel, ins, outs, [], 8, flops, in_specs=[VMEM] * len(ins), out_specs=[VMEM] * len(outs))
 
 
 def over(axis, blocks, *done):
@@ -354,41 +375,46 @@
     students = [student] + over("x", [student] * 3)
     part = shift(cut(proj), "zh", 1)
     proj_b = shift(proj, "c", 1)
-    sends = split(after(teacher, *students[1:]))
+    sends = split(after(teacher, *students[1:], proj_b))
     targets = over("x", sends)
 
-    proj_c = join([part, *over("y", [part] * 3)])
+    p1, p3 = (shift(after(part, *sends), "y", s) for s in (1, 3))
+    lower, upper = shift(p1[: BLOCK // 2], "y", 1), shift(p3[BLOCK // 2 :], "y", 3)
+    proj_c = join([part, p1, p3, lower, upper, mark(targets, SMALL)])
     proj_d = shift(proj_c, "c", 1)
 
-    near, near_other = error_and_other(0, students, after(proj, proj_c), proj_b, teacher, targets)
-    near_there = shift(near_other, "c", 1)
-    far, far_other = error_and_other(1, students, after(proj_c, near), proj_d, teacher, targets)
-    far_there = shift(far_other, "c", 1)
+    near, there = error_and_other(0, students, after(proj, proj_c), proj_b, teacher, targets)
+    near_there = shift(there, "c", 1)
+    far, there = error_and_other(1, students, after(proj_c, near), proj_d, teacher, targets)
+    far_there = shift(there, "c", 1)
 
     blocks = own_and_sum((2,), students, near, after(near_there, far))
     near_in = [shift(blocks[0], "y", 1), shift(blocks[1], "y", 3)]
-    partial = student_part(near, far, (proj, proj_b, proj_c, after(proj_d, *blocks)))
-    blocks = own_and_sum((1, 3, 0), students, near, after(near_there, partial[0]), near_in)
-    near_y = [blocks[2], shift(blocks[0], "y", 1), shift(blocks[1], "y", 3)]
     blocks = own_and_sum((2,), students, far, after(far_there, *blocks))
     far_in = [shift(blocks[0], "y", 1), shift(blocks[1], "y", 3)]
-    back2 = shift(after(partial[3], *blocks), "x", 2)
-    blocks = own_and_sum((1, 3, 0), students, far, far_there, far_in)
+    near_sum = own_and_sum((1, 3, 0), students, near, after(near_there, *blocks), near_in)
+    near_y = [near_sum[2], shift(near_sum[0], "y", 1), shift(near_sum[1], "y", 3)]
+    weights = (proj, proj_b, proj_c, after(proj_d, *far_in, near_sum[2]))
+    partial = student_part(near, far, weights)
+    back2 = shift(partial[3], "x", 2)
+    far_sum = own_and_sum((1, 3, 0), students, far, after(far_there, partial[0]), far_in)
+    ready = [after(b, *near_y[1:]) for b in far_sum[:2]]
+    far_y = [far_sum[2], shift(ready[0], "y", 1), shift(ready[1], "y", 3)]
 
     def over_y(terms):
         return in_vmem(
-            y_kernel, terms, [((WIDTH, ROWS), F32)] + [((WIDTH, ROWS), BF16)] * 3
+            y_kernel, terms, [((WIDTH, ROWS), F32)] + [((WIDTH, ROWS), BF16)] * 3, BIG
         )
 
-    near_z = over_y(near_y)
-    ready = after(blocks[0], *near_z), after(blocks[1], *near_z)
-    far_y = [blocks[2], shift(ready[0], "y", 1), shift(ready[1], "y", 3)]
+    near_z = over_y([after(near_y[0], *far_sum), *near_y[1:]])
     near_terms = [near_z[0]] + over("zl", near_z[1:])
-    back1 = shift(after(partial[1], *blocks), "x", 1)
-    back3 = shift(after(partial[2], *blocks), "x", 3)
-    far_z = over_y([after(far_y[0], back1, back2, back3, *near_terms), *far_y[1:]])
+    far_z = over_y([after(far_y[0], back2, *near_terms), *far_y[1:]])
     far_terms = [far_z[0]] + over("zl", far_z[1:])
-    far_part = in_vmem(z_kernel, far_terms, [((WIDTH, ROWS), BF16)])[0]
+    back1 = shift(after(partial[1], *far_z), "x", 1)
+    back3 = shift(after(partial[2], *far_z), "x", 3)
+    far_part = in_vmem(
+        z_kernel, [after(far_terms[0], back1, back3), *far_terms[1:]], [((WIDTH, ROWS), BF16)]
+    )[0]
     far_part = shift(far_part, "zh", 1)
     grad_student = in_vmem(
         student_sum_kernel, [partial[0], back1, back2, back3], [((TOK, DS), BF16)]

time: 165 us -> 155 us (0.939)
  waiting for transfers between devices: 80.5 us -> 65.8 us
  local copies, waits for them, and re-layouts: 0.01 us -> 3.04 us
  starting transfers between devices: 55.6 us -> 57.6 us
    ppermute x32 -> x33, waiting for transfers between devices: 80.5 us -> 65.8 us  [shift(): return lax.ppermute(array, axis, [(i, (i + by) % n) for i in range(n)])]
    unnamed x4 -> x8, local copies, waits for them, and re-layouts: 0.01 us -> 3.01 us
    ppermute x32 -> x33, starting transfers between devices: 55.6 us -> 57.6 us  [shift(): return lax.ppermute(array, axis, [(i, (i + by) % n) for i in range(n)])]
    pallas_call x15 -> x16, Pallas kernels: 27.8 us -> 27.8 us  [call(): pl.pallas_call(kernel, in_specs=in_specs or [ANY] * len(ins), out_specs=o...]
  transfers between devices with their start and end apart: 32 -> 33, of which waited for: 16 -> 13; matrix products, arithmetic and copies ran while one was open for 0% -> 0% of each run, Pallas kernels for 15% -> 17%
where the time goes in v2:
time: 155 us
  waiting for transfers between devices  65.8 us (42%)
  starting transfers between devices  57.6 us (37%)
  Pallas kernels  27.8 us (18%)
  local copies, waits for them, and re-layouts  3.04 us (2%)
    ppermute x33, waiting for transfers between devices, shift(): return lax.ppermute(array, axis, [(i, (i + by) % n) for i in range(n)])  65.8 us
    ppermute x33, starting transfers between devices, shift(): return lax.ppermute(array, axis, [(i, (i + by) % n) for i in range(n)])  57.6 us
    pallas_call x16, Pallas kernels, call(): pl.pallas_call(kernel, in_specs=in_specs or [ANY] * len(ins), out_specs=o...  27.8 us
  transfers between devices with their start and end apart: 33, of which 13 were waited for; matrix products, arithmetic and copies ran while one was open for 0% of the time, Pallas kernels for 17%

profile of v2, /device:TPU:32, one launch (start us, length us, event | category | flops | bytes accessed | tf_op | source)
XLA Modules:
  0.0 155.1 jit_solution(1785349448318519595)
XLA Ops:
  0.7 2.8 %collective-permute-start.2 = (bf16[128,2048]{1,0:T(8,128)(2,1)}, bf16[128,2048]{1,0:T(8,128)(2,1)S(1)}, u32[]{:S(2)}, u32[]{:S(2)}) collective-permute-start(bf16[128,2048]{1,0:T(8,128)(2,1)} %s0.11), channel_id=1, source_target_pairs={{0,12},{4,0},{8,4},{12,8},{1,13},{5,1},{9,5},{13,9},{2,14},{6,2},{... | collective-permute-start | bytes 1572872 | tf_op jit(solution)/shard_map/ppermute | solution.py:27
  3.6 0.8 collective-permute-start.1
  4.4 0.9 collective-permute-start
  5.3 1.6 %copy-done.1 = bf16[2048,512]{1,0:T(8,128)(2,1)S(1)} copy-done((bf16[2048,512]{1,0:T(8,128)(2,1)S(1)}, bf16[2048,512]{1,0:T(8,128)(2,1)}, u32[]{:S(2)}) %copy-start.1) | copy-done | bytes 2097176
  6.9 6.4 %collective-permute-start.3 = (bf16[512,512]{1,0:T(8,128)(2,1)S(1)}, bf16[512,512]{1,0:T(8,128)(2,1)S(1)}, u32[]{:S(2)}, u32[]{:S(2)}) collective-permute-start(bf16[512,512]{1,0:T(8,128)(2,1)S(1)} %shard_map.50), channel_id=1, source_target_pairs={{0,2},{2,0},{1,3},{3,1},{4,6},{6,4},{5,7},{7,5},{8,10},{10,8},{9,1... | collective-permute-start | bytes 1572872 | tf_op jit(solution)/shard_map/ppermute | solution.py:27
  13.3 13.7 %collective-permute-done.2.s3 = bf16[128,2048]{1,0:T(8,128)(2,1)S(1)} collective-permute-done((bf16[128,2048]{1,0:T(8,128)(2,1)}, bf16[128,2048]{1,0:T(8,128)(2,1)S(1)}, u32[]{:S(2)}, u32[]{:S(2)}) %collective-permute-start.2) | collective-permute-done | bytes 524320 | tf_op jit(solution)/shard_map/ppermute | solution.py:27
  26.9 3.6 %collective-permute-done.s1 = bf16[128,2048]{1,0:T(8,128)(2,1)S(1)} collective-permute-done((bf16[128,2048]{1,0:T(8,128)(2,1)}, bf16[128,2048]{1,0:T(8,128)(2,1)S(1)}, u32[]{:S(2)}, u32[]{:S(2)}) %collective-permute-start) | collective-permute-done | bytes 524320 | tf_op jit(solution)/shard_map/ppermute | solution.py:27
  30.5 0.4 shard_map.51
  30.9 5.4 %collective-permute-done.3.own = bf16[512,512]{1,0:T(8,128)(2,1)S(1)} collective-permute-done((bf16[512,512]{1,0:T(8,128)(2,1)S(1)}, bf16[512,512]{1,0:T(8,128)(2,1)S(1)}, u32[]{:S(2)}, u32[]{:S(2)}) %collective-permute-start.3) | collective-permute-done | bytes 524320 | tf_op jit(solution)/shard_map/ppermute | solution.py:27
  36.3 3.0 %collective-permute-start.6 = (bf16[512,512]{1,0:T(8,128)(2,1)S(1)}, bf16[512,512]{1,0:T(8,128)(2,1)S(1)}, u32[]{:S(2)}, u32[]{:S(2)}) collective-permute-start(bf16[512,512]{1,0:T(8,128)(2,1)S(1)} %collective-permute-done.3.own), channel_id=1, source_target_pairs={{0,192},{64,0},{128,64},{192,128},{1,193},{65,1},{129,65},{193,129... | collective-permute-start | bytes 1572872 | tf_op jit(solution)/shard_map/ppermute | solution.py:27
  39.3 2.1 %collective-permute-start.10 = (bf16[128,2048]{1,0:T(8,128)(2,1)S(1)}, bf16[128,2048]{1,0:T(8,128)(2,1)S(1)}, u32[]{:S(2)}, u32[]{:S(2)}) collective-permute-start(bf16[128,2048]{1,0:T(8,128)(2,1)S(1)} %get-tuple-element.50), channel_id=1, source_target_pairs={{0,8},{4,12},{8,0},{12,4},{1,9},{5,13},{9,1},{13,5},{2,10},{6,14},... | collective-permute-start | bytes 1572872 | tf_op jit(solution)/shard_map/ppermute | solution.py:27
  41.5 2.3 %collective-permute-start.11 = (bf16[128,2048]{1,0:T(8,128)(2,1)S(1)}, bf16[128,2048]{1,0:T(8,128)(2,1)S(1)}, u32[]{:S(2)}, u32[]{:S(2)}) collective-permute-start(bf16[128,2048]{1,0:T(8,128)(2,1)S(1)} %get-tuple-element.49), channel_id=1, source_target_pairs={{0,12},{4,0},{8,4},{12,8},{1,13},{5,1},{9,5},{13,9},{2,14},{6,2},{... | collective-permute-start | bytes 1572872 | tf_op jit(solution)/shard_map/ppermute | solution.py:27
  43.8 5.7 %collective-permute-done.6.p3 = bf16[512,512]{1,0:T(8,128)(2,1)S(1)} collective-permute-done((bf16[512,512]{1,0:T(8,128)(2,1)S(1)}, bf16[512,512]{1,0:T(8,128)(2,1)S(1)}, u32[]{:S(2)}, u32[]{:S(2)}) %collective-permute-start.6) | collective-permute-done | bytes 524320 | tf_op jit(solution)/shard_map/ppermute | solution.py:27
  49.6 3.8 %collective-permute-start.8 = (bf16[256,512]{1,0:T(8,128)(2,1)S(1)}, bf16[256,512]{1,0:T(8,128)(2,1)S(1)}, u32[]{:S(2)}, u32[]{:S(2)}) collective-permute-start(bf16[256,512]{1,0:T(8,128)(2,1)S(1)} %slice.9), channel_id=1, source_target_pairs={{0,192},{64,0},{128,64},{192,128},{1,193},{65,1},{129,65},{193,129... | collective-permute-start | bytes 786440 | tf_op jit(solution)/shard_map/ppermute | solution.py:27
  53.5 2.3 %collective-permute-done.10.refs_1_.t2 = bf16[128,2048]{1,0:T(8,128)(2,1)S(1)} collective-permute-done((bf16[128,2048]{1,0:T(8,128)(2,1)S(1)}, bf16[128,2048]{1,0:T(8,128)(2,1)S(1)}, u32[]{:S(2)}, u32[]{:S(2)}) %collective-permute-start.10) | collective-permute-done | bytes 524320 | tf_op jit(solution)/shard_map/ppermute | solution.py:27
  55.8 8.5 %collective-permute-done.11.refs_2_.t3 = bf16[128,2048]{1,0:T(8,128)(2,1)S(1)} collective-permute-done((bf16[128,2048]{1,0:T(8,128)(2,1)S(1)}, bf16[128,2048]{1,0:T(8,128)(2,1)S(1)}, u32[]{:S(2)}, u32[]{:S(2)}) %collective-permute-start.11) | collective-permute-done | bytes 524320 | tf_op jit(solution)/shard_map/ppermute | solution.py:27
  64.9 0.7 copy-done
  65.5 0.7 copy-done.2
  66.3 5.8 %shard_map.54 = (bf16[512,1024]{1,0:T(8,128)(2,1)S(1)}, bf16[512,2048]{1,0:T(8,128)(2,1)S(1)}) custom-call(bf16[128,2048]{1,0:T(8,128)(2,1)S(1)} %copy-done, bf16[128,2048]{1,0:T(8,128)(2,1)S(1)} %collective-permute-done.s1, bf16[128,2048]{1,0:T(8,128)(2,1)S(1)} %collective-permute-done.1.s2, bf16[128,2048]{1,0:T(8,128)(2,1)S(1)} %collective-permute-done.2.s3, ...), custom_call_target="tpu_custom_call" | custom-call | flops 99999997952 | bytes 1 | tf_op jit(solution)/shard_map/pallas_call | solution.py:55
  72.0 0.3 collective-permute-start.12
  72.3 5.8 %shard_map.55 = (bf16[512,1024]{1,0:T(8,128)(2,1)S(1)}, bf16[512,2048]{1,0:T(8,128)(2,1)S(1)}) custom-call(bf16[128,2048]{1,0:T(8,128)(2,1)S(1)} %copy-done, bf16[128,2048]{1,0:T(8,128)(2,1)S(1)} %collective-permute-done.s1, bf16[128,2048]{1,0:T(8,128)(2,1)S(1)} %collective-permute-done.1.s2, bf16[128,2048]{1,0:T(8,128)(2,1)S(1)} %collective-permute-done.2.s3, ...), custom_call_target="tpu_custom_call" | custom-call | flops 99999997952 | bytes 1 | tf_op jit(solution)/shard_map/pallas_call | solution.py:55
  78.1 0.5 collective-permute-start.14
  78.7 1.1 shard_map.56
  79.8 0.4 collective-permute-start.15
  80.2 2.9 %collective-permute-start.16 = (bf16[256,512]{1,0:T(8,128)(2,1)S(1)}, bf16[256,512]{1,0:T(8,128)(2,1)S(1)}, u32[]{:S(2)}, u32[]{:S(2)}) collective-permute-start(bf16[256,512]{1,0:T(8,128)(2,1)S(1)} %get-tuple-element.60), channel_id=1, source_target_pairs={{0,192},{64,0},{128,64},{192,128},{1,193},{65,1},{129,65},{193,129... | collective-permute-start | bytes 786440 | tf_op jit(solution)/shard_map/ppermute | solution.py:27
  83.1 1.1 shard_map.57
  84.3 3.2 %collective-permute-start.18 = (bf16[256,512]{1,0:T(8,128)(2,1)S(1)}, bf16[256,512]{1,0:T(8,128)(2,1)S(1)}, u32[]{:S(2)}, u32[]{:S(2)}) collective-permute-start(bf16[256,512]{1,0:T(8,128)(2,1)S(1)} %get-tuple-element.63), channel_id=1, source_target_pairs={{0,192},{64,0},{128,64},{192,128},{1,193},{65,1},{129,65},{193,129... | collective-permute-start | bytes 786440 | tf_op jit(solution)/shard_map/ppermute | solution.py:27
  87.5 2.7 %collective-permute-done.15.rest_0_ = bf16[256,512]{1,0:T(8,128)(2,1)S(1)} collective-permute-done((bf16[256,512]{1,0:T(8,128)(2,1)S(1)}, bf16[256,512]{1,0:T(8,128)(2,1)S(1)}, u32[]{:S(2)}, u32[]{:S(2)}) %collective-permute-start.15) | collective-permute-done | bytes 262176 | tf_op jit(solution)/shard_map/ppermute | solution.py:27
  90.2 2.4 %shard_map.58 = (bf16[512,512]{1,0:T(8,128)(2,1)S(1)}, bf16[512,512]{1,0:T(8,128)(2,1)S(1)}, bf16[512,512]{1,0:T(8,128)(2,1)S(1)}) custom-call(bf16[128,2048]{1,0:T(8,128)(2,1)S(1)} %copy-done, bf16[128,2048]{1,0:T(8,128)(2,1)S(1)} %collective-permute-done.s1, bf16[128,2048]{1,0:T(8,128)(2,1)S(1)} %collective-permute-done.1.s2, ...), custom_call_target="tpu_custom_call" | custom-call | flops 1 | bytes 1 | tf_op jit(solution)/shard_map/pallas_call | solution.py:55
  92.7 1.2 collective-permute-start.19
  93.9 2.2 %collective-permute-start.20 = (bf16[512,512]{1,0:T(8,128)(2,1)S(1)}, bf16[512,512]{1,0:T(8,128)(2,1)S(1)}, u32[]{:S(2)}, u32[]{:S(2)}) collective-permute-start(bf16[512,512]{1,0:T(8,128)(2,1)S(1)} %get-tuple-element.74), channel_id=1, source_target_pairs={{0,192},{64,0},{128,64},{192,128},{1,193},{65,1},{129,65},{193,129... | collective-permute-start | bytes 1572872 | tf_op jit(solution)/shard_map/ppermute | solution.py:27
  96.1 6.1 %shard_map.59 = (bf16[128,2048]{1,0:T(8,128)(2,1)S(1)}, bf16[128,2048]{1,0:T(8,128)(2,1)S(1)}, bf16[128,2048]{1,0:T(8,128)(2,1)S(1)}, bf16[128,2048]{1,0:T(8,128)(2,1)S(1)}) custom-call(bf16[512,1024]{1,0:T(8,128)(2,1)S(1)} %get-tuple-element.53.error.near, bf16[512,1024]{1,0:T(8,128)(2,1)S(1)} %get-tuple-element.56.error.far, ...), custom_call_target="tpu_custom_call" | custom-call | flops 99999997952 | bytes 1 | tf_op jit(solution)/shard_map/pallas_call | solution.py:55
  102.2 2.5 %shard_map.60 = (bf16[512,512]{1,0:T(8,128)(2,1)S(1)}, bf16[512,512]{1,0:T(8,128)(2,1)S(1)}, bf16[512,512]{1,0:T(8,128)(2,1)S(1)}) custom-call(bf16[128,2048]{1,0:T(8,128)(2,1)S(1)} %copy-done, bf16[128,2048]{1,0:T(8,128)(2,1)S(1)} %collective-permute-done.s1, bf16[128,2048]{1,0:T(8,128)(2,1)S(1)} %collective-permute-done.1.s2, ...), custom_call_target="tpu_custom_call" | custom-call | flops 1 | bytes 1 | tf_op jit(solution)/shard_map/pallas_call | solution.py:55
  104.6 2.8 %collective-permute-start.24 = (bf16[128,2048]{1,0:T(8,128)(2,1)S(1)}, bf16[128,2048]{1,0:T(8,128)(2,1)S(1)}, u32[]{:S(2)}, u32[]{:S(2)}) collective-permute-start(bf16[128,2048]{1,0:T(8,128)(2,1)S(1)} %get-tuple-element.79), channel_id=1, source_target_pairs={{0,8},{4,12},{8,0},{12,4},{1,9},{5,13},{9,1},{13,5},{2,10},{6,14},... | collective-permute-start | bytes 1572872 | tf_op jit(solution)/shard_map/ppermute | solution.py:27
  107.5 3.1 %collective-permute-start.26 = (bf16[512,512]{1,0:T(8,128)(2,1)S(1)}, bf16[512,512]{1,0:T(8,128)(2,1)S(1)}, u32[]{:S(2)}, u32[]{:S(2)}) collective-permute-start(bf16[512,512]{1,0:T(8,128)(2,1)S(1)} %get-tuple-element.82), channel_id=1, source_target_pairs={{0,192},{64,0},{128,64},{192,128},{1,193},{65,1},{129,65},{193,129... | collective-permute-start | bytes 1572872 | tf_op jit(solution)/shard_map/ppermute | solution.py:27
  111.0 1.7 %collective-permute-start.21 = (bf16[512,128]{1,0:T(8,128)(2,1)S(1)}, bf16[512,128]{1,0:T(8,128)(2,1)S(1)}, u32[]{:S(2)}, u32[]{:S(2)}) collective-permute-start(bf16[512,128]{1,0:T(8,128)(2,1)S(1)} %get-tuple-element.76), channel_id=1, source_target_pairs={{0,16},{16,32},{32,48},{48,0},{1,17},{17,33},{33,49},{49,1},{2,18}... | collective-permute-start | bytes 393224 | tf_op jit(solution)/shard_map/ppermute | solution.py:27
  112.6 4.2 %collective-permute-done.22.p2 = bf16[512,128]{1,0:T(8,128)(2,1)S(1)} collective-permute-done((bf16[512,128]{1,0:T(8,128)(2,1)S(1)}, bf16[512,128]{1,0:T(8,128)(2,1)S(1)}, u32[]{:S(2)}, u32[]{:S(2)}) %collective-permute-start.22) | collective-permute-done | bytes 131104 | tf_op jit(solution)/shard_map/ppermute | solution.py:27
  116.8 5.5 %collective-permute-start.23 = (bf16[512,128]{1,0:T(8,128)(2,1)S(1)}, bf16[512,128]{1,0:T(8,128)(2,1)S(1)}, u32[]{:S(2)}, u32[]{:S(2)}) collective-permute-start(bf16[512,128]{1,0:T(8,128)(2,1)S(1)} %get-tuple-element.78), channel_id=1, source_target_pairs={{0,48},{16,0},{32,16},{48,32},{1,49},{17,1},{33,17},{49,33},{2,50}... | collective-permute-start | bytes 393224 | tf_op jit(solution)/shard_map/ppermute | solution.py:27
  122.3 5.1 %collective-permute-done.23.p3 = bf16[512,128]{1,0:T(8,128)(2,1)S(1)} collective-permute-done((bf16[512,128]{1,0:T(8,128)(2,1)S(1)}, bf16[512,128]{1,0:T(8,128)(2,1)S(1)}, u32[]{:S(2)}, u32[]{:S(2)}) %collective-permute-start.23) | collective-permute-done | bytes 131104 | tf_op jit(solution)/shard_map/ppermute | solution.py:27
  127.7 3.2 %collective-permute-start.28 = (bf16[128,2048]{1,0:T(8,128)(2,1)S(1)}, bf16[128,2048]{1,0:T(8,128)(2,1)S(1)}, u32[]{:S(2)}, u32[]{:S(2)}) collective-permute-start(bf16[128,2048]{1,0:T(8,128)(2,1)S(1)} %get-tuple-element.90), channel_id=1, source_target_pairs={{0,12},{4,0},{8,4},{12,8},{1,13},{5,1},{9,5},{13,9},{2,14},{6,2},{... | collective-permute-start | bytes 1572872 | tf_op jit(solution)/shard_map/ppermute | solution.py:27
  131.1 2.2 %collective-permute-start.31 = (bf16[512,128]{1,0:T(8,128)(2,1)S(1)}, bf16[512,128]{1,0:T(8,128)(2,1)S(1)}, u32[]{:S(2)}, u32[]{:S(2)}) collective-permute-start(bf16[512,128]{1,0:T(8,128)(2,1)S(1)} %get-tuple-element.86), channel_id=1, source_target_pairs={{0,48},{16,0},{32,16},{48,32},{1,49},{17,1},{33,17},{49,33},{2,50}... | collective-permute-start | bytes 393224 | tf_op jit(solution)/shard_map/ppermute | solution.py:27
  133.4 1.5 collective-permute-start.29
  134.8 3.2 %collective-permute-done.27.p1 = bf16[128,2048]{1,0:T(8,128)(2,1)S(1)} collective-permute-done((bf16[128,2048]{1,0:T(8,128)(2,1)S(1)}, bf16[128,2048]{1,0:T(8,128)(2,1)S(1)}, u32[]{:S(2)}, u32[]{:S(2)}) %collective-permute-start.27) | collective-permute-done | bytes 524320 | tf_op jit(solution)/shard_map/ppermute | solution.py:27
  138.1 5.7 %collective-permute-done.31.p3 = bf16[512,128]{1,0:T(8,128)(2,1)S(1)} collective-permute-done((bf16[512,128]{1,0:T(8,128)(2,1)S(1)}, bf16[512,128]{1,0:T(8,128)(2,1)S(1)}, u32[]{:S(2)}, u32[]{:S(2)}) %collective-permute-start.31) | collective-permute-done | bytes 131104 | tf_op jit(solution)/shard_map/ppermute | solution.py:27
  143.9 3.8 %collective-permute-start.32 = (bf16[512,128]{1,0:T(8,128)(2,1)S(1)}, bf16[512,128]{1,0:T(8,128)(2,1)S(1)}, u32[]{:S(2)}, u32[]{:S(2)}) collective-permute-start(bf16[512,128]{1,0:T(8,128)(2,1)S(1)} %shard_map.63), channel_id=1, source_target_pairs={{0,2},{2,0},{1,3},{3,1},{4,6},{6,4},{5,7},{7,5},{8,10},{10,8},{9,1... | collective-permute-start | bytes 393224 | tf_op jit(solution)/shard_map/ppermute | solution.py:27
  147.7 1.0 shard_map.65
  148.7 5.5 %collective-permute-done.32.far = bf16[512,128]{1,0:T(8,128)(2,1)S(1)} collective-permute-done((bf16[512,128]{1,0:T(8,128)(2,1)S(1)}, bf16[512,128]{1,0:T(8,128)(2,1)S(1)}, u32[]{:S(2)}, u32[]{:S(2)}) %collective-permute-start.32) | collective-permute-done | bytes 131104 | tf_op jit(solution)/shard_map/ppermute | solution.py:27
  154.2 0.8 shard_map.64
  (44 shorter events, 2.0 us)
Async XLA Ops:
  0.6 29.9 %collective-permute-start.4 = (bf16[2048,512]{1,0:T(8,128)(2,1)}, bf16[2048,512]{1,0:T(8,128)(2,1)S(1)}, u32[]{:S(2)}, u32[]{:S(2)}) collective-permute-start(bf16[2048,512]{1,0:T(8,128)(2,1)} %wa.1), channel_id=1, source_target_pairs={{0,1},{1,0},{2,3},{3,2},{4,5},{5,4},{6,7},{7,6},{8,9},{9,8},{10,11... | collective-permute-start | bytes 6291464 | tf_op jit(solution)/shard_map/ppermute | solution.py:27
  0.7 26.2 %collective-permute-start.2 = (bf16[128,2048]{1,0:T(8,128)(2,1)}, bf16[128,2048]{1,0:T(8,128)(2,1)S(1)}, u32[]{:S(2)}, u32[]{:S(2)}) collective-permute-start(bf16[128,2048]{1,0:T(8,128)(2,1)} %s0.11), channel_id=1, source_target_pairs={{0,12},{4,0},{8,4},{12,8},{1,13},{5,1},{9,5},{13,9},{2,14},{6,2},{... | collective-permute-start | bytes 1572872 | tf_op jit(solution)/shard_map/ppermute | solution.py:27
  3.6 23.4 %collective-permute-start.1 = (bf16[128,2048]{1,0:T(8,128)(2,1)}, bf16[128,2048]{1,0:T(8,128)(2,1)S(1)}, u32[]{:S(2)}, u32[]{:S(2)}) collective-permute-start(bf16[128,2048]{1,0:T(8,128)(2,1)} %s0.11), channel_id=1, source_target_pairs={{0,8},{4,12},{8,0},{12,4},{1,9},{5,13},{9,1},{13,5},{2,10},{6,14},... | collective-permute-start | bytes 1572872 | tf_op jit(solution)/shard_map/ppermute | solution.py:27
  4.4 26.1 %collective-permute-start = (bf16[128,2048]{1,0:T(8,128)(2,1)}, bf16[128,2048]{1,0:T(8,128)(2,1)S(1)}, u32[]{:S(2)}, u32[]{:S(2)}) collective-permute-start(bf16[128,2048]{1,0:T(8,128)(2,1)} %s0.11), channel_id=1, source_target_pairs={{0,4},{4,8},{8,12},{12,0},{1,5},{5,9},{9,13},{13,1},{2,6},{6,10},{... | collective-permute-start | bytes 1572872 | tf_op jit(solution)/shard_map/ppermute | solution.py:27
  5.3 1.6 %copy-start.1 = (bf16[2048,512]{1,0:T(8,128)(2,1)S(1)}, bf16[2048,512]{1,0:T(8,128)(2,1)}, u32[]{:S(2)}) copy-start(bf16[2048,512]{1,0:T(8,128)(2,1)} %wa.1) | copy-start | bytes 6291460
  6.8 23.7 %copy-start.3 = (bf16[128,8192]{1,0:T(8,128)(2,1)S(1)}, bf16[128,8192]{1,0:T(8,128)(2,1)}, u32[]{:S(2)}) copy-start(bf16[128,8192]{1,0:T(8,128)(2,1)} %teacher.4) | copy-start | bytes 6291460
  6.9 29.4 %collective-permute-start.3 = (bf16[512,512]{1,0:T(8,128)(2,1)S(1)}, bf16[512,512]{1,0:T(8,128)(2,1)S(1)}, u32[]{:S(2)}, u32[]{:S(2)}) collective-permute-start(bf16[512,512]{1,0:T(8,128)(2,1)S(1)} %shard_map.50), channel_id=1, source_target_pairs={{0,2},{2,0},{1,3},{3,1},{4,6},{6,4},{5,7},{7,5},{8,10},{10,8},{9,1... | collective-permute-start | bytes 1572872 | tf_op jit(solution)/shard_map/ppermute | solution.py:27
  36.3 13.2 %collective-permute-start.6 = (bf16[512,512]{1,0:T(8,128)(2,1)S(1)}, bf16[512,512]{1,0:T(8,128)(2,1)S(1)}, u32[]{:S(2)}, u32[]{:S(2)}) collective-permute-start(bf16[512,512]{1,0:T(8,128)(2,1)S(1)} %collective-permute-done.3.own), channel_id=1, source_target_pairs={{0,192},{64,0},{128,64},{192,128},{1,193},{65,1},{129,65},{193,129... | collective-permute-start | bytes 1572872 | tf_op jit(solution)/shard_map/ppermute | solution.py:27
  39.3 14.0 %collective-permute-start.5 = (bf16[512,512]{1,0:T(8,128)(2,1)S(1)}, bf16[512,512]{1,0:T(8,128)(2,1)S(1)}, u32[]{:S(2)}, u32[]{:S(2)}) collective-permute-start(bf16[512,512]{1,0:T(8,128)(2,1)S(1)} %collective-permute-done.3.own), channel_id=1, source_target_pairs={{0,64},{64,128},{128,192},{192,0},{1,65},{65,129},{129,193},{193,1... | collective-permute-start | bytes 1572872 | tf_op jit(solution)/shard_map/ppermute | solution.py:27
  39.3 16.4 %collective-permute-start.10 = (bf16[128,2048]{1,0:T(8,128)(2,1)S(1)}, bf16[128,2048]{1,0:T(8,128)(2,1)S(1)}, u32[]{:S(2)}, u32[]{:S(2)}) collective-permute-start(bf16[128,2048]{1,0:T(8,128)(2,1)S(1)} %get-tuple-element.50), channel_id=1, source_target_pairs={{0,8},{4,12},{8,0},{12,4},{1,9},{5,13},{9,1},{13,5},{2,10},{6,14},... | collective-permute-start | bytes 1572872 | tf_op jit(solution)/shard_map/ppermute | solution.py:27
  41.5 22.7 %collective-permute-start.11 = (bf16[128,2048]{1,0:T(8,128)(2,1)S(1)}, bf16[128,2048]{1,0:T(8,128)(2,1)S(1)}, u32[]{:S(2)}, u32[]{:S(2)}) collective-permute-start(bf16[128,2048]{1,0:T(8,128)(2,1)S(1)} %get-tuple-element.49), channel_id=1, source_target_pairs={{0,12},{4,0},{8,4},{12,8},{1,13},{5,1},{9,5},{13,9},{2,14},{6,2},{... | collective-permute-start | bytes 1572872 | tf_op jit(solution)/shard_map/ppermute | solution.py:27
  43.8 20.7 %collective-permute-start.9 = (bf16[128,2048]{1,0:T(8,128)(2,1)S(1)}, bf16[128,2048]{1,0:T(8,128)(2,1)S(1)}, u32[]{:S(2)}, u32[]{:S(2)}) collective-permute-start(bf16[128,2048]{1,0:T(8,128)(2,1)S(1)} %get-tuple-element.48), channel_id=1, source_target_pairs={{0,4},{4,8},{8,12},{12,0},{1,5},{5,9},{9,13},{13,1},{2,6},{6,10},{... | collective-permute-start | bytes 1572872 | tf_op jit(solution)/shard_map/ppermute | solution.py:27
  49.6 14.9 %collective-permute-start.8 = (bf16[256,512]{1,0:T(8,128)(2,1)S(1)}, bf16[256,512]{1,0:T(8,128)(2,1)S(1)}, u32[]{:S(2)}, u32[]{:S(2)}) collective-permute-start(bf16[256,512]{1,0:T(8,128)(2,1)S(1)} %slice.9), channel_id=1, source_target_pairs={{0,192},{64,0},{128,64},{192,128},{1,193},{65,1},{129,65},{193,129... | collective-permute-start | bytes 786440 | tf_op jit(solution)/shard_map/ppermute | solution.py:27
  53.4 11.1 %collective-permute-start.7 = (bf16[256,512]{1,0:T(8,128)(2,1)S(1)}, bf16[256,512]{1,0:T(8,128)(2,1)S(1)}, u32[]{:S(2)}, u32[]{:S(2)}) collective-permute-start(bf16[256,512]{1,0:T(8,128)(2,1)S(1)} %slice.8), channel_id=1, source_target_pairs={{0,64},{64,128},{128,192},{192,0},{1,65},{65,129},{129,193},{193,1... | collective-permute-start | bytes 786440 | tf_op jit(solution)/shard_map/ppermute | solution.py:27
  64.5 1.0 copy-start
  64.5 1.8 %copy-start.2 = (bf16[2048,512]{1,0:T(8,128)(2,1)S(1)}, bf16[2048,512]{1,0:T(8,128)(2,1)}, u32[]{:S(2)}) copy-start(bf16[2048,512]{1,0:T(8,128)(2,1)} %wa.1) | copy-start | bytes 6291460
  64.8 7.6 %collective-permute-start.13 = (bf16[2048,512]{1,0:T(8,128)(2,1)S(1)}, bf16[2048,512]{1,0:T(8,128)(2,1)S(1)}, u32[]{:S(2)}, u32[]{:S(2)}) collective-permute-start(bf16[2048,512]{1,0:T(8,128)(2,1)S(1)} %shard_map.53.w_own.wc), channel_id=1, source_target_pairs={{0,1},{1,0},{2,3},{3,2},{4,5},{5,4},{6,7},{7,6},{8,9},{9,8},{10,11... | collective-permute-start | bytes 6291464 | tf_op jit(solution)/shard_map/ppermute | solution.py:27
  72.0 6.6 %collective-permute-start.12 = (bf16[512,2048]{1,0:T(8,128)(2,1)S(1)}, bf16[512,2048]{1,0:T(8,128)(2,1)S(1)}, u32[]{:S(2)}, u32[]{:S(2)}) collective-permute-start(bf16[512,2048]{1,0:T(8,128)(2,1)S(1)} %get-tuple-element.54), channel_id=1, source_target_pairs={{0,1},{1,0},{2,3},{3,2},{4,5},{5,4},{6,7},{7,6},{8,9},{9,8},{10,11... | collective-permute-start | bytes 6291464 | tf_op jit(solution)/shard_map/ppermute | solution.py:27
  78.1 5.0 %collective-permute-start.14 = (bf16[512,2048]{1,0:T(8,128)(2,1)S(1)}, bf16[512,2048]{1,0:T(8,128)(2,1)S(1)}, u32[]{:S(2)}, u32[]{:S(2)}) collective-permute-start(bf16[512,2048]{1,0:T(8,128)(2,1)S(1)} %get-tuple-element.57), channel_id=1, source_target_pairs={{0,1},{1,0},{2,3},{3,2},{4,5},{5,4},{6,7},{7,6},{8,9},{9,8},{10,11... | collective-permute-start | bytes 6291464 | tf_op jit(solution)/shard_map/ppermute | solution.py:27
  79.8 10.4 %collective-permute-start.15 = (bf16[256,512]{1,0:T(8,128)(2,1)S(1)}, bf16[256,512]{1,0:T(8,128)(2,1)S(1)}, u32[]{:S(2)}, u32[]{:S(2)}) collective-permute-start(bf16[256,512]{1,0:T(8,128)(2,1)S(1)} %get-tuple-element.59), channel_id=1, source_target_pairs={{0,64},{64,128},{128,192},{192,0},{1,65},{65,129},{129,193},{193,1... | collective-permute-start | bytes 786440 | tf_op jit(solution)/shard_map/ppermute | solution.py:27
  80.2 10.1 %collective-permute-start.16 = (bf16[256,512]{1,0:T(8,128)(2,1)S(1)}, bf16[256,512]{1,0:T(8,128)(2,1)S(1)}, u32[]{:S(2)}, u32[]{:S(2)}) collective-permute-start(bf16[256,512]{1,0:T(8,128)(2,1)S(1)} %get-tuple-element.60), channel_id=1, source_target_pairs={{0,192},{64,0},{128,64},{192,128},{1,193},{65,1},{129,65},{193,129... | collective-permute-start | bytes 786440 | tf_op jit(solution)/shard_map/ppermute | solution.py:27
  84.2 11.9 %collective-permute-start.17 = (bf16[256,512]{1,0:T(8,128)(2,1)S(1)}, bf16[256,512]{1,0:T(8,128)(2,1)S(1)}, u32[]{:S(2)}, u32[]{:S(2)}) collective-permute-start(bf16[256,512]{1,0:T(8,128)(2,1)S(1)} %get-tuple-element.62), channel_id=1, source_target_pairs={{0,64},{64,128},{128,192},{192,0},{1,65},{65,129},{129,193},{193,1... | collective-permute-start | bytes 786440 | tf_op jit(solution)/shard_map/ppermute | solution.py:27
  84.3 11.8 %collective-permute-start.18 = (bf16[256,512]{1,0:T(8,128)(2,1)S(1)}, bf16[256,512]{1,0:T(8,128)(2,1)S(1)}, u32[]{:S(2)}, u32[]{:S(2)}) collective-permute-start(bf16[256,512]{1,0:T(8,128)(2,1)S(1)} %get-tuple-element.63), channel_id=1, source_target_pairs={{0,192},{64,0},{128,64},{192,128},{1,193},{65,1},{129,65},{193,129... | collective-permute-start | bytes 786440 | tf_op jit(solution)/shard_map/ppermute | solution.py:27
  92.7 14.7 %collective-permute-start.19 = (bf16[512,512]{1,0:T(8,128)(2,1)S(1)}, bf16[512,512]{1,0:T(8,128)(2,1)S(1)}, u32[]{:S(2)}, u32[]{:S(2)}) collective-permute-start(bf16[512,512]{1,0:T(8,128)(2,1)S(1)} %get-tuple-element.73), channel_id=1, source_target_pairs={{0,64},{64,128},{128,192},{192,0},{1,65},{65,129},{129,193},{193,1... | collective-permute-start | bytes 1572872 | tf_op jit(solution)/shard_map/ppermute | solution.py:27
  93.9 13.5 %collective-permute-start.20 = (bf16[512,512]{1,0:T(8,128)(2,1)S(1)}, bf16[512,512]{1,0:T(8,128)(2,1)S(1)}, u32[]{:S(2)}, u32[]{:S(2)}) collective-permute-start(bf16[512,512]{1,0:T(8,128)(2,1)S(1)} %get-tuple-element.74), channel_id=1, source_target_pairs={{0,192},{64,0},{128,64},{192,128},{1,193},{65,1},{129,65},{193,129... | collective-permute-start | bytes 1572872 | tf_op jit(solution)/shard_map/ppermute | solution.py:27
  104.6 22.7 %collective-permute-start.24 = (bf16[128,2048]{1,0:T(8,128)(2,1)S(1)}, bf16[128,2048]{1,0:T(8,128)(2,1)S(1)}, u32[]{:S(2)}, u32[]{:S(2)}) collective-permute-start(bf16[128,2048]{1,0:T(8,128)(2,1)S(1)} %get-tuple-element.79), channel_id=1, source_target_pairs={{0,8},{4,12},{8,0},{12,4},{1,9},{5,13},{9,1},{13,5},{2,10},{6,14},... | collective-permute-start | bytes 1572872 | tf_op jit(solution)/shard_map/ppermute | solution.py:27
  107.4 19.9 %collective-permute-start.25 = (bf16[512,512]{1,0:T(8,128)(2,1)S(1)}, bf16[512,512]{1,0:T(8,128)(2,1)S(1)}, u32[]{:S(2)}, u32[]{:S(2)}) collective-permute-start(bf16[512,512]{1,0:T(8,128)(2,1)S(1)} %get-tuple-element.81), channel_id=1, source_target_pairs={{0,64},{64,128},{128,192},{192,0},{1,65},{65,129},{129,193},{193,1... | collective-permute-start | bytes 1572872 | tf_op jit(solution)/shard_map/ppermute | solution.py:27
  107.5 19.8 %collective-permute-start.26 = (bf16[512,512]{1,0:T(8,128)(2,1)S(1)}, bf16[512,512]{1,0:T(8,128)(2,1)S(1)}, u32[]{:S(2)}, u32[]{:S(2)}) collective-permute-start(bf16[512,512]{1,0:T(8,128)(2,1)S(1)} %get-tuple-element.82), channel_id=1, source_target_pairs={{0,192},{64,0},{128,64},{192,128},{1,193},{65,1},{129,65},{193,129... | collective-permute-start | bytes 1572872 | tf_op jit(solution)/shard_map/ppermute | solution.py:27
  110.9 6.0 %collective-permute-start.22 = (bf16[512,128]{1,0:T(8,128)(2,1)S(1)}, bf16[512,128]{1,0:T(8,128)(2,1)S(1)}, u32[]{:S(2)}, u32[]{:S(2)}) collective-permute-start(bf16[512,128]{1,0:T(8,128)(2,1)S(1)} %get-tuple-element.77), channel_id=1, source_target_pairs={{0,32},{16,48},{32,0},{48,16},{1,33},{17,49},{33,1},{49,17},{2,34}... | collective-permute-start | bytes 393224 | tf_op jit(solution)/shard_map/ppermute | solution.py:27
  111.0 11.3 %collective-permute-start.21 = (bf16[512,128]{1,0:T(8,128)(2,1)S(1)}, bf16[512,128]{1,0:T(8,128)(2,1)S(1)}, u32[]{:S(2)}, u32[]{:S(2)}) collective-permute-start(bf16[512,128]{1,0:T(8,128)(2,1)S(1)} %get-tuple-element.76), channel_id=1, source_target_pairs={{0,16},{16,32},{32,48},{48,0},{1,17},{17,33},{33,49},{49,1},{2,18}... | collective-permute-start | bytes 393224 | tf_op jit(solution)/shard_map/ppermute | solution.py:27
  116.8 10.5 %collective-permute-start.23 = (bf16[512,128]{1,0:T(8,128)(2,1)S(1)}, bf16[512,128]{1,0:T(8,128)(2,1)S(1)}, u32[]{:S(2)}, u32[]{:S(2)}) collective-permute-start(bf16[512,128]{1,0:T(8,128)(2,1)S(1)} %get-tuple-element.78), channel_id=1, source_target_pairs={{0,48},{16,0},{32,16},{48,32},{1,49},{17,1},{33,17},{49,33},{2,50}... | collective-permute-start | bytes 393224 | tf_op jit(solution)/shard_map/ppermute | solution.py:27
  127.6 10.5 %collective-permute-start.27 = (bf16[128,2048]{1,0:T(8,128)(2,1)S(1)}, bf16[128,2048]{1,0:T(8,128)(2,1)S(1)}, u32[]{:S(2)}, u32[]{:S(2)}) collective-permute-start(bf16[128,2048]{1,0:T(8,128)(2,1)S(1)} %get-tuple-element.88), channel_id=1, source_target_pairs={{0,4},{4,8},{8,12},{12,0},{1,5},{5,9},{9,13},{13,1},{2,6},{6,10},{... | collective-permute-start | bytes 1572872 | tf_op jit(solution)/shard_map/ppermute | solution.py:27
  127.7 10.4 %collective-permute-start.28 = (bf16[128,2048]{1,0:T(8,128)(2,1)S(1)}, bf16[128,2048]{1,0:T(8,128)(2,1)S(1)}, u32[]{:S(2)}, u32[]{:S(2)}) collective-permute-start(bf16[128,2048]{1,0:T(8,128)(2,1)S(1)} %get-tuple-element.90), channel_id=1, source_target_pairs={{0,12},{4,0},{8,4},{12,8},{1,13},{5,1},{9,5},{13,9},{2,14},{6,2},{... | collective-permute-start | bytes 1572872 | tf_op jit(solution)/shard_map/ppermute | solution.py:27
  130.9 7.2 %collective-permute-start.30 = (bf16[512,128]{1,0:T(8,128)(2,1)S(1)}, bf16[512,128]{1,0:T(8,128)(2,1)S(1)}, u32[]{:S(2)}, u32[]{:S(2)}) collective-permute-start(bf16[512,128]{1,0:T(8,128)(2,1)S(1)} %get-tuple-element.87), channel_id=1, source_target_pairs={{0,32},{16,48},{32,0},{48,16},{1,33},{17,49},{33,1},{49,17},{2,34}... | collective-permute-start | bytes 393224 | tf_op jit(solution)/shard_map/ppermute | solution.py:27
  131.1 12.6 %collective-permute-start.31 = (bf16[512,128]{1,0:T(8,128)(2,1)S(1)}, bf16[512,128]{1,0:T(8,128)(2,1)S(1)}, u32[]{:S(2)}, u32[]{:S(2)}) collective-permute-start(bf16[512,128]{1,0:T(8,128)(2,1)S(1)} %get-tuple-element.86), channel_id=1, source_target_pairs={{0,48},{16,0},{32,16},{48,32},{1,49},{17,1},{33,17},{49,33},{2,50}... | collective-permute-start | bytes 393224 | tf_op jit(solution)/shard_map/ppermute | solution.py:27
  133.4 10.4 %collective-permute-start.29 = (bf16[512,128]{1,0:T(8,128)(2,1)S(1)}, bf16[512,128]{1,0:T(8,128)(2,1)S(1)}, u32[]{:S(2)}, u32[]{:S(2)}) collective-permute-start(bf16[512,128]{1,0:T(8,128)(2,1)S(1)} %get-tuple-element.85), channel_id=1, source_target_pairs={{0,16},{16,32},{32,48},{48,0},{1,17},{17,33},{33,49},{49,1},{2,18}... | collective-permute-start | bytes 393224 | tf_op jit(solution)/shard_map/ppermute | solution.py:27
  143.9 10.4 %collective-permute-start.32 = (bf16[512,128]{1,0:T(8,128)(2,1)S(1)}, bf16[512,128]{1,0:T(8,128)(2,1)S(1)}, u32[]{:S(2)}, u32[]{:S(2)}) collective-permute-start(bf16[512,128]{1,0:T(8,128)(2,1)S(1)} %shard_map.63), channel_id=1, source_target_pairs={{0,2},{2,0},{1,3},{3,1},{4,6},{6,4},{5,7},{7,5},{8,10},{10,8},{9,1... | collective-permute-start | bytes 393224 | tf_op jit(solution)/shard_map/ppermute | solution.py:27

commit v3 on v2

v3 whole, which is shorter than its diff:
```python
import functools
import math

import jax
import jax.numpy as jnp
from jax import lax
from jax.experimental import pallas as pl
from jax.experimental.pallas import tpu as pltpu
from jax.sharding import Mesh
from jax.sharding import PartitionSpec as P

F32 = jnp.float32
BF16 = jnp.bfloat16
ALL = ("y", "zl", "x", "zh", "c")
ANY = pl.BlockSpec(memory_space=pl.ANY)
VMEM = pl.BlockSpec(memory_space=pltpu.VMEM)
N = 4
TOK, DS, WIDTH = 128, 2048, 512
BLOCK = DS // N
ROWS = BLOCK // N
BIG = 10**11
SMALL = 3 * 10**8
REST = 16


def shift(array, axis, by):
    n = lax.axis_size(axis)
    return lax.ppermute(array, axis, [(i, (i + by) % n) for i in range(n)])


def after(value, *done):
    return lax.optimization_barrier((*done, value))[-1]


def index(axis):
    return lax.axis_index(axis)


def columns(x_at, zh_at, c_at):
    return pl.ds(pl.multiple_of(((x_at * 2 + zh_at) * 2 + c_at) * WIDTH, WIDTH), WIDTH)


def place(at, size):
    return pl.ds(pl.multiple_of(at * size, size), size)


def pieces(zh, c):
    return ((zh, c), (zh, 1 - c), (1 - zh, c), (1 - zh, 1 - c))


def dot(a, b, da, db):
    return lax.dot_general(a, b, (((da,), (db,)), ((), ())), preferred_element_type=F32)


def call(kernel, ins, out_shapes, scratch, mib, flops=1, out_specs=None, in_specs=None):
    return pl.pallas_call(
        kernel,
        in_specs=in_specs or [ANY] * len(ins),
        out_specs=out_specs or [ANY] * len(out_shapes),
        out_shape=[jax.ShapeDtypeStruct(s, t) for s, t in out_shapes],
        scratch_shapes=scratch,
        cost_estimate=pl.CostEstimate(flops=flops, bytes_accessed=1, transcendentals=0),
        compiler_params=pltpu.CompilerParams(vmem_limit_bytes=mib * 2**20),
    )(*ins)


def run(pairs, sems, first=0):
    copies = [
        pltpu.make_async_copy(src, dst, sems.at[first + i]) for i, (src, dst) in enumerate(pairs)
    ]
    for copy in copies:
        copy.start()
    return copies


def cut_kernel(proj, part, sem):
    copy = pltpu.make_async_copy(proj.at[place(index("y"), BLOCK), :], part, sem)
    copy.start()
    copy.wait()


def cut(proj):
    return call(
        cut_kernel,
        (proj,),
        [((BLOCK, WIDTH), BF16)],
        [pltpu.SemaphoreType.DMA],
        4,
        out_specs=[VMEM],
    )[0]


def split_kernel(teacher, student, o1, o3, o2, sems):
    x, zh, c = (index(a) for a in ("x", "zh", "c"))
    pairs = []
    for s, out in ((1, o1), (3, o3), (2, o2)):
        pairs.append((student, out.at[pl.ds(TOK, TOK), :]))
        for j, (zh_at, c_at) in enumerate(pieces(zh, c)):
            pairs.append(
                (
                    teacher.at[:, columns((x + s) % N, zh_at, c_at)],
                    out.at[pl.ds(0, TOK), pl.ds(j * WIDTH, WIDTH)],
                )
            )
    for copy in run(pairs, sems):
        copy.wait()


def split(teacher, student):
    return call(
        split_kernel,
        (teacher, student),
        [((2 * TOK, 4 * WIDTH), BF16)] * 3,
        [pltpu.SemaphoreType.DMA((15,))],
        8,
        out_specs=[VMEM] * 3,
    )


def relay_kernel(part, p1, p3, lower, upper, sems):
    half = BLOCK // 2
    pairs = [
        (p1.at[:half, :], lower.at[:half, :]),
        (part.at[BLOCK - REST :, :], lower.at[half:, :]),
        (p3.at[half - REST :, :], upper.at[:half, :]),
        (part.at[:REST, :], upper.at[half:, :]),
    ]
    for copy in run(pairs, sems):
        copy.wait()


def relay(*ins):
    return call(
        relay_kernel,
        ins,
        [((BLOCK // 2 + REST, WIDTH), BF16)] * 2,
        [pltpu.SemaphoreType.DMA((4,))],
        4,
        out_specs=[VMEM] * 2,
    )


def join_kernel(own, p1, p3, lower, upper, _, out, sems):
    y = index("y")
    half = BLOCK // 2

    def rows(s, first, size):
        return out.at[pl.ds(pl.multiple_of((y + N - s) % N * BLOCK + first, REST), size), :]

    pairs = [
        (own, rows(0, 0, BLOCK)),
        (p1, rows(1, 0, BLOCK - REST)),
        (p3, rows(3, REST, BLOCK - REST)),
        (lower.at[:half, :], rows(2, 0, half)),
        (lower.at[half:, :], rows(1, BLOCK - REST, REST)),
        (upper.at[:half, :], rows(2, half, half)),
        (upper.at[half:, :], rows(3, 0, REST)),
    ]
    for copy in run(pairs, sems):
        copy.wait()


def join(parts):
    return call(
        join_kernel,
        parts,
        [((DS, WIDTH), BF16)],
        [pltpu.SemaphoreType.DMA((7,))],
        8,
        out_specs=[VMEM],
    )[0]


def mark_kernel(*refs):
    refs[-1][...] = jnp.zeros_like(refs[-1])


def mark(values, flops):
    return call(mark_kernel, values, [((8, 128), F32)], [], 1, flops, out_specs=[VMEM])[0]


def error_kernel(half, student, b1, b2, b3, w_own, w_other, teacher, errors, grads, *rest):
    students, targets, sems = rest
    x, zh, c = (index(a) for a in ("x", "zh", "c"))
    zh_at = zh if half == 0 else 1 - zh
    blocks = (b1, b2, b3)
    rows = [pl.ds(s * TOK, TOK) for s in range(N)]
    loads = run(
        [(student, students.at[rows[0], :])]
        + [(block.at[rows[1], :], students.at[row, :]) for block, row in zip(blocks, rows[1:])]
        + [
            (teacher.at[:, columns(x, zh_at, c_at)], targets.at[:, pl.ds(j * WIDTH, WIDTH)])
            for j, c_at in enumerate((c, 1 - c))
        ],
        sems,
    )
    for copy in loads:
        copy.wait()

    def one(j, weights):
        def step(i, _):
            here = j * WIDTH + i * 256
            cols = pl.ds(pl.multiple_of(here, 256), 256)
            away = pl.ds(pl.multiple_of(half * 2 * WIDTH + here, 256), 256)
            predicted = dot(students[...], weights[:, place(i, 256)], 1, 0)
            for s in range(N):
                target = targets[:, cols] if s == 0 else blocks[s - 1][rows[0], away]
                part = predicted[s * TOK : (s + 1) * TOK] - target.astype(F32)
                errors[rows[s], cols] = part.astype(BF16)

        lax.fori_loop(0, 2, step, None)

    one(1, w_other)
    turned = errors[:, pl.ds(WIDTH, WIDTH)].T

    def step(n, _):
        cols = place(n, BLOCK)
        grads[:, cols] = dot(turned, students[:, cols], 1, 0).astype(BF16)

    lax.fori_loop(0, N, step, None)
    one(0, w_own)


def error_and_other(half, student, blocks, w_own, w_other, teacher):
    n_tok = N * TOK
    return call(
        functools.partial(error_kernel, half),
        (student, *blocks, w_own, w_other, teacher),
        [((n_tok, 2 * WIDTH), BF16), ((WIDTH, DS), BF16)],
        [
            pltpu.VMEM((n_tok, DS), BF16),
            pltpu.VMEM((TOK, 2 * WIDTH), BF16),
            pltpu.SemaphoreType.DMA((6,)),
        ],
        12,
        BIG,
        in_specs=[ANY] + [VMEM] * 5 + [ANY],
        out_specs=[VMEM] * 2,
    )


def own_kernel(order, student, b1, b2, b3, error, there, *rest):
    ins, rest = rest[: len(order) - 1], rest[len(order) - 1 :]
    *outs, students, sems = rest
    y = index("y")
    held = (student, *(block.at[pl.ds(TOK, TOK), :] for block in (b1, b2, b3)))
    spots = [place((y + s) % N, BLOCK) for s in order]
    loads = [
        run(
            [
                (ref.at[:, spot], students.at[k, pl.ds(s * TOK, TOK), :])
                for s, ref in enumerate(held)
            ],
            sems,
            4 * k,
        )
        for k, spot in enumerate(spots)
    ]
    turned = error[:, pl.ds(0, WIDTH)].T
    half = WIDTH // 2
    for k, s in enumerate(order):
        for copy in loads[k]:
            copy.wait()
        total = dot(turned, students[k], 1, 0) + there[:, spots[k]].astype(F32)
        low, high = total[:half], total[half:]
        if s == 1:
            low = low + ins[0][...].astype(F32)
        elif s == 3:
            high = high + ins[1][...].astype(F32)
        if s == 2:
            outs[0][...] = low.astype(BF16)
            outs[1][...] = high.astype(BF16)
        else:
            outs[k][:half] = low.astype(BF16)
            outs[k][half:] = high.astype(BF16)


def own_and_sum(order, students, error, there, ins=(), flops=1):
    n_tok, n = N * TOK, len(order)
    halves = [((WIDTH // 2, BLOCK), BF16)] * 2
    outs = halves if order == (2,) else [((WIDTH, BLOCK), BF16)] * 3
    return call(
        functools.partial(own_kernel, order),
        (*students, error, there, *ins),
        outs,
        [pltpu.VMEM((n, n_tok, BLOCK), BF16), pltpu.SemaphoreType.DMA((4 * n,))],
        10,
        flops,
        in_specs=[ANY] * 4 + [VMEM] * (2 + len(ins)),
        out_specs=[VMEM] * len(outs),
    )


def student_kernel(near, far, wa, wb, wc, wd, o0, o1, o3, low, high):
    errors, weights = (near, far), (wa, wb, wc, wd)

    def step(n, _):
        cols = place(n, BLOCK)
        total = None
        for p in range(4):
            term = dot(errors[p // 2][:, pl.ds(p % 2 * WIDTH, WIDTH)], weights[p][cols, :], 1, 1)
            total = term if total is None else total + term
        for s, out in ((0, o0), (1, o3), (3, o1)):
            out[:, cols] = total[s * TOK : (s + 1) * TOK].astype(BF16)
        low[:, cols] = total[2 * TOK : 2 * TOK + TOK // 2].astype(BF16)
        high[:, cols] = total[2 * TOK + TOK // 2 : 3 * TOK].astype(BF16)

    lax.fori_loop(0, N, step, None)


def student_part(near, far, weights):
    return call(
        student_kernel,
        (near, far, *weights),
        [((TOK, DS), BF16)] * 3 + [((TOK // 2, DS), BF16)] * 2,
        [],
        12,
        BIG,
        in_specs=[VMEM] * 6,
        out_specs=[VMEM] * 5,
    )


def pass_kernel(b1, b3, low, high, o1, o3):
    half = TOK // 2
    o1[:half] = (b1[:half].astype(F32) + low[...].astype(F32)).astype(BF16)
    o1[half:] = b1[half:]
    o3[:half] = b3[:half]
    o3[half:] = (b3[half:].astype(F32) + high[...].astype(F32)).astype(BF16)


def y_kernel(a, b, c, *outs):
    zl = index("zl")
    for s, out in zip((0, 1, 3, 2), outs):
        cols = place((zl + s) % N, ROWS)
        total = a[:, cols].astype(F32) + b[:, cols].astype(F32) + c[:, cols].astype(F32)
        out[...] = total.astype(out.dtype)


def z_kernel(own, p1, p2, p3, out):
    total = own[...] + p1[...].astype(F32) + p2[...].astype(F32) + p3[...].astype(F32)
    out[...] = total.astype(BF16)


def final_kernel(own, p1, p2, p3, far, out):
    total = own[...] + p1[...].astype(F32) + p2[...].astype(F32) + p3[...].astype(F32)
    out[...] = (total + far[...].astype(F32)).T * (1.0 / math.sqrt(TOK * 256))


def student_sum_kernel(own, p1, p3, out):
    total = own[...].astype(F32) + p1[...].astype(F32)
    out[...] = (total + p3[...].astype(F32)).astype(BF16)


def in_vmem(kernel, ins, outs, flops=1):
    return call(kernel, ins, outs, [], 8, flops, in_specs=[VMEM] * len(ins), out_specs=[VMEM] * len(outs))


def over(axis, blocks, *done):
    got = {s: shift(after(b, *done), axis, s) for s, b in zip((1, 3, 2), blocks)}
    return [got[s] for s in (1, 2, 3)]


def body(teacher, student, proj):
    blocks = over("x", split(teacher, student))
    students = (student, *blocks)
    proj_b = shift(proj, "c", 1)
    part = after(shift(cut(proj), "zh", 1), proj_b)

    p1 = shift(part[: BLOCK - REST], "y", 1)
    p3 = shift(part[REST:], "y", 3)
    lower, upper = relay(part, p1, p3)
    lower, upper = shift(lower, "y", 1), shift(upper, "y", 3)
    proj_c = join([part, p1, p3, lower, upper, mark(blocks, SMALL)])
    proj_d = shift(proj_c, "c", 1)

    near, there = error_and_other(0, student, blocks, after(proj, proj_c), proj_b, teacher)
    near_there = shift(there, "c", 1)
    far, there = error_and_other(1, student, blocks, after(proj_c, near), proj_d, teacher)
    far_there = shift(there, "c", 1)

    sent = own_and_sum((2,), students, near, after(near_there, far))
    near_in = [shift(sent[0], "y", 1), shift(sent[1], "y", 3)]
    sent = own_and_sum((2,), students, far, after(far_there, *sent))
    far_in = [shift(sent[0], "y", 1), shift(sent[1], "y", 3)]
    weights = (proj, proj_b, proj_c, after(proj_d, *sent))
    partial = student_part(near, far, weights)
    far_sum = own_and_sum(
        (1, 3, 0), students, far, after(far_there, partial[0], *near_in), far_in
    )
    passed = shift(partial[3], "x", 1), shift(partial[4], "x", 3)
    back = in_vmem(pass_kernel, [*partial[1:3], *passed], [((TOK, DS), BF16)] * 2, BIG)
    back = shift(after(back[0], far_sum[2]), "x", 1), shift(after(back[1], far_sum[2]), "x", 3)
    far_y = [far_sum[2], shift(far_sum[0], "y", 1), shift(far_sum[1], "y", 3)]
    near_sum = own_and_sum(
        (1, 3, 0), students, near, after(near_there, *far_sum), near_in
    )
    sent = [after(b, *far_y[1:]) for b in near_sum[:2]]
    near_y = [near_sum[2], shift(sent[0], "y", 1), shift(sent[1], "y", 3)]

    def over_y(terms, flops):
        outs = [((WIDTH, ROWS), F32)] + [((WIDTH, ROWS), BF16)] * 3
        return in_vmem(y_kernel, terms, outs, flops)

    far_z = over_y(far_y, 1)
    far_terms = [far_z[0]] + over("zl", far_z[1:])
    far_terms = [after(far_terms[0], *back), *far_terms[1:]]
    far_part = in_vmem(z_kernel, far_terms, [((WIDTH, ROWS), BF16)])[0]
    near_z = over_y(near_y, BIG)
    far_part = shift(after(far_part, *near_z), "zh", 1)
    near_terms = [near_z[0]] + over("zl", near_z[1:])
    grad_student = in_vmem(
        student_sum_kernel, [partial[0], *back], [((TOK, DS), BF16)]
    )[0]
    grad_proj = in_vmem(final_kernel, [*near_terms, far_part], [((ROWS, WIDTH), F32)])[0]
    return grad_proj, grad_student


def solution(mesh):
    fine = Mesh(mesh.devices.reshape(4, 4, 4, 2, 2), ALL)
    tokens = P(ALL, None)
    return jax.shard_map(
        body,
        mesh=fine,
        in_specs=(tokens, tokens, P(None, ("x", "zh", "c"))),
        out_specs=(P(("y", "zl"), ("x", "zh", "c")), tokens),
        check_vma=False,
    )
```

time: 155 us -> 141 us (0.910)
  starting transfers between devices: 57.6 us -> 47.9 us
  Pallas kernels: 27.8 us -> 24.7 us
  waiting for transfers between devices: 65.8 us -> 64.2 us
    ppermute x33 -> x31, starting transfers between devices: 57.6 us -> 47.9 us  [shift(): return lax.ppermute(array, axis, [(i, (i + by) % n) for i in range(n)])]
    pallas_call x16 -> x18, Pallas kernels: 27.8 us -> 24.7 us  [call(): pl.pallas_call(kernel, in_specs=in_specs or [ANY] * len(ins), out_specs=o...]
    ppermute x33 -> x31, waiting for transfers between devices: 65.8 us -> 64.2 us  [shift(): return lax.ppermute(array, axis, [(i, (i + by) % n) for i in range(n)])]
  transfers between devices with their start and end apart: 33 -> 31, of which waited for: 13 -> 12; matrix products, arithmetic and copies ran while one was open for 0% -> 0% of each run, Pallas kernels for 17% -> 16%
where the time goes in v3:
time: 141 us; the launch traced here: 140 us
  waiting for transfers between devices  64.2 us (46%)
  starting transfers between devices  47.9 us (34%)
  Pallas kernels  24.7 us (18%)
  local copies, waits for them, and re-layouts  2.4 us (2%)
    ppermute x31, waiting for transfers between devices, shift(): return lax.ppermute(array, axis, [(i, (i + by) % n) for i in range(n)])  64.2 us
    ppermute x31, starting transfers between devices, shift(): return lax.ppermute(array, axis, [(i, (i + by) % n) for i in range(n)])  47.9 us
    pallas_call x18, Pallas kernels, call(): pl.pallas_call(kernel, in_specs=in_specs or [ANY] * len(ins), out_specs=o...  24.7 us
  transfers between devices with their start and end apart: 31, of which 12 were waited for; matrix products, arithmetic and copies ran while one was open for 0% of the time, Pallas kernels for 16%

profile of v3, /device:TPU:32, one launch (start us, length us, event | category | flops | bytes accessed | tf_op | source)
XLA Modules:
  0.0 140.1 jit_solution(10162895932932991200)
XLA Ops:
  0.8 1.7 %copy-done.2 = bf16[2048,512]{1,0:T(8,128)(2,1)S(1)} copy-done((bf16[2048,512]{1,0:T(8,128)(2,1)S(1)}, bf16[2048,512]{1,0:T(8,128)(2,1)}, u32[]{:S(2)}) %copy-start.2) | copy-done | bytes 2097176
  2.5 6.4 %collective-permute-start.4 = (bf16[512,512]{1,0:T(8,128)(2,1)S(1)}, bf16[512,512]{1,0:T(8,128)(2,1)S(1)}, u32[]{:S(2)}, u32[]{:S(2)}) collective-permute-start(bf16[512,512]{1,0:T(8,128)(2,1)S(1)} %shard_map.51), channel_id=1, source_target_pairs={{0,2},{2,0},{1,3},{3,1},{4,6},{6,4},{5,7},{7,5},{8,10},{10,8},{9,1... | collective-permute-start | bytes 1572872 | tf_op jit(solution)/shard_map/ppermute | solution.py:28
  8.9 0.6 shard_map.50
  9.5 1.6 %collective-permute-start = (bf16[256,2048]{1,0:T(8,128)(2,1)S(1)}, bf16[256,2048]{1,0:T(8,128)(2,1)S(1)}, u32[]{:S(2)}, u32[]{:S(2)}) collective-permute-start(bf16[256,2048]{1,0:T(8,128)(2,1)S(1)} %get-tuple-element.50), channel_id=1, source_target_pairs={{0,4},{4,8},{8,12},{12,0},{1,5},{5,9},{9,13},{13,1},{2,6},{6,10},{... | collective-permute-start | bytes 3145736 | tf_op jit(solution)/shard_map/ppermute | solution.py:28
  11.1 2.7 %collective-permute-start.1 = (bf16[256,2048]{1,0:T(8,128)(2,1)S(1)}, bf16[256,2048]{1,0:T(8,128)(2,1)S(1)}, u32[]{:S(2)}, u32[]{:S(2)}) collective-permute-start(bf16[256,2048]{1,0:T(8,128)(2,1)S(1)} %get-tuple-element.51), channel_id=1, source_target_pairs={{0,8},{4,12},{8,0},{12,4},{1,9},{5,13},{9,1},{13,5},{2,10},{6,14},... | collective-permute-start | bytes 3145736 | tf_op jit(solution)/shard_map/ppermute | solution.py:28
  13.8 1.4 %collective-permute-start.2 = (bf16[256,2048]{1,0:T(8,128)(2,1)S(1)}, bf16[256,2048]{1,0:T(8,128)(2,1)S(1)}, u32[]{:S(2)}, u32[]{:S(2)}) collective-permute-start(bf16[256,2048]{1,0:T(8,128)(2,1)S(1)} %get-tuple-element.52), channel_id=1, source_target_pairs={{0,12},{4,0},{8,4},{12,8},{1,13},{5,1},{9,5},{13,9},{2,14},{6,2},{... | collective-permute-start | bytes 3145736 | tf_op jit(solution)/shard_map/ppermute | solution.py:28
  15.2 17.5 %collective-permute-done.4.part.own = bf16[512,512]{1,0:T(8,128)(2,1)S(1)} collective-permute-done((bf16[512,512]{1,0:T(8,128)(2,1)S(1)}, bf16[512,512]{1,0:T(8,128)(2,1)S(1)}, u32[]{:S(2)}, u32[]{:S(2)}) %collective-permute-start.4) | collective-permute-done | bytes 524320 | tf_op jit(solution)/shard_map/ppermute | solution.py:28
  32.8 1.7 %collective-permute-start.5 = (bf16[496,512]{1,0:T(8,128)(2,1)S(1)}, bf16[496,512]{1,0:T(8,128)(2,1)S(1)}, u32[]{:S(2)}, u32[]{:S(2)}) collective-permute-start(bf16[496,512]{1,0:T(8,128)(2,1)S(1)} %get-tuple-element.99), channel_id=1, source_target_pairs={{0,64},{64,128},{128,192},{192,0},{1,65},{65,129},{129,193},{193,1... | collective-permute-start | bytes 1523720 | tf_op jit(solution)/shard_map/ppermute | solution.py:28
  34.5 1.7 %collective-permute-start.6 = (bf16[496,512]{1,0:T(8,128)(2,1)S(1)}, bf16[496,512]{1,0:T(8,128)(2,1)S(1)}, u32[]{:S(2)}, u32[]{:S(2)}) collective-permute-start(bf16[496,512]{1,0:T(8,128)(2,1)S(1)} %get-tuple-element.98), channel_id=1, source_target_pairs={{0,192},{64,0},{128,64},{192,128},{1,193},{65,1},{129,65},{193,129... | collective-permute-start | bytes 1523720 | tf_op jit(solution)/shard_map/ppermute | solution.py:28
  36.2 11.2 %collective-permute-done.5.p1 = bf16[496,512]{1,0:T(8,128)(2,1)S(1)} collective-permute-done((bf16[496,512]{1,0:T(8,128)(2,1)S(1)}, bf16[496,512]{1,0:T(8,128)(2,1)S(1)}, u32[]{:S(2)}, u32[]{:S(2)}) %collective-permute-start.5) | collective-permute-done | bytes 507936 | tf_op jit(solution)/shard_map/ppermute | solution.py:28
  47.5 1.7 %collective-permute-start.7 = (bf16[272,512]{1,0:T(8,128)(2,1)S(1)}, bf16[272,512]{1,0:T(8,128)(2,1)S(1)}, u32[]{:S(2)}, u32[]{:S(2)}) collective-permute-start(bf16[272,512]{1,0:T(8,128)(2,1)S(1)} %get-tuple-element.54), channel_id=1, source_target_pairs={{0,64},{64,128},{128,192},{192,0},{1,65},{65,129},{129,193},{193,1... | collective-permute-start | bytes 835592 | tf_op jit(solution)/shard_map/ppermute | solution.py:28
  49.1 1.7 %collective-permute-start.8 = (bf16[272,512]{1,0:T(8,128)(2,1)S(1)}, bf16[272,512]{1,0:T(8,128)(2,1)S(1)}, u32[]{:S(2)}, u32[]{:S(2)}) collective-permute-start(bf16[272,512]{1,0:T(8,128)(2,1)S(1)} %get-tuple-element.55), channel_id=1, source_target_pairs={{0,192},{64,0},{128,64},{192,128},{1,193},{65,1},{129,65},{193,129... | collective-permute-start | bytes 835592 | tf_op jit(solution)/shard_map/ppermute | solution.py:28
  50.8 8.5 %collective-permute-done.1.refs_1_.b2 = bf16[256,2048]{1,0:T(8,128)(2,1)S(1)} collective-permute-done((bf16[256,2048]{1,0:T(8,128)(2,1)S(1)}, bf16[256,2048]{1,0:T(8,128)(2,1)S(1)}, u32[]{:S(2)}, u32[]{:S(2)}) %collective-permute-start.1) | collective-permute-done | bytes 1048608 | tf_op jit(solution)/shard_map/ppermute | solution.py:28
  59.4 0.9 shard_map.54.w_own.wc
  60.4 0.6 copy-done.3
  60.9 5.1 %shard_map.55 = (bf16[512,1024]{1,0:T(8,128)(2,1)S(1)}, bf16[512,2048]{1,0:T(8,128)(2,1)S(1)}) custom-call(bf16[128,2048]{1,0:T(8,128)(2,1)S(1)} %copy-done, bf16[256,2048]{1,0:T(8,128)(2,1)S(1)} %collective-permute-done.refs_0_.b1, bf16[256,2048]{1,0:T(8,128)(2,1)S(1)} %collective-permute-done.1.refs_1_.b2, ...), custom_call_target="tpu_custom_call" | custom-call | flops 99999997952 | bytes 1 | tf_op jit(solution)/shard_map/pallas_call | solution.py:56
  66.2 5.1 %shard_map.56 = (bf16[512,1024]{1,0:T(8,128)(2,1)S(1)}, bf16[512,2048]{1,0:T(8,128)(2,1)S(1)}) custom-call(bf16[128,2048]{1,0:T(8,128)(2,1)S(1)} %copy-done, bf16[256,2048]{1,0:T(8,128)(2,1)S(1)} %collective-permute-done.refs_0_.b1, bf16[256,2048]{1,0:T(8,128)(2,1)S(1)} %collective-permute-done.1.refs_1_.b2, ...), custom_call_target="tpu_custom_call" | custom-call | flops 99999997952 | bytes 1 | tf_op jit(solution)/shard_map/pallas_call | solution.py:56
  71.3 0.5 collective-permute-start.11
  71.9 0.7 shard_map.57
  72.6 1.8 %collective-permute-start.12 = (bf16[256,512]{1,0:T(8,128)(2,1)S(1)}, bf16[256,512]{1,0:T(8,128)(2,1)S(1)}, u32[]{:S(2)}, u32[]{:S(2)}) collective-permute-start(bf16[256,512]{1,0:T(8,128)(2,1)S(1)} %get-tuple-element.62), channel_id=1, source_target_pairs={{0,64},{64,128},{128,192},{192,0},{1,65},{65,129},{129,193},{193,1... | collective-permute-start | bytes 786440 | tf_op jit(solution)/shard_map/ppermute | solution.py:28
  74.4 1.7 %collective-permute-start.13 = (bf16[256,512]{1,0:T(8,128)(2,1)S(1)}, bf16[256,512]{1,0:T(8,128)(2,1)S(1)}, u32[]{:S(2)}, u32[]{:S(2)}) collective-permute-start(bf16[256,512]{1,0:T(8,128)(2,1)S(1)} %get-tuple-element.63), channel_id=1, source_target_pairs={{0,192},{64,0},{128,64},{192,128},{1,193},{65,1},{129,65},{193,129... | collective-permute-start | bytes 786440 | tf_op jit(solution)/shard_map/ppermute | solution.py:28
  76.1 0.7 shard_map.58
  76.8 1.2 collective-permute-start.14
  78.1 2.1 %collective-permute-start.15 = (bf16[256,512]{1,0:T(8,128)(2,1)S(1)}, bf16[256,512]{1,0:T(8,128)(2,1)S(1)}, u32[]{:S(2)}, u32[]{:S(2)}) collective-permute-start(bf16[256,512]{1,0:T(8,128)(2,1)S(1)} %get-tuple-element.67), channel_id=1, source_target_pairs={{0,192},{64,0},{128,64},{192,128},{1,193},{65,1},{129,65},{193,129... | collective-permute-start | bytes 786440 | tf_op jit(solution)/shard_map/ppermute | solution.py:28
  80.2 5.1 %shard_map.59 = (bf16[128,2048]{1,0:T(8,128)(2,1)S(1)}, bf16[128,2048]{1,0:T(8,128)(2,1)S(1)}, bf16[128,2048]{1,0:T(8,128)(2,1)S(1)}, bf16[64,2048]{1,0:T(8,128)(2,1)S(1)}, bf16[64,2048]{1,0:T(8,128)(2,1)S(1)}) custom-call(bf16[512,1024]{1,0:T(8,128)(2,1)S(1)} %get-tuple-element.57.error.near, bf16[512,1024]{1,0:T(8,128)(2,1)S(1)} %get-tuple-element.59.error.far, ...), custom_call_target="tpu_custom_call" | custom-call | flops 99999997952 | bytes 1 | tf_op jit(solution)/shard_map/pallas_call | solution.py:56
  85.3 1.4 %collective-permute-start.23 = (bf16[64,2048]{1,0:T(8,128)(2,1)S(1)}, bf16[64,2048]{1,0:T(8,128)(2,1)S(1)}, u32[]{:S(2)}, u32[]{:S(2)}) collective-permute-start(bf16[64,2048]{1,0:T(8,128)(2,1)S(1)} %get-tuple-element.86), channel_id=1, source_target_pairs={{0,4},{4,8},{8,12},{12,0},{1,5},{5,9},{9,13},{13,1},{2,6},{6,10},{... | collective-permute-start | bytes 786440 | tf_op jit(solution)/shard_map/ppermute | solution.py:28
  86.7 1.9 %collective-permute-start.24 = (bf16[64,2048]{1,0:T(8,128)(2,1)S(1)}, bf16[64,2048]{1,0:T(8,128)(2,1)S(1)}, u32[]{:S(2)}, u32[]{:S(2)}) collective-permute-start(bf16[64,2048]{1,0:T(8,128)(2,1)S(1)} %get-tuple-element.87), channel_id=1, source_target_pairs={{0,12},{4,0},{8,4},{12,8},{1,13},{5,1},{9,5},{13,9},{2,14},{6,2},{... | collective-permute-start | bytes 786440 | tf_op jit(solution)/shard_map/ppermute | solution.py:28
  88.6 1.9 %shard_map.60 = (bf16[512,512]{1,0:T(8,128)(2,1)S(1)}, bf16[512,512]{1,0:T(8,128)(2,1)S(1)}, bf16[512,512]{1,0:T(8,128)(2,1)S(1)}) custom-call(bf16[128,2048]{1,0:T(8,128)(2,1)S(1)} %copy-done, bf16[256,2048]{1,0:T(8,128)(2,1)S(1)} %collective-permute-done.refs_0_.b1, bf16[256,2048]{1,0:T(8,128)(2,1)S(1)} %collective-permute-done.1.refs_1_.b2, ...), custom_call_target="tpu_custom_call" | custom-call | flops 1 | bytes 1 | tf_op jit(solution)/shard_map/pallas_call | solution.py:56
  90.5 1.0 collective-permute-start.16
  91.6 2.3 %collective-permute-start.17 = (bf16[512,512]{1,0:T(8,128)(2,1)S(1)}, bf16[512,512]{1,0:T(8,128)(2,1)S(1)}, u32[]{:S(2)}, u32[]{:S(2)}) collective-permute-start(bf16[512,512]{1,0:T(8,128)(2,1)S(1)} %get-tuple-element.72), channel_id=1, source_target_pairs={{0,192},{64,0},{128,64},{192,128},{1,193},{65,1},{129,65},{193,129... | collective-permute-start | bytes 1572872 | tf_op jit(solution)/shard_map/ppermute | solution.py:28
  93.8 0.4 collective-permute-done.23.low
  94.4 3.0 %collective-permute-start.26 = (bf16[128,2048]{1,0:T(8,128)(2,1)S(1)}, bf16[128,2048]{1,0:T(8,128)(2,1)S(1)}, u32[]{:S(2)}, u32[]{:S(2)}) collective-permute-start(bf16[128,2048]{1,0:T(8,128)(2,1)S(1)} %get-tuple-element.91), channel_id=1, source_target_pairs={{0,12},{4,0},{8,4},{12,8},{1,13},{5,1},{9,5},{13,9},{2,14},{6,2},{... | collective-permute-start | bytes 1572872 | tf_op jit(solution)/shard_map/ppermute | solution.py:28
  97.5 1.9 %shard_map.61 = (bf16[512,512]{1,0:T(8,128)(2,1)S(1)}, bf16[512,512]{1,0:T(8,128)(2,1)S(1)}, bf16[512,512]{1,0:T(8,128)(2,1)S(1)}) custom-call(bf16[128,2048]{1,0:T(8,128)(2,1)S(1)} %copy-done, bf16[256,2048]{1,0:T(8,128)(2,1)S(1)} %collective-permute-done.refs_0_.b1, bf16[256,2048]{1,0:T(8,128)(2,1)S(1)} %collective-permute-done.1.refs_1_.b2, ...), custom_call_target="tpu_custom_call" | custom-call | flops 1 | bytes 1 | tf_op jit(solution)/shard_map/pallas_call | solution.py:56
  99.4 5.2 %collective-permute-done.16.b = bf16[512,512]{1,0:T(8,128)(2,1)S(1)} collective-permute-done((bf16[512,512]{1,0:T(8,128)(2,1)S(1)}, bf16[512,512]{1,0:T(8,128)(2,1)S(1)}, u32[]{:S(2)}, u32[]{:S(2)}) %collective-permute-start.16) | collective-permute-done | bytes 524320 | tf_op jit(solution)/shard_map/ppermute | solution.py:28
  104.6 3.0 %collective-permute-start.19 = (bf16[512,512]{1,0:T(8,128)(2,1)S(1)}, bf16[512,512]{1,0:T(8,128)(2,1)S(1)}, u32[]{:S(2)}, u32[]{:S(2)}) collective-permute-start(bf16[512,512]{1,0:T(8,128)(2,1)S(1)} %get-tuple-element.79), channel_id=1, source_target_pairs={{0,192},{64,0},{128,64},{192,128},{1,193},{65,1},{129,65},{193,129... | collective-permute-start | bytes 1572872 | tf_op jit(solution)/shard_map/ppermute | solution.py:28
  107.8 1.1 collective-permute-start.27
  108.9 2.4 %collective-permute-start.28 = (bf16[512,128]{1,0:T(8,128)(2,1)S(1)}, bf16[512,128]{1,0:T(8,128)(2,1)S(1)}, u32[]{:S(2)}, u32[]{:S(2)}) collective-permute-start(bf16[512,128]{1,0:T(8,128)(2,1)S(1)} %get-tuple-element.95), channel_id=1, source_target_pairs={{0,32},{16,48},{32,0},{48,16},{1,33},{17,49},{33,1},{49,17},{2,34}... | collective-permute-start | bytes 393224 | tf_op jit(solution)/shard_map/ppermute | solution.py:28
  111.5 5.2 %collective-permute-done.27.p1 = bf16[512,128]{1,0:T(8,128)(2,1)S(1)} collective-permute-done((bf16[512,128]{1,0:T(8,128)(2,1)S(1)}, bf16[512,128]{1,0:T(8,128)(2,1)S(1)}, u32[]{:S(2)}, u32[]{:S(2)}) %collective-permute-start.27) | collective-permute-done | bytes 131104 | tf_op jit(solution)/shard_map/ppermute | solution.py:28
  116.7 1.4 %collective-permute-done.28.p2 = bf16[512,128]{1,0:T(8,128)(2,1)S(1)} collective-permute-done((bf16[512,128]{1,0:T(8,128)(2,1)S(1)}, bf16[512,128]{1,0:T(8,128)(2,1)S(1)}, u32[]{:S(2)}, u32[]{:S(2)}) %collective-permute-start.28) | collective-permute-done | bytes 131104 | tf_op jit(solution)/shard_map/ppermute | solution.py:28
  118.1 2.2 %collective-permute-done.29.p3 = bf16[512,128]{1,0:T(8,128)(2,1)S(1)} collective-permute-done((bf16[512,128]{1,0:T(8,128)(2,1)S(1)}, bf16[512,128]{1,0:T(8,128)(2,1)S(1)}, u32[]{:S(2)}, u32[]{:S(2)}) %collective-permute-start.29) | collective-permute-done | bytes 131104 | tf_op jit(solution)/shard_map/ppermute | solution.py:28
  120.6 2.2 %collective-permute-start.30 = (bf16[512,128]{1,0:T(8,128)(2,1)S(1)}, bf16[512,128]{1,0:T(8,128)(2,1)S(1)}, u32[]{:S(2)}, u32[]{:S(2)}) collective-permute-start(bf16[512,128]{1,0:T(8,128)(2,1)S(1)} %shard_map.65), channel_id=1, source_target_pairs={{0,2},{2,0},{1,3},{3,1},{4,6},{6,4},{5,7},{7,5},{8,10},{10,8},{9,1... | collective-permute-start | bytes 393224 | tf_op jit(solution)/shard_map/ppermute | solution.py:28
  122.8 0.9 collective-permute-start.20
  124.0 1.8 %collective-permute-start.22 = (bf16[512,128]{1,0:T(8,128)(2,1)S(1)}, bf16[512,128]{1,0:T(8,128)(2,1)S(1)}, u32[]{:S(2)}, u32[]{:S(2)}) collective-permute-start(bf16[512,128]{1,0:T(8,128)(2,1)S(1)} %get-tuple-element.83), channel_id=1, source_target_pairs={{0,48},{16,0},{32,16},{48,32},{1,49},{17,1},{33,17},{49,33},{2,50}... | collective-permute-start | bytes 393224 | tf_op jit(solution)/shard_map/ppermute | solution.py:28
  125.8 1.0 shard_map.67
  126.8 7.8 %collective-permute-done.30.far = bf16[512,128]{1,0:T(8,128)(2,1)S(1)} collective-permute-done((bf16[512,128]{1,0:T(8,128)(2,1)S(1)}, bf16[512,128]{1,0:T(8,128)(2,1)S(1)}, u32[]{:S(2)}, u32[]{:S(2)}) %collective-permute-start.30) | collective-permute-done | bytes 131104 | tf_op jit(solution)/shard_map/ppermute | solution.py:28
  135.0 1.4 collective-permute-done.21.p2
  136.3 3.0 %collective-permute-done.22.p3 = bf16[512,128]{1,0:T(8,128)(2,1)S(1)} collective-permute-done((bf16[512,128]{1,0:T(8,128)(2,1)S(1)}, bf16[512,128]{1,0:T(8,128)(2,1)S(1)}, u32[]{:S(2)}, u32[]{:S(2)}) %collective-permute-start.22) | collective-permute-done | bytes 131104 | tf_op jit(solution)/shard_map/ppermute | solution.py:28
  139.3 0.8 shard_map.66
  (41 shorter events, 2.3 us)
Async XLA Ops:
  0.6 8.3 %copy-start.1 = (bf16[128,8192]{1,0:T(8,128)(2,1)S(1)}, bf16[128,8192]{1,0:T(8,128)(2,1)}, u32[]{:S(2)}) copy-start(bf16[128,8192]{1,0:T(8,128)(2,1)} %teacher.5) | copy-start | bytes 6291460
  0.6 8.3 %copy-start = (bf16[128,2048]{1,0:T(8,128)(2,1)S(1)}, bf16[128,2048]{1,0:T(8,128)(2,1)}, u32[]{:S(2)}) copy-start(bf16[128,2048]{1,0:T(8,128)(2,1)} %student.13) | copy-start | bytes 1572868
  0.6 32.1 %collective-permute-start.3 = (bf16[2048,512]{1,0:T(8,128)(2,1)}, bf16[2048,512]{1,0:T(8,128)(2,1)S(1)}, u32[]{:S(2)}, u32[]{:S(2)}) collective-permute-start(bf16[2048,512]{1,0:T(8,128)(2,1)} %wa.1), channel_id=1, source_target_pairs={{0,1},{1,0},{2,3},{3,2},{4,5},{5,4},{6,7},{7,6},{8,9},{9,8},{10,11... | collective-permute-start | bytes 6291464 | tf_op jit(solution)/shard_map/ppermute | solution.py:28
  0.8 1.7 %copy-start.2 = (bf16[2048,512]{1,0:T(8,128)(2,1)S(1)}, bf16[2048,512]{1,0:T(8,128)(2,1)}, u32[]{:S(2)}) copy-start(bf16[2048,512]{1,0:T(8,128)(2,1)} %wa.1) | copy-start | bytes 6291460
  2.5 30.2 %collective-permute-start.4 = (bf16[512,512]{1,0:T(8,128)(2,1)S(1)}, bf16[512,512]{1,0:T(8,128)(2,1)S(1)}, u32[]{:S(2)}, u32[]{:S(2)}) collective-permute-start(bf16[512,512]{1,0:T(8,128)(2,1)S(1)} %shard_map.51), channel_id=1, source_target_pairs={{0,2},{2,0},{1,3},{3,1},{4,6},{6,4},{5,7},{7,5},{8,10},{10,8},{9,1... | collective-permute-start | bytes 1572872 | tf_op jit(solution)/shard_map/ppermute | solution.py:28
  9.5 41.3 %collective-permute-start = (bf16[256,2048]{1,0:T(8,128)(2,1)S(1)}, bf16[256,2048]{1,0:T(8,128)(2,1)S(1)}, u32[]{:S(2)}, u32[]{:S(2)}) collective-permute-start(bf16[256,2048]{1,0:T(8,128)(2,1)S(1)} %get-tuple-element.50), channel_id=1, source_target_pairs={{0,4},{4,8},{8,12},{12,0},{1,5},{5,9},{9,13},{13,1},{2,6},{6,10},{... | collective-permute-start | bytes 3145736 | tf_op jit(solution)/shard_map/ppermute | solution.py:28
  11.1 48.3 %collective-permute-start.1 = (bf16[256,2048]{1,0:T(8,128)(2,1)S(1)}, bf16[256,2048]{1,0:T(8,128)(2,1)S(1)}, u32[]{:S(2)}, u32[]{:S(2)}) collective-permute-start(bf16[256,2048]{1,0:T(8,128)(2,1)S(1)} %get-tuple-element.51), channel_id=1, source_target_pairs={{0,8},{4,12},{8,0},{12,4},{1,9},{5,13},{9,1},{13,5},{2,10},{6,14},... | collective-permute-start | bytes 3145736 | tf_op jit(solution)/shard_map/ppermute | solution.py:28
  13.8 45.5 %collective-permute-start.2 = (bf16[256,2048]{1,0:T(8,128)(2,1)S(1)}, bf16[256,2048]{1,0:T(8,128)(2,1)S(1)}, u32[]{:S(2)}, u32[]{:S(2)}) collective-permute-start(bf16[256,2048]{1,0:T(8,128)(2,1)S(1)} %get-tuple-element.52), channel_id=1, source_target_pairs={{0,12},{4,0},{8,4},{12,8},{1,13},{5,1},{9,5},{13,9},{2,14},{6,2},{... | collective-permute-start | bytes 3145736 | tf_op jit(solution)/shard_map/ppermute | solution.py:28
  32.8 14.5 %collective-permute-start.5 = (bf16[496,512]{1,0:T(8,128)(2,1)S(1)}, bf16[496,512]{1,0:T(8,128)(2,1)S(1)}, u32[]{:S(2)}, u32[]{:S(2)}) collective-permute-start(bf16[496,512]{1,0:T(8,128)(2,1)S(1)} %get-tuple-element.99), channel_id=1, source_target_pairs={{0,64},{64,128},{128,192},{192,0},{1,65},{65,129},{129,193},{193,1... | collective-permute-start | bytes 1523720 | tf_op jit(solution)/shard_map/ppermute | solution.py:28
  34.5 12.9 %collective-permute-start.6 = (bf16[496,512]{1,0:T(8,128)(2,1)S(1)}, bf16[496,512]{1,0:T(8,128)(2,1)S(1)}, u32[]{:S(2)}, u32[]{:S(2)}) collective-permute-start(bf16[496,512]{1,0:T(8,128)(2,1)S(1)} %get-tuple-element.98), channel_id=1, source_target_pairs={{0,192},{64,0},{128,64},{192,128},{1,193},{65,1},{129,65},{193,129... | collective-permute-start | bytes 1523720 | tf_op jit(solution)/shard_map/ppermute | solution.py:28
  47.5 11.9 %collective-permute-start.7 = (bf16[272,512]{1,0:T(8,128)(2,1)S(1)}, bf16[272,512]{1,0:T(8,128)(2,1)S(1)}, u32[]{:S(2)}, u32[]{:S(2)}) collective-permute-start(bf16[272,512]{1,0:T(8,128)(2,1)S(1)} %get-tuple-element.54), channel_id=1, source_target_pairs={{0,64},{64,128},{128,192},{192,0},{1,65},{65,129},{129,193},{193,1... | collective-permute-start | bytes 835592 | tf_op jit(solution)/shard_map/ppermute | solution.py:28
  49.1 10.2 %collective-permute-start.8 = (bf16[272,512]{1,0:T(8,128)(2,1)S(1)}, bf16[272,512]{1,0:T(8,128)(2,1)S(1)}, u32[]{:S(2)}, u32[]{:S(2)}) collective-permute-start(bf16[272,512]{1,0:T(8,128)(2,1)S(1)} %get-tuple-element.55), channel_id=1, source_target_pairs={{0,192},{64,0},{128,64},{192,128},{1,193},{65,1},{129,65},{193,129... | collective-permute-start | bytes 835592 | tf_op jit(solution)/shard_map/ppermute | solution.py:28
  59.4 1.6 %copy-start.3 = (bf16[2048,512]{1,0:T(8,128)(2,1)S(1)}, bf16[2048,512]{1,0:T(8,128)(2,1)}, u32[]{:S(2)}) copy-start(bf16[2048,512]{1,0:T(8,128)(2,1)} %wa.1) | copy-start | bytes 6291460
  60.3 5.9 %collective-permute-start.9 = (bf16[2048,512]{1,0:T(8,128)(2,1)S(1)}, bf16[2048,512]{1,0:T(8,128)(2,1)S(1)}, u32[]{:S(2)}, u32[]{:S(2)}) collective-permute-start(bf16[2048,512]{1,0:T(8,128)(2,1)S(1)} %shard_map.54.w_own.wc), channel_id=1, source_target_pairs={{0,1},{1,0},{2,3},{3,2},{4,5},{5,4},{6,7},{7,6},{8,9},{9,8},{10,11... | collective-permute-start | bytes 6291464 | tf_op jit(solution)/shard_map/ppermute | solution.py:28
  66.1 5.8 %collective-permute-start.10 = (bf16[512,2048]{1,0:T(8,128)(2,1)S(1)}, bf16[512,2048]{1,0:T(8,128)(2,1)S(1)}, u32[]{:S(2)}, u32[]{:S(2)}) collective-permute-start(bf16[512,2048]{1,0:T(8,128)(2,1)S(1)} %get-tuple-element.60), channel_id=1, source_target_pairs={{0,1},{1,0},{2,3},{3,2},{4,5},{5,4},{6,7},{7,6},{8,9},{9,8},{10,11... | collective-permute-start | bytes 6291464 | tf_op jit(solution)/shard_map/ppermute | solution.py:28
  71.3 4.8 %collective-permute-start.11 = (bf16[512,2048]{1,0:T(8,128)(2,1)S(1)}, bf16[512,2048]{1,0:T(8,128)(2,1)S(1)}, u32[]{:S(2)}, u32[]{:S(2)}) collective-permute-start(bf16[512,2048]{1,0:T(8,128)(2,1)S(1)} %get-tuple-element.64), channel_id=1, source_target_pairs={{0,1},{1,0},{2,3},{3,2},{4,5},{5,4},{6,7},{7,6},{8,9},{9,8},{10,11... | collective-permute-start | bytes 6291464 | tf_op jit(solution)/shard_map/ppermute | solution.py:28
  72.6 14.1 %collective-permute-start.12 = (bf16[256,512]{1,0:T(8,128)(2,1)S(1)}, bf16[256,512]{1,0:T(8,128)(2,1)S(1)}, u32[]{:S(2)}, u32[]{:S(2)}) collective-permute-start(bf16[256,512]{1,0:T(8,128)(2,1)S(1)} %get-tuple-element.62), channel_id=1, source_target_pairs={{0,64},{64,128},{128,192},{192,0},{1,65},{65,129},{129,193},{193,1... | collective-permute-start | bytes 786440 | tf_op jit(solution)/shard_map/ppermute | solution.py:28
  74.4 14.2 %collective-permute-start.13 = (bf16[256,512]{1,0:T(8,128)(2,1)S(1)}, bf16[256,512]{1,0:T(8,128)(2,1)S(1)}, u32[]{:S(2)}, u32[]{:S(2)}) collective-permute-start(bf16[256,512]{1,0:T(8,128)(2,1)S(1)} %get-tuple-element.63), channel_id=1, source_target_pairs={{0,192},{64,0},{128,64},{192,128},{1,193},{65,1},{129,65},{193,129... | collective-permute-start | bytes 786440 | tf_op jit(solution)/shard_map/ppermute | solution.py:28
  76.8 11.8 %collective-permute-start.14 = (bf16[256,512]{1,0:T(8,128)(2,1)S(1)}, bf16[256,512]{1,0:T(8,128)(2,1)S(1)}, u32[]{:S(2)}, u32[]{:S(2)}) collective-permute-start(bf16[256,512]{1,0:T(8,128)(2,1)S(1)} %get-tuple-element.66), channel_id=1, source_target_pairs={{0,64},{64,128},{128,192},{192,0},{1,65},{65,129},{129,193},{193,1... | collective-permute-start | bytes 786440 | tf_op jit(solution)/shard_map/ppermute | solution.py:28
  78.1 10.6 %collective-permute-start.15 = (bf16[256,512]{1,0:T(8,128)(2,1)S(1)}, bf16[256,512]{1,0:T(8,128)(2,1)S(1)}, u32[]{:S(2)}, u32[]{:S(2)}) collective-permute-start(bf16[256,512]{1,0:T(8,128)(2,1)S(1)} %get-tuple-element.67), channel_id=1, source_target_pairs={{0,192},{64,0},{128,64},{192,128},{1,193},{65,1},{129,65},{193,129... | collective-permute-start | bytes 786440 | tf_op jit(solution)/shard_map/ppermute | solution.py:28
  85.3 9.0 %collective-permute-start.23 = (bf16[64,2048]{1,0:T(8,128)(2,1)S(1)}, bf16[64,2048]{1,0:T(8,128)(2,1)S(1)}, u32[]{:S(2)}, u32[]{:S(2)}) collective-permute-start(bf16[64,2048]{1,0:T(8,128)(2,1)S(1)} %get-tuple-element.86), channel_id=1, source_target_pairs={{0,4},{4,8},{8,12},{12,0},{1,5},{5,9},{9,13},{13,1},{2,6},{6,10},{... | collective-permute-start | bytes 786440 | tf_op jit(solution)/shard_map/ppermute | solution.py:28
  86.7 7.6 %collective-permute-start.24 = (bf16[64,2048]{1,0:T(8,128)(2,1)S(1)}, bf16[64,2048]{1,0:T(8,128)(2,1)S(1)}, u32[]{:S(2)}, u32[]{:S(2)}) collective-permute-start(bf16[64,2048]{1,0:T(8,128)(2,1)S(1)} %get-tuple-element.87), channel_id=1, source_target_pairs={{0,12},{4,0},{8,4},{12,8},{1,13},{5,1},{9,5},{13,9},{2,14},{6,2},{... | collective-permute-start | bytes 786440 | tf_op jit(solution)/shard_map/ppermute | solution.py:28
  90.5 14.1 %collective-permute-start.16 = (bf16[512,512]{1,0:T(8,128)(2,1)S(1)}, bf16[512,512]{1,0:T(8,128)(2,1)S(1)}, u32[]{:S(2)}, u32[]{:S(2)}) collective-permute-start(bf16[512,512]{1,0:T(8,128)(2,1)S(1)} %get-tuple-element.71), channel_id=1, source_target_pairs={{0,64},{64,128},{128,192},{192,0},{1,65},{65,129},{129,193},{193,1... | collective-permute-start | bytes 1572872 | tf_op jit(solution)/shard_map/ppermute | solution.py:28
  91.6 13.0 %collective-permute-start.17 = (bf16[512,512]{1,0:T(8,128)(2,1)S(1)}, bf16[512,512]{1,0:T(8,128)(2,1)S(1)}, u32[]{:S(2)}, u32[]{:S(2)}) collective-permute-start(bf16[512,512]{1,0:T(8,128)(2,1)S(1)} %get-tuple-element.72), channel_id=1, source_target_pairs={{0,192},{64,0},{128,64},{192,128},{1,193},{65,1},{129,65},{193,129... | collective-permute-start | bytes 1572872 | tf_op jit(solution)/shard_map/ppermute | solution.py:28
  94.4 14.4 %collective-permute-start.26 = (bf16[128,2048]{1,0:T(8,128)(2,1)S(1)}, bf16[128,2048]{1,0:T(8,128)(2,1)S(1)}, u32[]{:S(2)}, u32[]{:S(2)}) collective-permute-start(bf16[128,2048]{1,0:T(8,128)(2,1)S(1)} %get-tuple-element.91), channel_id=1, source_target_pairs={{0,12},{4,0},{8,4},{12,8},{1,13},{5,1},{9,5},{13,9},{2,14},{6,2},{... | collective-permute-start | bytes 1572872 | tf_op jit(solution)/shard_map/ppermute | solution.py:28
  97.5 13.8 %collective-permute-start.25 = (bf16[128,2048]{1,0:T(8,128)(2,1)S(1)}, bf16[128,2048]{1,0:T(8,128)(2,1)S(1)}, u32[]{:S(2)}, u32[]{:S(2)}) collective-permute-start(bf16[128,2048]{1,0:T(8,128)(2,1)S(1)} %get-tuple-element.89), channel_id=1, source_target_pairs={{0,4},{4,8},{8,12},{12,0},{1,5},{5,9},{9,13},{13,1},{2,6},{6,10},{... | collective-permute-start | bytes 1572872 | tf_op jit(solution)/shard_map/ppermute | solution.py:28
  104.6 15.8 %collective-permute-start.19 = (bf16[512,512]{1,0:T(8,128)(2,1)S(1)}, bf16[512,512]{1,0:T(8,128)(2,1)S(1)}, u32[]{:S(2)}, u32[]{:S(2)}) collective-permute-start(bf16[512,512]{1,0:T(8,128)(2,1)S(1)} %get-tuple-element.79), channel_id=1, source_target_pairs={{0,192},{64,0},{128,64},{192,128},{1,193},{65,1},{129,65},{193,129... | collective-permute-start | bytes 1572872 | tf_op jit(solution)/shard_map/ppermute | solution.py:28
  107.5 12.8 %collective-permute-start.18 = (bf16[512,512]{1,0:T(8,128)(2,1)S(1)}, bf16[512,512]{1,0:T(8,128)(2,1)S(1)}, u32[]{:S(2)}, u32[]{:S(2)}) collective-permute-start(bf16[512,512]{1,0:T(8,128)(2,1)S(1)} %get-tuple-element.77), channel_id=1, source_target_pairs={{0,64},{64,128},{128,192},{192,0},{1,65},{65,129},{129,193},{193,1... | collective-permute-start | bytes 1572872 | tf_op jit(solution)/shard_map/ppermute | solution.py:28
  107.8 8.9 %collective-permute-start.27 = (bf16[512,128]{1,0:T(8,128)(2,1)S(1)}, bf16[512,128]{1,0:T(8,128)(2,1)S(1)}, u32[]{:S(2)}, u32[]{:S(2)}) collective-permute-start(bf16[512,128]{1,0:T(8,128)(2,1)S(1)} %get-tuple-element.94), channel_id=1, source_target_pairs={{0,16},{16,32},{32,48},{48,0},{1,17},{17,33},{33,49},{49,1},{2,18}... | collective-permute-start | bytes 393224 | tf_op jit(solution)/shard_map/ppermute | solution.py:28
  108.9 9.2 %collective-permute-start.28 = (bf16[512,128]{1,0:T(8,128)(2,1)S(1)}, bf16[512,128]{1,0:T(8,128)(2,1)S(1)}, u32[]{:S(2)}, u32[]{:S(2)}) collective-permute-start(bf16[512,128]{1,0:T(8,128)(2,1)S(1)} %get-tuple-element.95), channel_id=1, source_target_pairs={{0,32},{16,48},{32,0},{48,16},{1,33},{17,49},{33,1},{49,17},{2,34}... | collective-permute-start | bytes 393224 | tf_op jit(solution)/shard_map/ppermute | solution.py:28
  111.2 9.1 %collective-permute-start.29 = (bf16[512,128]{1,0:T(8,128)(2,1)S(1)}, bf16[512,128]{1,0:T(8,128)(2,1)S(1)}, u32[]{:S(2)}, u32[]{:S(2)}) collective-permute-start(bf16[512,128]{1,0:T(8,128)(2,1)S(1)} %get-tuple-element.96), channel_id=1, source_target_pairs={{0,48},{16,0},{32,16},{48,32},{1,49},{17,1},{33,17},{49,33},{2,50}... | collective-permute-start | bytes 393224 | tf_op jit(solution)/shard_map/ppermute | solution.py:28
  120.6 14.0 %collective-permute-start.30 = (bf16[512,128]{1,0:T(8,128)(2,1)S(1)}, bf16[512,128]{1,0:T(8,128)(2,1)S(1)}, u32[]{:S(2)}, u32[]{:S(2)}) collective-permute-start(bf16[512,128]{1,0:T(8,128)(2,1)S(1)} %shard_map.65), channel_id=1, source_target_pairs={{0,2},{2,0},{1,3},{3,1},{4,6},{6,4},{5,7},{7,5},{8,10},{10,8},{9,1... | collective-permute-start | bytes 393224 | tf_op jit(solution)/shard_map/ppermute | solution.py:28
  122.8 12.2 %collective-permute-start.20 = (bf16[512,128]{1,0:T(8,128)(2,1)S(1)}, bf16[512,128]{1,0:T(8,128)(2,1)S(1)}, u32[]{:S(2)}, u32[]{:S(2)}) collective-permute-start(bf16[512,128]{1,0:T(8,128)(2,1)S(1)} %get-tuple-element.81), channel_id=1, source_target_pairs={{0,16},{16,32},{32,48},{48,0},{1,17},{17,33},{33,49},{49,1},{2,18}... | collective-permute-start | bytes 393224 | tf_op jit(solution)/shard_map/ppermute | solution.py:28
  123.7 12.6 %collective-permute-start.21 = (bf16[512,128]{1,0:T(8,128)(2,1)S(1)}, bf16[512,128]{1,0:T(8,128)(2,1)S(1)}, u32[]{:S(2)}, u32[]{:S(2)}) collective-permute-start(bf16[512,128]{1,0:T(8,128)(2,1)S(1)} %get-tuple-element.82), channel_id=1, source_target_pairs={{0,32},{16,48},{32,0},{48,16},{1,33},{17,49},{33,1},{49,17},{2,34}... | collective-permute-start | bytes 393224 | tf_op jit(solution)/shard_map/ppermute | solution.py:28
  124.0 15.2 %collective-permute-start.22 = (bf16[512,128]{1,0:T(8,128)(2,1)S(1)}, bf16[512,128]{1,0:T(8,128)(2,1)S(1)}, u32[]{:S(2)}, u32[]{:S(2)}) collective-permute-start(bf16[512,128]{1,0:T(8,128)(2,1)S(1)} %get-tuple-element.83), channel_id=1, source_target_pairs={{0,48},{16,0},{32,16},{48,32},{1,49},{17,1},{33,17},{49,33},{2,50}... | collective-permute-start | bytes 393224 | tf_op jit(solution)/shard_map/ppermute | solution.py:28

commit v4 on v3

--- a/solution.py
+++ b/solution.py
@@ -20,12 +20,16 @@
 ROWS = BLOCK // N
 BIG = 10**11
 SMALL = 3 * 10**8
-REST = 16
+MEDIUM = 5 * 10**9
 
 
 def shift(array, axis, by):
     n = lax.axis_size(axis)
     return lax.ppermute(array, axis, [(i, (i + by) % n) for i in range(n)])
+
+
+def swap(array, bit):
+    return lax.ppermute(array, "zl", [(i, i ^ bit) for i in range(N)])
 
 
 def after(value, *done):
@@ -117,55 +121,47 @@
     )
 
 
-def relay_kernel(part, p1, p3, lower, upper, sems):
+def relay_kernel(p1, p3, lower, upper, sems):
     half = BLOCK // 2
+    for copy in run([(p1.at[:half, :], lower), (p3.at[half:, :], upper)], sems):
+        copy.wait()
+
+
+def relay(*ins):
+    return call(
+        relay_kernel,
+        ins,
+        [((BLOCK // 2, WIDTH), BF16)] * 2,
+        [pltpu.SemaphoreType.DMA((2,))],
+        4,
+        out_specs=[VMEM] * 2,
+    )
+
+
+def join_kernel(own, p1, p3, lower, upper, _, out, sems):
+    y = index("y")
+    half = BLOCK // 2
+
+    def rows(s, first, size):
+        return out.at[pl.ds(pl.multiple_of((y + N - s) % N * BLOCK + first, half), size), :]
+
     pairs = [
-        (p1.at[:half, :], lower.at[:half, :]),
-        (part.at[BLOCK - REST :, :], lower.at[half:, :]),
-        (p3.at[half - REST :, :], upper.at[:half, :]),
-        (part.at[:REST, :], upper.at[half:, :]),
+        (own, rows(0, 0, BLOCK)),
+        (p1, rows(1, 0, BLOCK)),
+        (p3, rows(3, 0, BLOCK)),
+        (lower, rows(2, 0, half)),
+        (upper, rows(2, half, half)),
     ]
     for copy in run(pairs, sems):
         copy.wait()
 
 
-def relay(*ins):
-    return call(
-        relay_kernel,
-        ins,
-        [((BLOCK // 2 + REST, WIDTH), BF16)] * 2,
-        [pltpu.SemaphoreType.DMA((4,))],
-        4,
-        out_specs=[VMEM] * 2,
-    )
-
-
-def join_kernel(own, p1, p3, lower, upper, _, out, sems):
-    y = index("y")
-    half = BLOCK // 2
-
-    def rows(s, first, size):
-        return out.at[pl.ds(pl.multiple_of((y + N - s) % N * BLOCK + first, REST), size), :]
-
-    pairs = [
-        (own, rows(0, 0, BLOCK)),
-        (p1, rows(1, 0, BLOCK - REST)),
-        (p3, rows(3, REST, BLOCK - REST)),
-        (lower.at[:half, :], rows(2, 0, half)),
-        (lower.at[half:, :], rows(1, BLOCK - REST, REST)),
-        (upper.at[:half, :], rows(2, half, half)),
-        (upper.at[half:, :], rows(3, 0, REST)),
-    ]
-    for copy in run(pairs, sems):
-        copy.wait()
-
-
 def join(parts):
     return call(
         join_kernel,
         parts,
         [((DS, WIDTH), BF16)],
-        [pltpu.SemaphoreType.DMA((7,))],
+        [pltpu.SemaphoreType.DMA((5,))],
         8,
         out_specs=[VMEM],
     )[0]
@@ -239,8 +235,8 @@
     )
 
 
-def own_kernel(order, student, b1, b2, b3, error, there, *rest):
-    ins, rest = rest[: len(order) - 1], rest[len(order) - 1 :]
+def own_kernel(order, n_in, student, b1, b2, b3, error, there, *rest):
+    ins, rest = rest[:n_in], rest[n_in:]
     *outs, students, sems = rest
     y = index("y")
     held = (student, *(block.at[pl.ds(TOK, TOK), :] for block in (b1, b2, b3)))
@@ -263,9 +259,9 @@
             copy.wait()
         total = dot(turned, students[k], 1, 0) + there[:, spots[k]].astype(F32)
         low, high = total[:half], total[half:]
-        if s == 1:
+        if ins and s == 1:
             low = low + ins[0][...].astype(F32)
-        elif s == 3:
+        elif ins and s == 3:
             high = high + ins[1][...].astype(F32)
         if s == 2:
             outs[0][...] = low.astype(BF16)
@@ -280,7 +276,7 @@
     halves = [((WIDTH // 2, BLOCK), BF16)] * 2
     outs = halves if order == (2,) else [((WIDTH, BLOCK), BF16)] * 3
     return call(
-        functools.partial(own_kernel, order),
+        functools.partial(own_kernel, order, len(ins)),
         (*students, error, there, *ins),
         outs,
         [pltpu.VMEM((n, n_tok, BLOCK), BF16), pltpu.SemaphoreType.DMA((4 * n,))],
@@ -322,29 +318,38 @@
 
 
 def pass_kernel(b1, b3, low, high, o1, o3):
-    half = TOK // 2
+    half = b1.shape[0] // 2
     o1[:half] = (b1[:half].astype(F32) + low[...].astype(F32)).astype(BF16)
     o1[half:] = b1[half:]
     o3[:half] = b3[:half]
     o3[half:] = (b3[half:].astype(F32) + high[...].astype(F32)).astype(BF16)
 
 
-def y_kernel(a, b, c, *outs):
+def y_kernel(a, b, c, own, other, out):
     zl = index("zl")
-    for s, out in zip((0, 1, 3, 2), outs):
-        cols = place((zl + s) % N, ROWS)
-        total = a[:, cols].astype(F32) + b[:, cols].astype(F32) + c[:, cols].astype(F32)
-        out[...] = total.astype(out.dtype)
-
-
-def z_kernel(own, p1, p2, p3, out):
-    total = own[...] + p1[...].astype(F32) + p2[...].astype(F32) + p3[...].astype(F32)
-    out[...] = total.astype(BF16)
-
-
-def final_kernel(own, p1, p2, p3, far, out):
-    total = own[...] + p1[...].astype(F32) + p2[...].astype(F32) + p3[...].astype(F32)
-    out[...] = (total + far[...].astype(F32)).T * (1.0 / math.sqrt(TOK * 256))
+
+    def block(at):
+        cols = place(at, ROWS)
+        return a[:, cols].astype(F32) + b[:, cols].astype(F32) + c[:, cols].astype(F32)
+
+    own[...] = block(zl)
+    other[...] = block(zl ^ 2)
+    out[:, :ROWS] = block(zl ^ 1).astype(BF16)
+    out[:, ROWS:] = block(zl ^ 3).astype(BF16)
+
+
+def pair_kernel(own, other, got, total, out):
+    total[...] = own[...] + got[:, :ROWS].astype(F32)
+    out[...] = (other[...] + got[:, ROWS:].astype(F32)).astype(BF16)
+
+
+def z_kernel(own, got, out):
+    out[...] = (own[...] + got[...].astype(F32)).astype(BF16)
+
+
+def final_kernel(own, got, far, out):
+    total = own[...] + got[...].astype(F32) + far[...].astype(F32)
+    out[...] = total.T * (1.0 / math.sqrt(TOK * 256))
 
 
 def student_sum_kernel(own, p1, p3, out):
@@ -367,9 +372,8 @@
     proj_b = shift(proj, "c", 1)
     part = after(shift(cut(proj), "zh", 1), proj_b)
 
-    p1 = shift(part[: BLOCK - REST], "y", 1)
-    p3 = shift(part[REST:], "y", 3)
-    lower, upper = relay(part, p1, p3)
+    p1, p3 = shift(part, "y", 1), shift(part, "y", 3)
+    lower, upper = relay(p1, p3)
     lower, upper = shift(lower, "y", 1), shift(upper, "y", 3)
     proj_c = join([part, p1, p3, lower, upper, mark(blocks, SMALL)])
     proj_d = shift(proj_c, "c", 1)
@@ -383,32 +387,33 @@
     near_in = [shift(sent[0], "y", 1), shift(sent[1], "y", 3)]
     sent = own_and_sum((2,), students, far, after(far_there, *sent))
     far_in = [shift(sent[0], "y", 1), shift(sent[1], "y", 3)]
-    weights = (proj, proj_b, proj_c, after(proj_d, *sent))
+    far_sum = own_and_sum((1, 3, 0), students, far, after(far_there, *sent))
+    weights = (proj, proj_b, proj_c, after(proj_d, *far_sum))
     partial = student_part(near, far, weights)
-    far_sum = own_and_sum(
-        (1, 3, 0), students, far, after(far_there, partial[0], *near_in), far_in
-    )
+    terms = [*far_sum[:2], after(far_in[0], partial[0], *near_in), far_in[1]]
+    ready = in_vmem(pass_kernel, terms, [((WIDTH, BLOCK), BF16)] * 2)
     passed = shift(partial[3], "x", 1), shift(partial[4], "x", 3)
     back = in_vmem(pass_kernel, [*partial[1:3], *passed], [((TOK, DS), BF16)] * 2, BIG)
-    back = shift(after(back[0], far_sum[2]), "x", 1), shift(after(back[1], far_sum[2]), "x", 3)
-    far_y = [far_sum[2], shift(far_sum[0], "y", 1), shift(far_sum[1], "y", 3)]
+    back = shift(after(back[0], ready[0]), "x", 1), shift(after(back[1], ready[0]), "x", 3)
+    far_y = [far_sum[2], shift(ready[0], "y", 1), shift(ready[1], "y", 3)]
     near_sum = own_and_sum(
-        (1, 3, 0), students, near, after(near_there, *far_sum), near_in
+        (1, 3, 0), students, near, after(near_there, *ready), near_in
     )
     sent = [after(b, *far_y[1:]) for b in near_sum[:2]]
     near_y = [near_sum[2], shift(sent[0], "y", 1), shift(sent[1], "y", 3)]
 
-    def over_y(terms, flops):
-        outs = [((WIDTH, ROWS), F32)] + [((WIDTH, ROWS), BF16)] * 3
-        return in_vmem(y_kernel, terms, outs, flops)
-
-    far_z = over_y(far_y, 1)
-    far_terms = [far_z[0]] + over("zl", far_z[1:])
-    far_terms = [after(far_terms[0], *back), *far_terms[1:]]
-    far_part = in_vmem(z_kernel, far_terms, [((WIDTH, ROWS), BF16)])[0]
-    near_z = over_y(near_y, BIG)
-    far_part = shift(after(far_part, *near_z), "zh", 1)
-    near_terms = [near_z[0]] + over("zl", near_z[1:])
+    def over_y_and_pair(terms, flops):
+        outs = [((WIDTH, ROWS), F32)] * 2 + [((WIDTH, 2 * ROWS), BF16)]
+        own, other, out = in_vmem(y_kernel, terms, outs, flops)
+        outs = [((WIDTH, ROWS), F32), ((WIDTH, ROWS), BF16)]
+        own, out = in_vmem(pair_kernel, [own, other, swap(out, 1)], outs)
+        return [own, swap(out, 2)]
+
+    far_terms = over_y_and_pair(far_y, 1)
+    far_terms = [after(far_terms[0], *back), far_terms[1]]
+    far_part = in_vmem(z_kernel, far_terms, [((WIDTH, ROWS), BF16)], MEDIUM)[0]
+    near_terms = over_y_and_pair(near_y, BIG)
+    far_part = shift(far_part, "zh", 1)
     grad_student = in_vmem(
         student_sum_kernel, [partial[0], *back], [((TOK, DS), BF16)]
     )[0]

time: 141 us -> 139 us (0.986)
  starting transfers between devices: 47.9 us -> 44.8 us
    ppermute x31 -> x25, waiting for transfers between devices: 64.2 us -> 47.8 us  [shift(): return lax.ppermute(array, axis, [(i, (i + by) % n) for i in range(n)])]
    ppermute x0 -> x4, waiting for transfers between devices: none -> 16.3 us  [swap(): return lax.ppermute(array, 'zl', [(i, i ^ bit) for i in range(N)])]
    ppermute x31 -> x25, starting transfers between devices: 47.9 us -> 39.4 us  [shift(): return lax.ppermute(array, axis, [(i, (i + by) % n) for i in range(n)])]
    ppermute x0 -> x4, starting transfers between devices: none -> 5.42 us  [swap(): return lax.ppermute(array, 'zl', [(i, i ^ bit) for i in range(N)])]
    pallas_call x18 -> x21, Pallas kernels: 24.7 us -> 24.1 us  [call(): pl.pallas_call(kernel, in_specs=in_specs or [ANY] * len(ins), out_specs=o...]
  transfers between devices with their start and end apart: 31 -> 29, of which waited for: 12 -> 11; matrix products, arithmetic and copies ran while one was open for 0% -> 0% of each run, Pallas kernels for 16% -> 17%
where the time goes in v4:
time: 139 us; the launch traced here: 137 us
  waiting for transfers between devices  64.1 us (46%)
  starting transfers between devices  44.8 us (32%)
  Pallas kernels  24.1 us (17%)
  local copies, waits for them, and re-layouts  2.98 us (2%)
    ppermute x25, waiting for transfers between devices, shift(): return lax.ppermute(array, axis, [(i, (i + by) % n) for i in range(n)])  47.8 us
    ppermute x25, starting transfers between devices, shift(): return lax.ppermute(array, axis, [(i, (i + by) % n) for i in range(n)])  39.4 us
    pallas_call x21, Pallas kernels, call(): pl.pallas_call(kernel, in_specs=in_specs or [ANY] * len(ins), out_specs=o...  24.1 us
    ppermute x4, waiting for transfers between devices, swap(): return lax.ppermute(array, 'zl', [(i, i ^ bit) for i in range(N)])  16.3 us
    ppermute x4, starting transfers between devices, swap(): return lax.ppermute(array, 'zl', [(i, i ^ bit) for i in range(N)])  5.42 us
    unnamed x8, local copies, waits for them, and re-layouts  2.98 us
  transfers between devices with their start and end apart: 29, of which 11 were waited for; matrix products, arithmetic and copies ran while one was open for 0% of the time, Pallas kernels for 17%

profile of v4, /device:TPU:32, one launch (start us, length us, event | category | flops | bytes accessed | tf_op | source)
XLA Modules:
  0.0 136.8 jit_solution(7326812492841642453)
XLA Ops:
  0.8 1.7 %copy-done.2 = bf16[2048,512]{1,0:T(8,128)(2,1)S(1)} copy-done((bf16[2048,512]{1,0:T(8,128)(2,1)S(1)}, bf16[2048,512]{1,0:T(8,128)(2,1)}, u32[]{:S(2)}) %copy-start.2) | copy-done | bytes 2097176
  2.5 6.4 %collective-permute-start.4 = (bf16[512,512]{1,0:T(8,128)(2,1)S(1)}, bf16[512,512]{1,0:T(8,128)(2,1)S(1)}, u32[]{:S(2)}, u32[]{:S(2)}) collective-permute-start(bf16[512,512]{1,0:T(8,128)(2,1)S(1)} %shard_map.51), channel_id=1, source_target_pairs={{0,2},{2,0},{1,3},{3,1},{4,6},{6,4},{5,7},{7,5},{8,10},{10,8},{9,1... | collective-permute-start | bytes 1572872 | tf_op jit(solution)/shard_map/ppermute | solution.py:28
  8.9 0.6 shard_map.50
  9.5 1.6 %collective-permute-start = (bf16[256,2048]{1,0:T(8,128)(2,1)S(1)}, bf16[256,2048]{1,0:T(8,128)(2,1)S(1)}, u32[]{:S(2)}, u32[]{:S(2)}) collective-permute-start(bf16[256,2048]{1,0:T(8,128)(2,1)S(1)} %get-tuple-element.54), channel_id=1, source_target_pairs={{0,4},{4,8},{8,12},{12,0},{1,5},{5,9},{9,13},{13,1},{2,6},{6,10},{... | collective-permute-start | bytes 3145736 | tf_op jit(solution)/shard_map/ppermute | solution.py:28
  11.1 2.7 %collective-permute-start.1 = (bf16[256,2048]{1,0:T(8,128)(2,1)S(1)}, bf16[256,2048]{1,0:T(8,128)(2,1)S(1)}, u32[]{:S(2)}, u32[]{:S(2)}) collective-permute-start(bf16[256,2048]{1,0:T(8,128)(2,1)S(1)} %get-tuple-element.55), channel_id=1, source_target_pairs={{0,8},{4,12},{8,0},{12,4},{1,9},{5,13},{9,1},{13,5},{2,10},{6,14},... | collective-permute-start | bytes 3145736 | tf_op jit(solution)/shard_map/ppermute | solution.py:28
  13.8 1.4 %collective-permute-start.2 = (bf16[256,2048]{1,0:T(8,128)(2,1)S(1)}, bf16[256,2048]{1,0:T(8,128)(2,1)S(1)}, u32[]{:S(2)}, u32[]{:S(2)}) collective-permute-start(bf16[256,2048]{1,0:T(8,128)(2,1)S(1)} %get-tuple-element.56), channel_id=1, source_target_pairs={{0,12},{4,0},{8,4},{12,8},{1,13},{5,1},{9,5},{13,9},{2,14},{6,2},{... | collective-permute-start | bytes 3145736 | tf_op jit(solution)/shard_map/ppermute | solution.py:28
  15.2 17.5 %collective-permute-done.4.own = bf16[512,512]{1,0:T(8,128)(2,1)S(1)} collective-permute-done((bf16[512,512]{1,0:T(8,128)(2,1)S(1)}, bf16[512,512]{1,0:T(8,128)(2,1)S(1)}, u32[]{:S(2)}, u32[]{:S(2)}) %collective-permute-start.4) | collective-permute-done | bytes 524320 | tf_op jit(solution)/shard_map/ppermute | solution.py:28
  32.8 1.6 %collective-permute-start.5 = (bf16[512,512]{1,0:T(8,128)(2,1)S(1)}, bf16[512,512]{1,0:T(8,128)(2,1)S(1)}, u32[]{:S(2)}, u32[]{:S(2)}) collective-permute-start(bf16[512,512]{1,0:T(8,128)(2,1)S(1)} %collective-permute-done.4.own), channel_id=1, source_target_pairs={{0,64},{64,128},{128,192},{192,0},{1,65},{65,129},{129,193},{193,1... | collective-permute-start | bytes 1572872 | tf_op jit(solution)/shard_map/ppermute | solution.py:28
  34.3 1.7 %collective-permute-start.6 = (bf16[512,512]{1,0:T(8,128)(2,1)S(1)}, bf16[512,512]{1,0:T(8,128)(2,1)S(1)}, u32[]{:S(2)}, u32[]{:S(2)}) collective-permute-start(bf16[512,512]{1,0:T(8,128)(2,1)S(1)} %collective-permute-done.4.own), channel_id=1, source_target_pairs={{0,192},{64,0},{128,64},{192,128},{1,193},{65,1},{129,65},{193,129... | collective-permute-start | bytes 1572872 | tf_op jit(solution)/shard_map/ppermute | solution.py:28
  36.0 11.5 %collective-permute-done.5.p1 = bf16[512,512]{1,0:T(8,128)(2,1)S(1)} collective-permute-done((bf16[512,512]{1,0:T(8,128)(2,1)S(1)}, bf16[512,512]{1,0:T(8,128)(2,1)S(1)}, u32[]{:S(2)}, u32[]{:S(2)}) %collective-permute-start.5) | collective-permute-done | bytes 524320 | tf_op jit(solution)/shard_map/ppermute | solution.py:28
  47.6 1.7 %collective-permute-start.7 = (bf16[256,512]{1,0:T(8,128)(2,1)S(1)}, bf16[256,512]{1,0:T(8,128)(2,1)S(1)}, u32[]{:S(2)}, u32[]{:S(2)}) collective-permute-start(bf16[256,512]{1,0:T(8,128)(2,1)S(1)} %get-tuple-element.58), channel_id=1, source_target_pairs={{0,64},{64,128},{128,192},{192,0},{1,65},{65,129},{129,193},{193,1... | collective-permute-start | bytes 786440 | tf_op jit(solution)/shard_map/ppermute | solution.py:28
  49.3 1.7 %collective-permute-start.8 = (bf16[256,512]{1,0:T(8,128)(2,1)S(1)}, bf16[256,512]{1,0:T(8,128)(2,1)S(1)}, u32[]{:S(2)}, u32[]{:S(2)}) collective-permute-start(bf16[256,512]{1,0:T(8,128)(2,1)S(1)} %get-tuple-element.59), channel_id=1, source_target_pairs={{0,192},{64,0},{128,64},{192,128},{1,193},{65,1},{129,65},{193,129... | collective-permute-start | bytes 786440 | tf_op jit(solution)/shard_map/ppermute | solution.py:28
  50.9 8.4 %collective-permute-done.1.refs_1_.b2 = bf16[256,2048]{1,0:T(8,128)(2,1)S(1)} collective-permute-done((bf16[256,2048]{1,0:T(8,128)(2,1)S(1)}, bf16[256,2048]{1,0:T(8,128)(2,1)S(1)}, u32[]{:S(2)}, u32[]{:S(2)}) %collective-permute-start.1) | collective-permute-done | bytes 1048608 | tf_op jit(solution)/shard_map/ppermute | solution.py:28
  59.4 0.2 shard_map.54.w_own.wc
  59.7 1.2 copy-done.3
  60.9 5.1 %shard_map.55 = (bf16[512,1024]{1,0:T(8,128)(2,1)S(1)}, bf16[512,2048]{1,0:T(8,128)(2,1)S(1)}) custom-call(bf16[128,2048]{1,0:T(8,128)(2,1)S(1)} %copy-done, bf16[256,2048]{1,0:T(8,128)(2,1)S(1)} %collective-permute-done.refs_0_.b1, bf16[256,2048]{1,0:T(8,128)(2,1)S(1)} %collective-permute-done.1.refs_1_.b2, ...), custom_call_target="tpu_custom_call" | custom-call | flops 99999997952 | bytes 1 | tf_op jit(solution)/shard_map/pallas_call | solution.py:60
  66.2 5.1 %shard_map.56 = (bf16[512,1024]{1,0:T(8,128)(2,1)S(1)}, bf16[512,2048]{1,0:T(8,128)(2,1)S(1)}) custom-call(bf16[128,2048]{1,0:T(8,128)(2,1)S(1)} %copy-done, bf16[256,2048]{1,0:T(8,128)(2,1)S(1)} %collective-permute-done.refs_0_.b1, bf16[256,2048]{1,0:T(8,128)(2,1)S(1)} %collective-permute-done.1.refs_1_.b2, ...), custom_call_target="tpu_custom_call" | custom-call | flops 99999997952 | bytes 1 | tf_op jit(solution)/shard_map/pallas_call | solution.py:60
  71.3 0.6 collective-permute-start.11
  71.9 0.7 shard_map.57
  72.6 1.8 %collective-permute-start.12 = (bf16[256,512]{1,0:T(8,128)(2,1)S(1)}, bf16[256,512]{1,0:T(8,128)(2,1)S(1)}, u32[]{:S(2)}, u32[]{:S(2)}) collective-permute-start(bf16[256,512]{1,0:T(8,128)(2,1)S(1)} %get-tuple-element.66), channel_id=1, source_target_pairs={{0,64},{64,128},{128,192},{192,0},{1,65},{65,129},{129,193},{193,1... | collective-permute-start | bytes 786440 | tf_op jit(solution)/shard_map/ppermute | solution.py:28
  74.4 1.7 %collective-permute-start.13 = (bf16[256,512]{1,0:T(8,128)(2,1)S(1)}, bf16[256,512]{1,0:T(8,128)(2,1)S(1)}, u32[]{:S(2)}, u32[]{:S(2)}) collective-permute-start(bf16[256,512]{1,0:T(8,128)(2,1)S(1)} %get-tuple-element.67), channel_id=1, source_target_pairs={{0,192},{64,0},{128,64},{192,128},{1,193},{65,1},{129,65},{193,129... | collective-permute-start | bytes 786440 | tf_op jit(solution)/shard_map/ppermute | solution.py:28
  76.1 0.7 shard_map.58
  76.8 1.2 collective-permute-start.14
  78.1 2.1 %collective-permute-start.15 = (bf16[256,512]{1,0:T(8,128)(2,1)S(1)}, bf16[256,512]{1,0:T(8,128)(2,1)S(1)}, u32[]{:S(2)}, u32[]{:S(2)}) collective-permute-start(bf16[256,512]{1,0:T(8,128)(2,1)S(1)} %get-tuple-element.71), channel_id=1, source_target_pairs={{0,192},{64,0},{128,64},{192,128},{1,193},{65,1},{129,65},{193,129... | collective-permute-start | bytes 786440 | tf_op jit(solution)/shard_map/ppermute | solution.py:28
  80.2 1.9 %shard_map.59 = (bf16[512,512]{1,0:T(8,128)(2,1)S(1)}, bf16[512,512]{1,0:T(8,128)(2,1)S(1)}, bf16[512,512]{1,0:T(8,128)(2,1)S(1)}) custom-call(bf16[128,2048]{1,0:T(8,128)(2,1)S(1)} %copy-done, bf16[256,2048]{1,0:T(8,128)(2,1)S(1)} %collective-permute-done.refs_0_.b1, bf16[256,2048]{1,0:T(8,128)(2,1)S(1)} %collective-permute-done.1.refs_1_.b2, ...), custom_call_target="tpu_custom_call" | custom-call | flops 1 | bytes 1 | tf_op jit(solution)/shard_map/pallas_call | solution.py:60
  82.0 5.1 %shard_map.60 = (bf16[128,2048]{1,0:T(8,128)(2,1)S(1)}, bf16[128,2048]{1,0:T(8,128)(2,1)S(1)}, bf16[128,2048]{1,0:T(8,128)(2,1)S(1)}, bf16[64,2048]{1,0:T(8,128)(2,1)S(1)}, bf16[64,2048]{1,0:T(8,128)(2,1)S(1)}) custom-call(bf16[512,1024]{1,0:T(8,128)(2,1)S(1)} %get-tuple-element.61.error.near, bf16[512,1024]{1,0:T(8,128)(2,1)S(1)} %get-tuple-element.63.error.far, ...), custom_call_target="tpu_custom_call" | custom-call | flops 99999997952 | bytes 1 | tf_op jit(solution)/shard_map/pallas_call | solution.py:60
  87.2 1.4 %collective-permute-start.22 = (bf16[64,2048]{1,0:T(8,128)(2,1)S(1)}, bf16[64,2048]{1,0:T(8,128)(2,1)S(1)}, u32[]{:S(2)}, u32[]{:S(2)}) collective-permute-start(bf16[64,2048]{1,0:T(8,128)(2,1)S(1)} %get-tuple-element.94), channel_id=1, source_target_pairs={{0,4},{4,8},{8,12},{12,0},{1,5},{5,9},{9,13},{13,1},{2,6},{6,10},{... | collective-permute-start | bytes 786440 | tf_op jit(solution)/shard_map/ppermute | solution.py:28
  88.6 1.9 %collective-permute-start.23 = (bf16[64,2048]{1,0:T(8,128)(2,1)S(1)}, bf16[64,2048]{1,0:T(8,128)(2,1)S(1)}, u32[]{:S(2)}, u32[]{:S(2)}) collective-permute-start(bf16[64,2048]{1,0:T(8,128)(2,1)S(1)} %get-tuple-element.95), channel_id=1, source_target_pairs={{0,12},{4,0},{8,4},{12,8},{1,13},{5,1},{9,5},{13,9},{2,14},{6,2},{... | collective-permute-start | bytes 786440 | tf_op jit(solution)/shard_map/ppermute | solution.py:28
  90.7 3.2 %collective-permute-start.17 = (bf16[512,512]{1,0:T(8,128)(2,1)S(1)}, bf16[512,512]{1,0:T(8,128)(2,1)S(1)}, u32[]{:S(2)}, u32[]{:S(2)}) collective-permute-start(bf16[512,512]{1,0:T(8,128)(2,1)S(1)} %get-tuple-element.80), channel_id=1, source_target_pairs={{0,192},{64,0},{128,64},{192,128},{1,193},{65,1},{129,65},{193,129... | collective-permute-start | bytes 1572872 | tf_op jit(solution)/shard_map/ppermute | solution.py:28
  94.0 2.2 %collective-permute-done.22.low = bf16[64,2048]{1,0:T(8,128)(2,1)S(1)} collective-permute-done((bf16[64,2048]{1,0:T(8,128)(2,1)S(1)}, bf16[64,2048]{1,0:T(8,128)(2,1)S(1)}, u32[]{:S(2)}, u32[]{:S(2)}) %collective-permute-start.22) | collective-permute-done | bytes 262176 | tf_op jit(solution)/shard_map/ppermute | solution.py:28
  96.3 3.0 %collective-permute-start.25 = (bf16[128,2048]{1,0:T(8,128)(2,1)S(1)}, bf16[128,2048]{1,0:T(8,128)(2,1)S(1)}, u32[]{:S(2)}, u32[]{:S(2)}) collective-permute-start(bf16[128,2048]{1,0:T(8,128)(2,1)S(1)} %get-tuple-element.99), channel_id=1, source_target_pairs={{0,12},{4,0},{8,4},{12,8},{1,13},{5,1},{9,5},{13,9},{2,14},{6,2},{... | collective-permute-start | bytes 1572872 | tf_op jit(solution)/shard_map/ppermute | solution.py:28
  99.3 1.9 %shard_map.62 = (bf16[512,512]{1,0:T(8,128)(2,1)S(1)}, bf16[512,512]{1,0:T(8,128)(2,1)S(1)}, bf16[512,512]{1,0:T(8,128)(2,1)S(1)}) custom-call(bf16[128,2048]{1,0:T(8,128)(2,1)S(1)} %copy-done, bf16[256,2048]{1,0:T(8,128)(2,1)S(1)} %collective-permute-done.refs_0_.b1, bf16[256,2048]{1,0:T(8,128)(2,1)S(1)} %collective-permute-done.1.refs_1_.b2, ...), custom_call_target="tpu_custom_call" | custom-call | flops 1 | bytes 1 | tf_op jit(solution)/shard_map/pallas_call | solution.py:60
  101.2 3.5 %collective-permute-done.16.b = bf16[512,512]{1,0:T(8,128)(2,1)S(1)} collective-permute-done((bf16[512,512]{1,0:T(8,128)(2,1)S(1)}, bf16[512,512]{1,0:T(8,128)(2,1)S(1)}, u32[]{:S(2)}, u32[]{:S(2)}) %collective-permute-start.16) | collective-permute-done | bytes 524320 | tf_op jit(solution)/shard_map/ppermute | solution.py:28
  104.7 3.0 %collective-permute-start.19 = (bf16[512,512]{1,0:T(8,128)(2,1)S(1)}, bf16[512,512]{1,0:T(8,128)(2,1)S(1)}, u32[]{:S(2)}, u32[]{:S(2)}) collective-permute-start(bf16[512,512]{1,0:T(8,128)(2,1)S(1)} %get-tuple-element.86), channel_id=1, source_target_pairs={{0,192},{64,0},{128,64},{192,128},{1,193},{65,1},{129,65},{193,129... | collective-permute-start | bytes 1572872 | tf_op jit(solution)/shard_map/ppermute | solution.py:28
  107.7 0.2 shard_map.66
  107.9 1.1 collective-permute-start.26
  109.0 5.5 %collective-permute-done.26.got = bf16[512,256]{1,0:T(8,128)(2,1)S(1)} collective-permute-done((bf16[512,256]{1,0:T(8,128)(2,1)S(1)}, bf16[512,256]{1,0:T(8,128)(2,1)S(1)}, u32[]{:S(2)}, u32[]{:S(2)}) %collective-permute-start.26) | collective-permute-done | bytes 262176 | tf_op jit(solution)/shard_map/ppermute | solution.py:32
  114.5 1.4 %collective-permute-start.27 = (bf16[512,128]{1,0:T(8,128)(2,1)S(1)}, bf16[512,128]{1,0:T(8,128)(2,1)S(1)}, u32[]{:S(2)}, u32[]{:S(2)}) collective-permute-start(bf16[512,128]{1,0:T(8,128)(2,1)S(1)} %get-tuple-element.105), channel_id=1, source_target_pairs={{0,32},{16,48},{32,0},{48,16},{1,33},{17,49},{33,1},{49,17},{2,34}... | collective-permute-start | bytes 393224 | tf_op jit(solution)/shard_map/ppermute | solution.py:32
  115.9 0.8 collective-permute-done.19.c
  116.7 3.4 %collective-permute-done.18.b = bf16[512,512]{1,0:T(8,128)(2,1)S(1)} collective-permute-done((bf16[512,512]{1,0:T(8,128)(2,1)S(1)}, bf16[512,512]{1,0:T(8,128)(2,1)S(1)}, u32[]{:S(2)}, u32[]{:S(2)}) %collective-permute-start.18) | collective-permute-done | bytes 524320 | tf_op jit(solution)/shard_map/ppermute | solution.py:28
  120.4 1.1 collective-permute-start.20
  121.5 0.4 collective-permute-start.28
  121.9 7.9 %collective-permute-done.20.got = bf16[512,256]{1,0:T(8,128)(2,1)S(1)} collective-permute-done((bf16[512,256]{1,0:T(8,128)(2,1)S(1)}, bf16[512,256]{1,0:T(8,128)(2,1)S(1)}, u32[]{:S(2)}, u32[]{:S(2)}) %collective-permute-start.20) | collective-permute-done | bytes 262176 | tf_op jit(solution)/shard_map/ppermute | solution.py:32
  129.9 1.8 %collective-permute-start.21 = (bf16[512,128]{1,0:T(8,128)(2,1)S(1)}, bf16[512,128]{1,0:T(8,128)(2,1)S(1)}, u32[]{:S(2)}, u32[]{:S(2)}) collective-permute-start(bf16[512,128]{1,0:T(8,128)(2,1)S(1)} %get-tuple-element.91), channel_id=1, source_target_pairs={{0,32},{16,48},{32,0},{48,16},{1,33},{17,49},{33,1},{49,17},{2,34}... | collective-permute-start | bytes 393224 | tf_op jit(solution)/shard_map/ppermute | solution.py:32
  131.8 1.0 shard_map.70
  132.8 0.4 collective-permute-done.28.far
  133.2 2.8 %collective-permute-done.21.got = bf16[512,128]{1,0:T(8,128)(2,1)S(1)} collective-permute-done((bf16[512,128]{1,0:T(8,128)(2,1)S(1)}, bf16[512,128]{1,0:T(8,128)(2,1)S(1)}, u32[]{:S(2)}, u32[]{:S(2)}) %collective-permute-start.21) | collective-permute-done | bytes 131104 | tf_op jit(solution)/shard_map/ppermute | solution.py:32
  136.0 0.8 shard_map.69
  (39 shorter events, 1.2 us)
Async XLA Ops:
  0.6 8.3 %copy-start.1 = (bf16[128,8192]{1,0:T(8,128)(2,1)S(1)}, bf16[128,8192]{1,0:T(8,128)(2,1)}, u32[]{:S(2)}) copy-start(bf16[128,8192]{1,0:T(8,128)(2,1)} %teacher.5) | copy-start | bytes 6291460
  0.6 8.3 %copy-start = (bf16[128,2048]{1,0:T(8,128)(2,1)S(1)}, bf16[128,2048]{1,0:T(8,128)(2,1)}, u32[]{:S(2)}) copy-start(bf16[128,2048]{1,0:T(8,128)(2,1)} %student.13) | copy-start | bytes 1572868
  0.6 32.1 %collective-permute-start.3 = (bf16[2048,512]{1,0:T(8,128)(2,1)}, bf16[2048,512]{1,0:T(8,128)(2,1)S(1)}, u32[]{:S(2)}, u32[]{:S(2)}) collective-permute-start(bf16[2048,512]{1,0:T(8,128)(2,1)} %wa.1), channel_id=1, source_target_pairs={{0,1},{1,0},{2,3},{3,2},{4,5},{5,4},{6,7},{7,6},{8,9},{9,8},{10,11... | collective-permute-start | bytes 6291464 | tf_op jit(solution)/shard_map/ppermute | solution.py:28
  0.8 1.7 %copy-start.2 = (bf16[2048,512]{1,0:T(8,128)(2,1)S(1)}, bf16[2048,512]{1,0:T(8,128)(2,1)}, u32[]{:S(2)}) copy-start(bf16[2048,512]{1,0:T(8,128)(2,1)} %wa.1) | copy-start | bytes 6291460
  2.5 30.2 %collective-permute-start.4 = (bf16[512,512]{1,0:T(8,128)(2,1)S(1)}, bf16[512,512]{1,0:T(8,128)(2,1)S(1)}, u32[]{:S(2)}, u32[]{:S(2)}) collective-permute-start(bf16[512,512]{1,0:T(8,128)(2,1)S(1)} %shard_map.51), channel_id=1, source_target_pairs={{0,2},{2,0},{1,3},{3,1},{4,6},{6,4},{5,7},{7,5},{8,10},{10,8},{9,1... | collective-permute-start | bytes 1572872 | tf_op jit(solution)/shard_map/ppermute | solution.py:28
  9.5 41.4 %collective-permute-start = (bf16[256,2048]{1,0:T(8,128)(2,1)S(1)}, bf16[256,2048]{1,0:T(8,128)(2,1)S(1)}, u32[]{:S(2)}, u32[]{:S(2)}) collective-permute-start(bf16[256,2048]{1,0:T(8,128)(2,1)S(1)} %get-tuple-element.54), channel_id=1, source_target_pairs={{0,4},{4,8},{8,12},{12,0},{1,5},{5,9},{9,13},{13,1},{2,6},{6,10},{... | collective-permute-start | bytes 3145736 | tf_op jit(solution)/shard_map/ppermute | solution.py:28
  11.1 48.3 %collective-permute-start.1 = (bf16[256,2048]{1,0:T(8,128)(2,1)S(1)}, bf16[256,2048]{1,0:T(8,128)(2,1)S(1)}, u32[]{:S(2)}, u32[]{:S(2)}) collective-permute-start(bf16[256,2048]{1,0:T(8,128)(2,1)S(1)} %get-tuple-element.55), channel_id=1, source_target_pairs={{0,8},{4,12},{8,0},{12,4},{1,9},{5,13},{9,1},{13,5},{2,10},{6,14},... | collective-permute-start | bytes 3145736 | tf_op jit(solution)/shard_map/ppermute | solution.py:28
  13.8 45.5 %collective-permute-start.2 = (bf16[256,2048]{1,0:T(8,128)(2,1)S(1)}, bf16[256,2048]{1,0:T(8,128)(2,1)S(1)}, u32[]{:S(2)}, u32[]{:S(2)}) collective-permute-start(bf16[256,2048]{1,0:T(8,128)(2,1)S(1)} %get-tuple-element.56), channel_id=1, source_target_pairs={{0,12},{4,0},{8,4},{12,8},{1,13},{5,1},{9,5},{13,9},{2,14},{6,2},{... | collective-permute-start | bytes 3145736 | tf_op jit(solution)/shard_map/ppermute | solution.py:28
  32.8 14.8 %collective-permute-start.5 = (bf16[512,512]{1,0:T(8,128)(2,1)S(1)}, bf16[512,512]{1,0:T(8,128)(2,1)S(1)}, u32[]{:S(2)}, u32[]{:S(2)}) collective-permute-start(bf16[512,512]{1,0:T(8,128)(2,1)S(1)} %collective-permute-done.4.own), channel_id=1, source_target_pairs={{0,64},{64,128},{128,192},{192,0},{1,65},{65,129},{129,193},{193,1... | collective-permute-start | bytes 1572872 | tf_op jit(solution)/shard_map/ppermute | solution.py:28
  34.3 13.2 %collective-permute-start.6 = (bf16[512,512]{1,0:T(8,128)(2,1)S(1)}, bf16[512,512]{1,0:T(8,128)(2,1)S(1)}, u32[]{:S(2)}, u32[]{:S(2)}) collective-permute-start(bf16[512,512]{1,0:T(8,128)(2,1)S(1)} %collective-permute-done.4.own), channel_id=1, source_target_pairs={{0,192},{64,0},{128,64},{192,128},{1,193},{65,1},{129,65},{193,129... | collective-permute-start | bytes 1572872 | tf_op jit(solution)/shard_map/ppermute | solution.py:28
  47.6 11.7 %collective-permute-start.7 = (bf16[256,512]{1,0:T(8,128)(2,1)S(1)}, bf16[256,512]{1,0:T(8,128)(2,1)S(1)}, u32[]{:S(2)}, u32[]{:S(2)}) collective-permute-start(bf16[256,512]{1,0:T(8,128)(2,1)S(1)} %get-tuple-element.58), channel_id=1, source_target_pairs={{0,64},{64,128},{128,192},{192,0},{1,65},{65,129},{129,193},{193,1... | collective-permute-start | bytes 786440 | tf_op jit(solution)/shard_map/ppermute | solution.py:28
  49.3 10.1 %collective-permute-start.8 = (bf16[256,512]{1,0:T(8,128)(2,1)S(1)}, bf16[256,512]{1,0:T(8,128)(2,1)S(1)}, u32[]{:S(2)}, u32[]{:S(2)}) collective-permute-start(bf16[256,512]{1,0:T(8,128)(2,1)S(1)} %get-tuple-element.59), channel_id=1, source_target_pairs={{0,192},{64,0},{128,64},{192,128},{1,193},{65,1},{129,65},{193,129... | collective-permute-start | bytes 786440 | tf_op jit(solution)/shard_map/ppermute | solution.py:28
  59.4 1.6 %copy-start.3 = (bf16[2048,512]{1,0:T(8,128)(2,1)S(1)}, bf16[2048,512]{1,0:T(8,128)(2,1)}, u32[]{:S(2)}) copy-start(bf16[2048,512]{1,0:T(8,128)(2,1)} %wa.1) | copy-start | bytes 6291460
  59.6 6.6 %collective-permute-start.9 = (bf16[2048,512]{1,0:T(8,128)(2,1)S(1)}, bf16[2048,512]{1,0:T(8,128)(2,1)S(1)}, u32[]{:S(2)}, u32[]{:S(2)}) collective-permute-start(bf16[2048,512]{1,0:T(8,128)(2,1)S(1)} %shard_map.54.w_own.wc), channel_id=1, source_target_pairs={{0,1},{1,0},{2,3},{3,2},{4,5},{5,4},{6,7},{7,6},{8,9},{9,8},{10,11... | collective-permute-start | bytes 6291464 | tf_op jit(solution)/shard_map/ppermute | solution.py:28
  66.1 5.8 %collective-permute-start.10 = (bf16[512,2048]{1,0:T(8,128)(2,1)S(1)}, bf16[512,2048]{1,0:T(8,128)(2,1)S(1)}, u32[]{:S(2)}, u32[]{:S(2)}) collective-permute-start(bf16[512,2048]{1,0:T(8,128)(2,1)S(1)} %get-tuple-element.64), channel_id=1, source_target_pairs={{0,1},{1,0},{2,3},{3,2},{4,5},{5,4},{6,7},{7,6},{8,9},{9,8},{10,11... | collective-permute-start | bytes 6291464 | tf_op jit(solution)/shard_map/ppermute | solution.py:28
  71.3 4.8 %collective-permute-start.11 = (bf16[512,2048]{1,0:T(8,128)(2,1)S(1)}, bf16[512,2048]{1,0:T(8,128)(2,1)S(1)}, u32[]{:S(2)}, u32[]{:S(2)}) collective-permute-start(bf16[512,2048]{1,0:T(8,128)(2,1)S(1)} %get-tuple-element.68), channel_id=1, source_target_pairs={{0,1},{1,0},{2,3},{3,2},{4,5},{5,4},{6,7},{7,6},{8,9},{9,8},{10,11... | collective-permute-start | bytes 6291464 | tf_op jit(solution)/shard_map/ppermute | solution.py:28
  72.6 16.0 %collective-permute-start.12 = (bf16[256,512]{1,0:T(8,128)(2,1)S(1)}, bf16[256,512]{1,0:T(8,128)(2,1)S(1)}, u32[]{:S(2)}, u32[]{:S(2)}) collective-permute-start(bf16[256,512]{1,0:T(8,128)(2,1)S(1)} %get-tuple-element.66), channel_id=1, source_target_pairs={{0,64},{64,128},{128,192},{192,0},{1,65},{65,129},{129,193},{193,1... | collective-permute-start | bytes 786440 | tf_op jit(solution)/shard_map/ppermute | solution.py:28
  74.4 16.0 %collective-permute-start.13 = (bf16[256,512]{1,0:T(8,128)(2,1)S(1)}, bf16[256,512]{1,0:T(8,128)(2,1)S(1)}, u32[]{:S(2)}, u32[]{:S(2)}) collective-permute-start(bf16[256,512]{1,0:T(8,128)(2,1)S(1)} %get-tuple-element.67), channel_id=1, source_target_pairs={{0,192},{64,0},{128,64},{192,128},{1,193},{65,1},{129,65},{193,129... | collective-permute-start | bytes 786440 | tf_op jit(solution)/shard_map/ppermute | solution.py:28
  76.8 13.6 %collective-permute-start.14 = (bf16[256,512]{1,0:T(8,128)(2,1)S(1)}, bf16[256,512]{1,0:T(8,128)(2,1)S(1)}, u32[]{:S(2)}, u32[]{:S(2)}) collective-permute-start(bf16[256,512]{1,0:T(8,128)(2,1)S(1)} %get-tuple-element.70), channel_id=1, source_target_pairs={{0,64},{64,128},{128,192},{192,0},{1,65},{65,129},{129,193},{193,1... | collective-permute-start | bytes 786440 | tf_op jit(solution)/shard_map/ppermute | solution.py:28
  78.1 12.4 %collective-permute-start.15 = (bf16[256,512]{1,0:T(8,128)(2,1)S(1)}, bf16[256,512]{1,0:T(8,128)(2,1)S(1)}, u32[]{:S(2)}, u32[]{:S(2)}) collective-permute-start(bf16[256,512]{1,0:T(8,128)(2,1)S(1)} %get-tuple-element.71), channel_id=1, source_target_pairs={{0,192},{64,0},{128,64},{192,128},{1,193},{65,1},{129,65},{193,129... | collective-permute-start | bytes 786440 | tf_op jit(solution)/shard_map/ppermute | solution.py:28
  87.2 9.0 %collective-permute-start.22 = (bf16[64,2048]{1,0:T(8,128)(2,1)S(1)}, bf16[64,2048]{1,0:T(8,128)(2,1)S(1)}, u32[]{:S(2)}, u32[]{:S(2)}) collective-permute-start(bf16[64,2048]{1,0:T(8,128)(2,1)S(1)} %get-tuple-element.94), channel_id=1, source_target_pairs={{0,4},{4,8},{8,12},{12,0},{1,5},{5,9},{9,13},{13,1},{2,6},{6,10},{... | collective-permute-start | bytes 786440 | tf_op jit(solution)/shard_map/ppermute | solution.py:28
  88.6 7.6 %collective-permute-start.23 = (bf16[64,2048]{1,0:T(8,128)(2,1)S(1)}, bf16[64,2048]{1,0:T(8,128)(2,1)S(1)}, u32[]{:S(2)}, u32[]{:S(2)}) collective-permute-start(bf16[64,2048]{1,0:T(8,128)(2,1)S(1)} %get-tuple-element.95), channel_id=1, source_target_pairs={{0,12},{4,0},{8,4},{12,8},{1,13},{5,1},{9,5},{13,9},{2,14},{6,2},{... | collective-permute-start | bytes 786440 | tf_op jit(solution)/shard_map/ppermute | solution.py:28
  90.6 14.1 %collective-permute-start.16 = (bf16[512,512]{1,0:T(8,128)(2,1)S(1)}, bf16[512,512]{1,0:T(8,128)(2,1)S(1)}, u32[]{:S(2)}, u32[]{:S(2)}) collective-permute-start(bf16[512,512]{1,0:T(8,128)(2,1)S(1)} %get-tuple-element.79), channel_id=1, source_target_pairs={{0,64},{64,128},{128,192},{192,0},{1,65},{65,129},{129,193},{193,1... | collective-permute-start | bytes 1572872 | tf_op jit(solution)/shard_map/ppermute | solution.py:28
  90.7 14.0 %collective-permute-start.17 = (bf16[512,512]{1,0:T(8,128)(2,1)S(1)}, bf16[512,512]{1,0:T(8,128)(2,1)S(1)}, u32[]{:S(2)}, u32[]{:S(2)}) collective-permute-start(bf16[512,512]{1,0:T(8,128)(2,1)S(1)} %get-tuple-element.80), channel_id=1, source_target_pairs={{0,192},{64,0},{128,64},{192,128},{1,193},{65,1},{129,65},{193,129... | collective-permute-start | bytes 1572872 | tf_op jit(solution)/shard_map/ppermute | solution.py:28
  96.3 19.6 %collective-permute-start.25 = (bf16[128,2048]{1,0:T(8,128)(2,1)S(1)}, bf16[128,2048]{1,0:T(8,128)(2,1)S(1)}, u32[]{:S(2)}, u32[]{:S(2)}) collective-permute-start(bf16[128,2048]{1,0:T(8,128)(2,1)S(1)} %get-tuple-element.99), channel_id=1, source_target_pairs={{0,12},{4,0},{8,4},{12,8},{1,13},{5,1},{9,5},{13,9},{2,14},{6,2},{... | collective-permute-start | bytes 1572872 | tf_op jit(solution)/shard_map/ppermute | solution.py:28
  99.3 16.6 %collective-permute-start.24 = (bf16[128,2048]{1,0:T(8,128)(2,1)S(1)}, bf16[128,2048]{1,0:T(8,128)(2,1)S(1)}, u32[]{:S(2)}, u32[]{:S(2)}) collective-permute-start(bf16[128,2048]{1,0:T(8,128)(2,1)S(1)} %get-tuple-element.97), channel_id=1, source_target_pairs={{0,4},{4,8},{8,12},{12,0},{1,5},{5,9},{9,13},{13,1},{2,6},{6,10},{... | collective-permute-start | bytes 1572872 | tf_op jit(solution)/shard_map/ppermute | solution.py:28
  104.7 12.0 %collective-permute-start.19 = (bf16[512,512]{1,0:T(8,128)(2,1)S(1)}, bf16[512,512]{1,0:T(8,128)(2,1)S(1)}, u32[]{:S(2)}, u32[]{:S(2)}) collective-permute-start(bf16[512,512]{1,0:T(8,128)(2,1)S(1)} %get-tuple-element.86), channel_id=1, source_target_pairs={{0,192},{64,0},{128,64},{192,128},{1,193},{65,1},{129,65},{193,129... | collective-permute-start | bytes 1572872 | tf_op jit(solution)/shard_map/ppermute | solution.py:28
  107.7 12.5 %collective-permute-start.18 = (bf16[512,512]{1,0:T(8,128)(2,1)S(1)}, bf16[512,512]{1,0:T(8,128)(2,1)S(1)}, u32[]{:S(2)}, u32[]{:S(2)}) collective-permute-start(bf16[512,512]{1,0:T(8,128)(2,1)S(1)} %get-tuple-element.84), channel_id=1, source_target_pairs={{0,64},{64,128},{128,192},{192,0},{1,65},{65,129},{129,193},{193,1... | collective-permute-start | bytes 1572872 | tf_op jit(solution)/shard_map/ppermute | solution.py:28
  107.9 6.6 %collective-permute-start.26 = (bf16[512,256]{1,0:T(8,128)(2,1)S(1)}, bf16[512,256]{1,0:T(8,128)(2,1)S(1)}, u32[]{:S(2)}, u32[]{:S(2)}) collective-permute-start(bf16[512,256]{1,0:T(8,128)(2,1)S(1)} %get-tuple-element.102), channel_id=1, source_target_pairs={{0,16},{16,0},{32,48},{48,32},{1,17},{17,1},{33,49},{49,33},{2,18}... | collective-permute-start | bytes 786440 | tf_op jit(solution)/shard_map/ppermute | solution.py:32
  114.5 6.9 %collective-permute-start.27 = (bf16[512,128]{1,0:T(8,128)(2,1)S(1)}, bf16[512,128]{1,0:T(8,128)(2,1)S(1)}, u32[]{:S(2)}, u32[]{:S(2)}) collective-permute-start(bf16[512,128]{1,0:T(8,128)(2,1)S(1)} %get-tuple-element.105), channel_id=1, source_target_pairs={{0,32},{16,48},{32,0},{48,16},{1,33},{17,49},{33,1},{49,17},{2,34}... | collective-permute-start | bytes 393224 | tf_op jit(solution)/shard_map/ppermute | solution.py:32
  120.4 9.5 %collective-permute-start.20 = (bf16[512,256]{1,0:T(8,128)(2,1)S(1)}, bf16[512,256]{1,0:T(8,128)(2,1)S(1)}, u32[]{:S(2)}, u32[]{:S(2)}) collective-permute-start(bf16[512,256]{1,0:T(8,128)(2,1)S(1)} %get-tuple-element.89), channel_id=1, source_target_pairs={{0,16},{16,0},{32,48},{48,32},{1,17},{17,1},{33,49},{49,33},{2,18}... | collective-permute-start | bytes 786440 | tf_op jit(solution)/shard_map/ppermute | solution.py:32
  121.5 11.7 %collective-permute-start.28 = (bf16[512,128]{1,0:T(8,128)(2,1)S(1)}, bf16[512,128]{1,0:T(8,128)(2,1)S(1)}, u32[]{:S(2)}, u32[]{:S(2)}) collective-permute-start(bf16[512,128]{1,0:T(8,128)(2,1)S(1)} %shard_map.68), channel_id=1, source_target_pairs={{0,2},{2,0},{1,3},{3,1},{4,6},{6,4},{5,7},{7,5},{8,10},{10,8},{9,1... | collective-permute-start | bytes 393224 | tf_op jit(solution)/shard_map/ppermute | solution.py:28
  129.9 6.1 %collective-permute-start.21 = (bf16[512,128]{1,0:T(8,128)(2,1)S(1)}, bf16[512,128]{1,0:T(8,128)(2,1)S(1)}, u32[]{:S(2)}, u32[]{:S(2)}) collective-permute-start(bf16[512,128]{1,0:T(8,128)(2,1)S(1)} %get-tuple-element.91), channel_id=1, source_target_pairs={{0,32},{16,48},{32,0},{48,16},{1,33},{17,49},{33,1},{49,17},{2,34}... | collective-permute-start | bytes 393224 | tf_op jit(solution)/shard_map/ppermute | solution.py:32

commit v5 on v4

--- a/solution.py
+++ b/solution.py
@@ -194,17 +194,13 @@
         copy.wait()
 
     def one(j, weights):
-        def step(i, _):
-            here = j * WIDTH + i * 256
-            cols = pl.ds(pl.multiple_of(here, 256), 256)
-            away = pl.ds(pl.multiple_of(half * 2 * WIDTH + here, 256), 256)
-            predicted = dot(students[...], weights[:, place(i, 256)], 1, 0)
-            for s in range(N):
-                target = targets[:, cols] if s == 0 else blocks[s - 1][rows[0], away]
-                part = predicted[s * TOK : (s + 1) * TOK] - target.astype(F32)
-                errors[rows[s], cols] = part.astype(BF16)
-
-        lax.fori_loop(0, 2, step, None)
+        cols = pl.ds(j * WIDTH, WIDTH)
+        away = pl.ds((half * 2 + j) * WIDTH, WIDTH)
+        predicted = dot(students[...], weights[...], 1, 0)
+        for s in range(N):
+            target = targets[:, cols] if s == 0 else blocks[s - 1][rows[0], away]
+            part = predicted[s * TOK : (s + 1) * TOK] - target.astype(F32)
+            errors[rows[s], cols] = part.astype(BF16)
 
     one(1, w_other)
     turned = errors[:, pl.ds(WIDTH, WIDTH)].T

time: 139 us -> 138 us (level)
  transfers between devices with their start and end apart: 29 -> 29, of which waited for: 11 -> 11; matrix products, arithmetic and copies ran while one was open for 0% -> 0% of each run, Pallas kernels for 17% -> 16%
where the time goes in v5:
time: 138 us; the launch traced here: 136 us
  waiting for transfers between devices  63.5 us (46%)
  starting transfers between devices  45.5 us (33%)
  Pallas kernels  23.1 us (17%)
  local copies, waits for them, and re-layouts  2.98 us (2%)
    ppermute x25, waiting for transfers between devices, shift(): return lax.ppermute(array, axis, [(i, (i + by) % n) for i in range(n)])  47.9 us
    ppermute x25, starting transfers between devices, shift(): return lax.ppermute(array, axis, [(i, (i + by) % n) for i in range(n)])  39.4 us
    pallas_call x21, Pallas kernels, call(): pl.pallas_call(kernel, in_specs=in_specs or [ANY] * len(ins), out_specs=o...  23.1 us
    ppermute x4, waiting for transfers between devices, swap(): return lax.ppermute(array, 'zl', [(i, i ^ bit) for i in range(N)])  15.6 us
    ppermute x4, starting transfers between devices, swap(): return lax.ppermute(array, 'zl', [(i, i ^ bit) for i in range(N)])  6.09 us
    unnamed x8, local copies, waits for them, and re-layouts  2.98 us
  transfers between devices with their start and end apart: 29, of which 11 were waited for; matrix products, arithmetic and copies ran while one was open for 0% of the time, Pallas kernels for 16%

profile of v5, /device:TPU:32, one launch (start us, length us, event | category | flops | bytes accessed | tf_op | source)
XLA Modules:
  0.0 135.9 jit_solution(17707414079001993139)
XLA Ops:
  0.8 1.7 %copy-done.2 = bf16[2048,512]{1,0:T(8,128)(2,1)S(1)} copy-done((bf16[2048,512]{1,0:T(8,128)(2,1)S(1)}, bf16[2048,512]{1,0:T(8,128)(2,1)}, u32[]{:S(2)}) %copy-start.2) | copy-done | bytes 2097176
  2.5 6.4 %collective-permute-start.4 = (bf16[512,512]{1,0:T(8,128)(2,1)S(1)}, bf16[512,512]{1,0:T(8,128)(2,1)S(1)}, u32[]{:S(2)}, u32[]{:S(2)}) collective-permute-start(bf16[512,512]{1,0:T(8,128)(2,1)S(1)} %shard_map.51), channel_id=1, source_target_pairs={{0,2},{2,0},{1,3},{3,1},{4,6},{6,4},{5,7},{7,5},{8,10},{10,8},{9,1... | collective-permute-start | bytes 1572872 | tf_op jit(solution)/shard_map/ppermute | solution.py:28
  8.9 0.6 shard_map.50
  9.5 1.6 %collective-permute-start = (bf16[256,2048]{1,0:T(8,128)(2,1)S(1)}, bf16[256,2048]{1,0:T(8,128)(2,1)S(1)}, u32[]{:S(2)}, u32[]{:S(2)}) collective-permute-start(bf16[256,2048]{1,0:T(8,128)(2,1)S(1)} %get-tuple-element.54), channel_id=1, source_target_pairs={{0,4},{4,8},{8,12},{12,0},{1,5},{5,9},{9,13},{13,1},{2,6},{6,10},{... | collective-permute-start | bytes 3145736 | tf_op jit(solution)/shard_map/ppermute | solution.py:28
  11.1 2.7 %collective-permute-start.1 = (bf16[256,2048]{1,0:T(8,128)(2,1)S(1)}, bf16[256,2048]{1,0:T(8,128)(2,1)S(1)}, u32[]{:S(2)}, u32[]{:S(2)}) collective-permute-start(bf16[256,2048]{1,0:T(8,128)(2,1)S(1)} %get-tuple-element.55), channel_id=1, source_target_pairs={{0,8},{4,12},{8,0},{12,4},{1,9},{5,13},{9,1},{13,5},{2,10},{6,14},... | collective-permute-start | bytes 3145736 | tf_op jit(solution)/shard_map/ppermute | solution.py:28
  13.8 1.4 %collective-permute-start.2 = (bf16[256,2048]{1,0:T(8,128)(2,1)S(1)}, bf16[256,2048]{1,0:T(8,128)(2,1)S(1)}, u32[]{:S(2)}, u32[]{:S(2)}) collective-permute-start(bf16[256,2048]{1,0:T(8,128)(2,1)S(1)} %get-tuple-element.56), channel_id=1, source_target_pairs={{0,12},{4,0},{8,4},{12,8},{1,13},{5,1},{9,5},{13,9},{2,14},{6,2},{... | collective-permute-start | bytes 3145736 | tf_op jit(solution)/shard_map/ppermute | solution.py:28
  15.2 17.5 %collective-permute-done.4.own = bf16[512,512]{1,0:T(8,128)(2,1)S(1)} collective-permute-done((bf16[512,512]{1,0:T(8,128)(2,1)S(1)}, bf16[512,512]{1,0:T(8,128)(2,1)S(1)}, u32[]{:S(2)}, u32[]{:S(2)}) %collective-permute-start.4) | collective-permute-done | bytes 524320 | tf_op jit(solution)/shard_map/ppermute | solution.py:28
  32.8 1.6 %collective-permute-start.5 = (bf16[512,512]{1,0:T(8,128)(2,1)S(1)}, bf16[512,512]{1,0:T(8,128)(2,1)S(1)}, u32[]{:S(2)}, u32[]{:S(2)}) collective-permute-start(bf16[512,512]{1,0:T(8,128)(2,1)S(1)} %collective-permute-done.4.own), channel_id=1, source_target_pairs={{0,64},{64,128},{128,192},{192,0},{1,65},{65,129},{129,193},{193,1... | collective-permute-start | bytes 1572872 | tf_op jit(solution)/shard_map/ppermute | solution.py:28
  34.3 1.7 %collective-permute-start.6 = (bf16[512,512]{1,0:T(8,128)(2,1)S(1)}, bf16[512,512]{1,0:T(8,128)(2,1)S(1)}, u32[]{:S(2)}, u32[]{:S(2)}) collective-permute-start(bf16[512,512]{1,0:T(8,128)(2,1)S(1)} %collective-permute-done.4.own), channel_id=1, source_target_pairs={{0,192},{64,0},{128,64},{192,128},{1,193},{65,1},{129,65},{193,129... | collective-permute-start | bytes 1572872 | tf_op jit(solution)/shard_map/ppermute | solution.py:28
  36.0 11.5 %collective-permute-done.5.p1 = bf16[512,512]{1,0:T(8,128)(2,1)S(1)} collective-permute-done((bf16[512,512]{1,0:T(8,128)(2,1)S(1)}, bf16[512,512]{1,0:T(8,128)(2,1)S(1)}, u32[]{:S(2)}, u32[]{:S(2)}) %collective-permute-start.5) | collective-permute-done | bytes 524320 | tf_op jit(solution)/shard_map/ppermute | solution.py:28
  47.6 1.7 %collective-permute-start.7 = (bf16[256,512]{1,0:T(8,128)(2,1)S(1)}, bf16[256,512]{1,0:T(8,128)(2,1)S(1)}, u32[]{:S(2)}, u32[]{:S(2)}) collective-permute-start(bf16[256,512]{1,0:T(8,128)(2,1)S(1)} %get-tuple-element.58), channel_id=1, source_target_pairs={{0,64},{64,128},{128,192},{192,0},{1,65},{65,129},{129,193},{193,1... | collective-permute-start | bytes 786440 | tf_op jit(solution)/shard_map/ppermute | solution.py:28
  49.3 1.7 %collective-permute-start.8 = (bf16[256,512]{1,0:T(8,128)(2,1)S(1)}, bf16[256,512]{1,0:T(8,128)(2,1)S(1)}, u32[]{:S(2)}, u32[]{:S(2)}) collective-permute-start(bf16[256,512]{1,0:T(8,128)(2,1)S(1)} %get-tuple-element.59), channel_id=1, source_target_pairs={{0,192},{64,0},{128,64},{192,128},{1,193},{65,1},{129,65},{193,129... | collective-permute-start | bytes 786440 | tf_op jit(solution)/shard_map/ppermute | solution.py:28
  50.9 8.4 %collective-permute-done.1.refs_1_.b2 = bf16[256,2048]{1,0:T(8,128)(2,1)S(1)} collective-permute-done((bf16[256,2048]{1,0:T(8,128)(2,1)S(1)}, bf16[256,2048]{1,0:T(8,128)(2,1)S(1)}, u32[]{:S(2)}, u32[]{:S(2)}) %collective-permute-start.1) | collective-permute-done | bytes 1048608 | tf_op jit(solution)/shard_map/ppermute | solution.py:28
  59.4 0.2 shard_map.54.w_own.wc
  59.7 1.2 copy-done.3
  60.9 4.6 %shard_map.55 = (bf16[512,1024]{1,0:T(8,128)(2,1)S(1)}, bf16[512,2048]{1,0:T(8,128)(2,1)S(1)}) custom-call(bf16[128,2048]{1,0:T(8,128)(2,1)S(1)} %copy-done, bf16[256,2048]{1,0:T(8,128)(2,1)S(1)} %collective-permute-done.refs_0_.b1, bf16[256,2048]{1,0:T(8,128)(2,1)S(1)} %collective-permute-done.1.refs_1_.b2, ...), custom_call_target="tpu_custom_call" | custom-call | flops 99999997952 | bytes 1 | tf_op jit(solution)/shard_map/pallas_call | solution.py:60
  65.7 4.6 %shard_map.56 = (bf16[512,1024]{1,0:T(8,128)(2,1)S(1)}, bf16[512,2048]{1,0:T(8,128)(2,1)S(1)}) custom-call(bf16[128,2048]{1,0:T(8,128)(2,1)S(1)} %copy-done, bf16[256,2048]{1,0:T(8,128)(2,1)S(1)} %collective-permute-done.refs_0_.b1, bf16[256,2048]{1,0:T(8,128)(2,1)S(1)} %collective-permute-done.1.refs_1_.b2, ...), custom_call_target="tpu_custom_call" | custom-call | flops 99999997952 | bytes 1 | tf_op jit(solution)/shard_map/pallas_call | solution.py:60
  70.3 0.7 collective-permute-start.11
  71.0 0.7 shard_map.57
  71.8 1.7 %collective-permute-start.12 = (bf16[256,512]{1,0:T(8,128)(2,1)S(1)}, bf16[256,512]{1,0:T(8,128)(2,1)S(1)}, u32[]{:S(2)}, u32[]{:S(2)}) collective-permute-start(bf16[256,512]{1,0:T(8,128)(2,1)S(1)} %get-tuple-element.66), channel_id=1, source_target_pairs={{0,64},{64,128},{128,192},{192,0},{1,65},{65,129},{129,193},{193,1... | collective-permute-start | bytes 786440 | tf_op jit(solution)/shard_map/ppermute | solution.py:28
  73.4 1.7 %collective-permute-start.13 = (bf16[256,512]{1,0:T(8,128)(2,1)S(1)}, bf16[256,512]{1,0:T(8,128)(2,1)S(1)}, u32[]{:S(2)}, u32[]{:S(2)}) collective-permute-start(bf16[256,512]{1,0:T(8,128)(2,1)S(1)} %get-tuple-element.67), channel_id=1, source_target_pairs={{0,192},{64,0},{128,64},{192,128},{1,193},{65,1},{129,65},{193,129... | collective-permute-start | bytes 786440 | tf_op jit(solution)/shard_map/ppermute | solution.py:28
  75.1 0.7 shard_map.58
  75.8 1.4 %collective-permute-start.14 = (bf16[256,512]{1,0:T(8,128)(2,1)S(1)}, bf16[256,512]{1,0:T(8,128)(2,1)S(1)}, u32[]{:S(2)}, u32[]{:S(2)}) collective-permute-start(bf16[256,512]{1,0:T(8,128)(2,1)S(1)} %get-tuple-element.70), channel_id=1, source_target_pairs={{0,64},{64,128},{128,192},{192,0},{1,65},{65,129},{129,193},{193,1... | collective-permute-start | bytes 786440 | tf_op jit(solution)/shard_map/ppermute | solution.py:28
  77.2 1.9 %collective-permute-start.15 = (bf16[256,512]{1,0:T(8,128)(2,1)S(1)}, bf16[256,512]{1,0:T(8,128)(2,1)S(1)}, u32[]{:S(2)}, u32[]{:S(2)}) collective-permute-start(bf16[256,512]{1,0:T(8,128)(2,1)S(1)} %get-tuple-element.71), channel_id=1, source_target_pairs={{0,192},{64,0},{128,64},{192,128},{1,193},{65,1},{129,65},{193,129... | collective-permute-start | bytes 786440 | tf_op jit(solution)/shard_map/ppermute | solution.py:28
  79.1 1.9 %shard_map.59 = (bf16[512,512]{1,0:T(8,128)(2,1)S(1)}, bf16[512,512]{1,0:T(8,128)(2,1)S(1)}, bf16[512,512]{1,0:T(8,128)(2,1)S(1)}) custom-call(bf16[128,2048]{1,0:T(8,128)(2,1)S(1)} %copy-done, bf16[256,2048]{1,0:T(8,128)(2,1)S(1)} %collective-permute-done.refs_0_.b1, bf16[256,2048]{1,0:T(8,128)(2,1)S(1)} %collective-permute-done.1.refs_1_.b2, ...), custom_call_target="tpu_custom_call" | custom-call | flops 1 | bytes 1 | tf_op jit(solution)/shard_map/pallas_call | solution.py:60
  81.0 5.1 %shard_map.60 = (bf16[128,2048]{1,0:T(8,128)(2,1)S(1)}, bf16[128,2048]{1,0:T(8,128)(2,1)S(1)}, bf16[128,2048]{1,0:T(8,128)(2,1)S(1)}, bf16[64,2048]{1,0:T(8,128)(2,1)S(1)}, bf16[64,2048]{1,0:T(8,128)(2,1)S(1)}) custom-call(bf16[512,1024]{1,0:T(8,128)(2,1)S(1)} %get-tuple-element.61.error.near, bf16[512,1024]{1,0:T(8,128)(2,1)S(1)} %get-tuple-element.63.error.far, ...), custom_call_target="tpu_custom_call" | custom-call | flops 99999997952 | bytes 1 | tf_op jit(solution)/shard_map/pallas_call | solution.py:60
  86.1 1.4 %collective-permute-start.22 = (bf16[64,2048]{1,0:T(8,128)(2,1)S(1)}, bf16[64,2048]{1,0:T(8,128)(2,1)S(1)}, u32[]{:S(2)}, u32[]{:S(2)}) collective-permute-start(bf16[64,2048]{1,0:T(8,128)(2,1)S(1)} %get-tuple-element.94), channel_id=1, source_target_pairs={{0,4},{4,8},{8,12},{12,0},{1,5},{5,9},{9,13},{13,1},{2,6},{6,10},{... | collective-permute-start | bytes 786440 | tf_op jit(solution)/shard_map/ppermute | solution.py:28
  87.5 1.9 %collective-permute-start.23 = (bf16[64,2048]{1,0:T(8,128)(2,1)S(1)}, bf16[64,2048]{1,0:T(8,128)(2,1)S(1)}, u32[]{:S(2)}, u32[]{:S(2)}) collective-permute-start(bf16[64,2048]{1,0:T(8,128)(2,1)S(1)} %get-tuple-element.95), channel_id=1, source_target_pairs={{0,12},{4,0},{8,4},{12,8},{1,13},{5,1},{9,5},{13,9},{2,14},{6,2},{... | collective-permute-start | bytes 786440 | tf_op jit(solution)/shard_map/ppermute | solution.py:28
  89.8 3.1 %collective-permute-start.17 = (bf16[512,512]{1,0:T(8,128)(2,1)S(1)}, bf16[512,512]{1,0:T(8,128)(2,1)S(1)}, u32[]{:S(2)}, u32[]{:S(2)}) collective-permute-start(bf16[512,512]{1,0:T(8,128)(2,1)S(1)} %get-tuple-element.80), channel_id=1, source_target_pairs={{0,192},{64,0},{128,64},{192,128},{1,193},{65,1},{129,65},{193,129... | collective-permute-start | bytes 1572872 | tf_op jit(solution)/shard_map/ppermute | solution.py:28
  92.9 2.4 %collective-permute-done.22.low = bf16[64,2048]{1,0:T(8,128)(2,1)S(1)} collective-permute-done((bf16[64,2048]{1,0:T(8,128)(2,1)S(1)}, bf16[64,2048]{1,0:T(8,128)(2,1)S(1)}, u32[]{:S(2)}, u32[]{:S(2)}) %collective-permute-start.22) | collective-permute-done | bytes 262176 | tf_op jit(solution)/shard_map/ppermute | solution.py:28
  95.5 3.0 %collective-permute-start.25 = (bf16[128,2048]{1,0:T(8,128)(2,1)S(1)}, bf16[128,2048]{1,0:T(8,128)(2,1)S(1)}, u32[]{:S(2)}, u32[]{:S(2)}) collective-permute-start(bf16[128,2048]{1,0:T(8,128)(2,1)S(1)} %get-tuple-element.99), channel_id=1, source_target_pairs={{0,12},{4,0},{8,4},{12,8},{1,13},{5,1},{9,5},{13,9},{2,14},{6,2},{... | collective-permute-start | bytes 1572872 | tf_op jit(solution)/shard_map/ppermute | solution.py:28
  98.5 1.9 %shard_map.62 = (bf16[512,512]{1,0:T(8,128)(2,1)S(1)}, bf16[512,512]{1,0:T(8,128)(2,1)S(1)}, bf16[512,512]{1,0:T(8,128)(2,1)S(1)}) custom-call(bf16[128,2048]{1,0:T(8,128)(2,1)S(1)} %copy-done, bf16[256,2048]{1,0:T(8,128)(2,1)S(1)} %collective-permute-done.refs_0_.b1, bf16[256,2048]{1,0:T(8,128)(2,1)S(1)} %collective-permute-done.1.refs_1_.b2, ...), custom_call_target="tpu_custom_call" | custom-call | flops 1 | bytes 1 | tf_op jit(solution)/shard_map/pallas_call | solution.py:60
  100.4 3.5 %collective-permute-done.16.b = bf16[512,512]{1,0:T(8,128)(2,1)S(1)} collective-permute-done((bf16[512,512]{1,0:T(8,128)(2,1)S(1)}, bf16[512,512]{1,0:T(8,128)(2,1)S(1)}, u32[]{:S(2)}, u32[]{:S(2)}) %collective-permute-start.16) | collective-permute-done | bytes 524320 | tf_op jit(solution)/shard_map/ppermute | solution.py:28
  103.8 3.0 %collective-permute-start.19 = (bf16[512,512]{1,0:T(8,128)(2,1)S(1)}, bf16[512,512]{1,0:T(8,128)(2,1)S(1)}, u32[]{:S(2)}, u32[]{:S(2)}) collective-permute-start(bf16[512,512]{1,0:T(8,128)(2,1)S(1)} %get-tuple-element.86), channel_id=1, source_target_pairs={{0,192},{64,0},{128,64},{192,128},{1,193},{65,1},{129,65},{193,129... | collective-permute-start | bytes 1572872 | tf_op jit(solution)/shard_map/ppermute | solution.py:28
  106.8 0.2 shard_map.66
  107.0 1.1 collective-permute-start.26
  108.1 5.4 %collective-permute-done.26.got = bf16[512,256]{1,0:T(8,128)(2,1)S(1)} collective-permute-done((bf16[512,256]{1,0:T(8,128)(2,1)S(1)}, bf16[512,256]{1,0:T(8,128)(2,1)S(1)}, u32[]{:S(2)}, u32[]{:S(2)}) %collective-permute-start.26) | collective-permute-done | bytes 262176 | tf_op jit(solution)/shard_map/ppermute | solution.py:32
  113.5 1.5 %collective-permute-start.27 = (bf16[512,128]{1,0:T(8,128)(2,1)S(1)}, bf16[512,128]{1,0:T(8,128)(2,1)S(1)}, u32[]{:S(2)}, u32[]{:S(2)}) collective-permute-start(bf16[512,128]{1,0:T(8,128)(2,1)S(1)} %get-tuple-element.105), channel_id=1, source_target_pairs={{0,32},{16,48},{32,0},{48,16},{1,33},{17,49},{33,1},{49,17},{2,34}... | collective-permute-start | bytes 393224 | tf_op jit(solution)/shard_map/ppermute | solution.py:32
  115.1 1.0 collective-permute-done.19.c
  116.1 3.4 %collective-permute-done.18.b = bf16[512,512]{1,0:T(8,128)(2,1)S(1)} collective-permute-done((bf16[512,512]{1,0:T(8,128)(2,1)S(1)}, bf16[512,512]{1,0:T(8,128)(2,1)S(1)}, u32[]{:S(2)}, u32[]{:S(2)}) %collective-permute-start.18) | collective-permute-done | bytes 524320 | tf_op jit(solution)/shard_map/ppermute | solution.py:28
  119.5 0.2 shard_map.63
  119.7 1.1 collective-permute-start.20
  120.8 0.4 collective-permute-start.28
  121.3 7.7 %collective-permute-done.20.got = bf16[512,256]{1,0:T(8,128)(2,1)S(1)} collective-permute-done((bf16[512,256]{1,0:T(8,128)(2,1)S(1)}, bf16[512,256]{1,0:T(8,128)(2,1)S(1)}, u32[]{:S(2)}, u32[]{:S(2)}) %collective-permute-start.20) | collective-permute-done | bytes 262176 | tf_op jit(solution)/shard_map/ppermute | solution.py:32
  129.0 2.3 %collective-permute-start.21 = (bf16[512,128]{1,0:T(8,128)(2,1)S(1)}, bf16[512,128]{1,0:T(8,128)(2,1)S(1)}, u32[]{:S(2)}, u32[]{:S(2)}) collective-permute-start(bf16[512,128]{1,0:T(8,128)(2,1)S(1)} %get-tuple-element.91), channel_id=1, source_target_pairs={{0,32},{16,48},{32,0},{48,16},{1,33},{17,49},{33,1},{49,17},{2,34}... | collective-permute-start | bytes 393224 | tf_op jit(solution)/shard_map/ppermute | solution.py:32
  131.3 1.0 shard_map.70
  132.5 2.5 %collective-permute-done.21.got = bf16[512,128]{1,0:T(8,128)(2,1)S(1)} collective-permute-done((bf16[512,128]{1,0:T(8,128)(2,1)S(1)}, bf16[512,128]{1,0:T(8,128)(2,1)S(1)}, u32[]{:S(2)}, u32[]{:S(2)}) %collective-permute-start.21) | collective-permute-done | bytes 131104 | tf_op jit(solution)/shard_map/ppermute | solution.py:32
  135.1 0.8 shard_map.69
  (39 shorter events, 1.2 us)
Async XLA Ops:
  0.6 8.3 %copy-start.1 = (bf16[128,8192]{1,0:T(8,128)(2,1)S(1)}, bf16[128,8192]{1,0:T(8,128)(2,1)}, u32[]{:S(2)}) copy-start(bf16[128,8192]{1,0:T(8,128)(2,1)} %teacher.5) | copy-start | bytes 6291460
  0.6 8.3 %copy-start = (bf16[128,2048]{1,0:T(8,128)(2,1)S(1)}, bf16[128,2048]{1,0:T(8,128)(2,1)}, u32[]{:S(2)}) copy-start(bf16[128,2048]{1,0:T(8,128)(2,1)} %student.13) | copy-start | bytes 1572868
  0.6 32.1 %collective-permute-start.3 = (bf16[2048,512]{1,0:T(8,128)(2,1)}, bf16[2048,512]{1,0:T(8,128)(2,1)S(1)}, u32[]{:S(2)}, u32[]{:S(2)}) collective-permute-start(bf16[2048,512]{1,0:T(8,128)(2,1)} %wa.1), channel_id=1, source_target_pairs={{0,1},{1,0},{2,3},{3,2},{4,5},{5,4},{6,7},{7,6},{8,9},{9,8},{10,11... | collective-permute-start | bytes 6291464 | tf_op jit(solution)/shard_map/ppermute | solution.py:28
  0.8 1.7 %copy-start.2 = (bf16[2048,512]{1,0:T(8,128)(2,1)S(1)}, bf16[2048,512]{1,0:T(8,128)(2,1)}, u32[]{:S(2)}) copy-start(bf16[2048,512]{1,0:T(8,128)(2,1)} %wa.1) | copy-start | bytes 6291460
  2.5 30.2 %collective-permute-start.4 = (bf16[512,512]{1,0:T(8,128)(2,1)S(1)}, bf16[512,512]{1,0:T(8,128)(2,1)S(1)}, u32[]{:S(2)}, u32[]{:S(2)}) collective-permute-start(bf16[512,512]{1,0:T(8,128)(2,1)S(1)} %shard_map.51), channel_id=1, source_target_pairs={{0,2},{2,0},{1,3},{3,1},{4,6},{6,4},{5,7},{7,5},{8,10},{10,8},{9,1... | collective-permute-start | bytes 1572872 | tf_op jit(solution)/shard_map/ppermute | solution.py:28
  9.5 41.4 %collective-permute-start = (bf16[256,2048]{1,0:T(8,128)(2,1)S(1)}, bf16[256,2048]{1,0:T(8,128)(2,1)S(1)}, u32[]{:S(2)}, u32[]{:S(2)}) collective-permute-start(bf16[256,2048]{1,0:T(8,128)(2,1)S(1)} %get-tuple-element.54), channel_id=1, source_target_pairs={{0,4},{4,8},{8,12},{12,0},{1,5},{5,9},{9,13},{13,1},{2,6},{6,10},{... | collective-permute-start | bytes 3145736 | tf_op jit(solution)/shard_map/ppermute | solution.py:28
  11.1 48.3 %collective-permute-start.1 = (bf16[256,2048]{1,0:T(8,128)(2,1)S(1)}, bf16[256,2048]{1,0:T(8,128)(2,1)S(1)}, u32[]{:S(2)}, u32[]{:S(2)}) collective-permute-start(bf16[256,2048]{1,0:T(8,128)(2,1)S(1)} %get-tuple-element.55), channel_id=1, source_target_pairs={{0,8},{4,12},{8,0},{12,4},{1,9},{5,13},{9,1},{13,5},{2,10},{6,14},... | collective-permute-start | bytes 3145736 | tf_op jit(solution)/shard_map/ppermute | solution.py:28
  13.8 45.5 %collective-permute-start.2 = (bf16[256,2048]{1,0:T(8,128)(2,1)S(1)}, bf16[256,2048]{1,0:T(8,128)(2,1)S(1)}, u32[]{:S(2)}, u32[]{:S(2)}) collective-permute-start(bf16[256,2048]{1,0:T(8,128)(2,1)S(1)} %get-tuple-element.56), channel_id=1, source_target_pairs={{0,12},{4,0},{8,4},{12,8},{1,13},{5,1},{9,5},{13,9},{2,14},{6,2},{... | collective-permute-start | bytes 3145736 | tf_op jit(solution)/shard_map/ppermute | solution.py:28
  32.8 14.8 %collective-permute-start.5 = (bf16[512,512]{1,0:T(8,128)(2,1)S(1)}, bf16[512,512]{1,0:T(8,128)(2,1)S(1)}, u32[]{:S(2)}, u32[]{:S(2)}) collective-permute-start(bf16[512,512]{1,0:T(8,128)(2,1)S(1)} %collective-permute-done.4.own), channel_id=1, source_target_pairs={{0,64},{64,128},{128,192},{192,0},{1,65},{65,129},{129,193},{193,1... | collective-permute-start | bytes 1572872 | tf_op jit(solution)/shard_map/ppermute | solution.py:28
  34.3 13.2 %collective-permute-start.6 = (bf16[512,512]{1,0:T(8,128)(2,1)S(1)}, bf16[512,512]{1,0:T(8,128)(2,1)S(1)}, u32[]{:S(2)}, u32[]{:S(2)}) collective-permute-start(bf16[512,512]{1,0:T(8,128)(2,1)S(1)} %collective-permute-done.4.own), channel_id=1, source_target_pairs={{0,192},{64,0},{128,64},{192,128},{1,193},{65,1},{129,65},{193,129... | collective-permute-start | bytes 1572872 | tf_op jit(solution)/shard_map/ppermute | solution.py:28
  47.6 11.7 %collective-permute-start.7 = (bf16[256,512]{1,0:T(8,128)(2,1)S(1)}, bf16[256,512]{1,0:T(8,128)(2,1)S(1)}, u32[]{:S(2)}, u32[]{:S(2)}) collective-permute-start(bf16[256,512]{1,0:T(8,128)(2,1)S(1)} %get-tuple-element.58), channel_id=1, source_target_pairs={{0,64},{64,128},{128,192},{192,0},{1,65},{65,129},{129,193},{193,1... | collective-permute-start | bytes 786440 | tf_op jit(solution)/shard_map/ppermute | solution.py:28
  49.3 10.1 %collective-permute-start.8 = (bf16[256,512]{1,0:T(8,128)(2,1)S(1)}, bf16[256,512]{1,0:T(8,128)(2,1)S(1)}, u32[]{:S(2)}, u32[]{:S(2)}) collective-permute-start(bf16[256,512]{1,0:T(8,128)(2,1)S(1)} %get-tuple-element.59), channel_id=1, source_target_pairs={{0,192},{64,0},{128,64},{192,128},{1,193},{65,1},{129,65},{193,129... | collective-permute-start | bytes 786440 | tf_op jit(solution)/shard_map/ppermute | solution.py:28
  59.4 1.6 %copy-start.3 = (bf16[2048,512]{1,0:T(8,128)(2,1)S(1)}, bf16[2048,512]{1,0:T(8,128)(2,1)}, u32[]{:S(2)}) copy-start(bf16[2048,512]{1,0:T(8,128)(2,1)} %wa.1) | copy-start | bytes 6291460
  59.6 6.0 %collective-permute-start.9 = (bf16[2048,512]{1,0:T(8,128)(2,1)S(1)}, bf16[2048,512]{1,0:T(8,128)(2,1)S(1)}, u32[]{:S(2)}, u32[]{:S(2)}) collective-permute-start(bf16[2048,512]{1,0:T(8,128)(2,1)S(1)} %shard_map.54.w_own.wc), channel_id=1, source_target_pairs={{0,1},{1,0},{2,3},{3,2},{4,5},{5,4},{6,7},{7,6},{8,9},{9,8},{10,11... | collective-permute-start | bytes 6291464 | tf_op jit(solution)/shard_map/ppermute | solution.py:28
  65.6 5.5 %collective-permute-start.10 = (bf16[512,2048]{1,0:T(8,128)(2,1)S(1)}, bf16[512,2048]{1,0:T(8,128)(2,1)S(1)}, u32[]{:S(2)}, u32[]{:S(2)}) collective-permute-start(bf16[512,2048]{1,0:T(8,128)(2,1)S(1)} %get-tuple-element.64), channel_id=1, source_target_pairs={{0,1},{1,0},{2,3},{3,2},{4,5},{5,4},{6,7},{7,6},{8,9},{9,8},{10,11... | collective-permute-start | bytes 6291464 | tf_op jit(solution)/shard_map/ppermute | solution.py:28
  70.3 4.8 %collective-permute-start.11 = (bf16[512,2048]{1,0:T(8,128)(2,1)S(1)}, bf16[512,2048]{1,0:T(8,128)(2,1)S(1)}, u32[]{:S(2)}, u32[]{:S(2)}) collective-permute-start(bf16[512,2048]{1,0:T(8,128)(2,1)S(1)} %get-tuple-element.68), channel_id=1, source_target_pairs={{0,1},{1,0},{2,3},{3,2},{4,5},{5,4},{6,7},{7,6},{8,9},{9,8},{10,11... | collective-permute-start | bytes 6291464 | tf_op jit(solution)/shard_map/ppermute | solution.py:28
  71.8 15.8 %collective-permute-start.12 = (bf16[256,512]{1,0:T(8,128)(2,1)S(1)}, bf16[256,512]{1,0:T(8,128)(2,1)S(1)}, u32[]{:S(2)}, u32[]{:S(2)}) collective-permute-start(bf16[256,512]{1,0:T(8,128)(2,1)S(1)} %get-tuple-element.66), channel_id=1, source_target_pairs={{0,64},{64,128},{128,192},{192,0},{1,65},{65,129},{129,193},{193,1... | collective-permute-start | bytes 786440 | tf_op jit(solution)/shard_map/ppermute | solution.py:28
  73.4 16.0 %collective-permute-start.13 = (bf16[256,512]{1,0:T(8,128)(2,1)S(1)}, bf16[256,512]{1,0:T(8,128)(2,1)S(1)}, u32[]{:S(2)}, u32[]{:S(2)}) collective-permute-start(bf16[256,512]{1,0:T(8,128)(2,1)S(1)} %get-tuple-element.67), channel_id=1, source_target_pairs={{0,192},{64,0},{128,64},{192,128},{1,193},{65,1},{129,65},{193,129... | collective-permute-start | bytes 786440 | tf_op jit(solution)/shard_map/ppermute | solution.py:28
  75.8 13.6 %collective-permute-start.14 = (bf16[256,512]{1,0:T(8,128)(2,1)S(1)}, bf16[256,512]{1,0:T(8,128)(2,1)S(1)}, u32[]{:S(2)}, u32[]{:S(2)}) collective-permute-start(bf16[256,512]{1,0:T(8,128)(2,1)S(1)} %get-tuple-element.70), channel_id=1, source_target_pairs={{0,64},{64,128},{128,192},{192,0},{1,65},{65,129},{129,193},{193,1... | collective-permute-start | bytes 786440 | tf_op jit(solution)/shard_map/ppermute | solution.py:28
  77.2 12.2 %collective-permute-start.15 = (bf16[256,512]{1,0:T(8,128)(2,1)S(1)}, bf16[256,512]{1,0:T(8,128)(2,1)S(1)}, u32[]{:S(2)}, u32[]{:S(2)}) collective-permute-start(bf16[256,512]{1,0:T(8,128)(2,1)S(1)} %get-tuple-element.71), channel_id=1, source_target_pairs={{0,192},{64,0},{128,64},{192,128},{1,193},{65,1},{129,65},{193,129... | collective-permute-start | bytes 786440 | tf_op jit(solution)/shard_map/ppermute | solution.py:28
  86.1 9.2 %collective-permute-start.22 = (bf16[64,2048]{1,0:T(8,128)(2,1)S(1)}, bf16[64,2048]{1,0:T(8,128)(2,1)S(1)}, u32[]{:S(2)}, u32[]{:S(2)}) collective-permute-start(bf16[64,2048]{1,0:T(8,128)(2,1)S(1)} %get-tuple-element.94), channel_id=1, source_target_pairs={{0,4},{4,8},{8,12},{12,0},{1,5},{5,9},{9,13},{13,1},{2,6},{6,10},{... | collective-permute-start | bytes 786440 | tf_op jit(solution)/shard_map/ppermute | solution.py:28
  87.5 7.8 %collective-permute-start.23 = (bf16[64,2048]{1,0:T(8,128)(2,1)S(1)}, bf16[64,2048]{1,0:T(8,128)(2,1)S(1)}, u32[]{:S(2)}, u32[]{:S(2)}) collective-permute-start(bf16[64,2048]{1,0:T(8,128)(2,1)S(1)} %get-tuple-element.95), channel_id=1, source_target_pairs={{0,12},{4,0},{8,4},{12,8},{1,13},{5,1},{9,5},{13,9},{2,14},{6,2},{... | collective-permute-start | bytes 786440 | tf_op jit(solution)/shard_map/ppermute | solution.py:28
  89.6 14.2 %collective-permute-start.16 = (bf16[512,512]{1,0:T(8,128)(2,1)S(1)}, bf16[512,512]{1,0:T(8,128)(2,1)S(1)}, u32[]{:S(2)}, u32[]{:S(2)}) collective-permute-start(bf16[512,512]{1,0:T(8,128)(2,1)S(1)} %get-tuple-element.79), channel_id=1, source_target_pairs={{0,64},{64,128},{128,192},{192,0},{1,65},{65,129},{129,193},{193,1... | collective-permute-start | bytes 1572872 | tf_op jit(solution)/shard_map/ppermute | solution.py:28
  89.8 14.1 %collective-permute-start.17 = (bf16[512,512]{1,0:T(8,128)(2,1)S(1)}, bf16[512,512]{1,0:T(8,128)(2,1)S(1)}, u32[]{:S(2)}, u32[]{:S(2)}) collective-permute-start(bf16[512,512]{1,0:T(8,128)(2,1)S(1)} %get-tuple-element.80), channel_id=1, source_target_pairs={{0,192},{64,0},{128,64},{192,128},{1,193},{65,1},{129,65},{193,129... | collective-permute-start | bytes 1572872 | tf_op jit(solution)/shard_map/ppermute | solution.py:28
  95.5 19.6 %collective-permute-start.25 = (bf16[128,2048]{1,0:T(8,128)(2,1)S(1)}, bf16[128,2048]{1,0:T(8,128)(2,1)S(1)}, u32[]{:S(2)}, u32[]{:S(2)}) collective-permute-start(bf16[128,2048]{1,0:T(8,128)(2,1)S(1)} %get-tuple-element.99), channel_id=1, source_target_pairs={{0,12},{4,0},{8,4},{12,8},{1,13},{5,1},{9,5},{13,9},{2,14},{6,2},{... | collective-permute-start | bytes 1572872 | tf_op jit(solution)/shard_map/ppermute | solution.py:28
  98.5 16.6 %collective-permute-start.24 = (bf16[128,2048]{1,0:T(8,128)(2,1)S(1)}, bf16[128,2048]{1,0:T(8,128)(2,1)S(1)}, u32[]{:S(2)}, u32[]{:S(2)}) collective-permute-start(bf16[128,2048]{1,0:T(8,128)(2,1)S(1)} %get-tuple-element.97), channel_id=1, source_target_pairs={{0,4},{4,8},{8,12},{12,0},{1,5},{5,9},{9,13},{13,1},{2,6},{6,10},{... | collective-permute-start | bytes 1572872 | tf_op jit(solution)/shard_map/ppermute | solution.py:28
  103.8 12.2 %collective-permute-start.19 = (bf16[512,512]{1,0:T(8,128)(2,1)S(1)}, bf16[512,512]{1,0:T(8,128)(2,1)S(1)}, u32[]{:S(2)}, u32[]{:S(2)}) collective-permute-start(bf16[512,512]{1,0:T(8,128)(2,1)S(1)} %get-tuple-element.86), channel_id=1, source_target_pairs={{0,192},{64,0},{128,64},{192,128},{1,193},{65,1},{129,65},{193,129... | collective-permute-start | bytes 1572872 | tf_op jit(solution)/shard_map/ppermute | solution.py:28
  106.8 12.7 %collective-permute-start.18 = (bf16[512,512]{1,0:T(8,128)(2,1)S(1)}, bf16[512,512]{1,0:T(8,128)(2,1)S(1)}, u32[]{:S(2)}, u32[]{:S(2)}) collective-permute-start(bf16[512,512]{1,0:T(8,128)(2,1)S(1)} %get-tuple-element.84), channel_id=1, source_target_pairs={{0,64},{64,128},{128,192},{192,0},{1,65},{65,129},{129,193},{193,1... | collective-permute-start | bytes 1572872 | tf_op jit(solution)/shard_map/ppermute | solution.py:28
  107.0 6.5 %collective-permute-start.26 = (bf16[512,256]{1,0:T(8,128)(2,1)S(1)}, bf16[512,256]{1,0:T(8,128)(2,1)S(1)}, u32[]{:S(2)}, u32[]{:S(2)}) collective-permute-start(bf16[512,256]{1,0:T(8,128)(2,1)S(1)} %get-tuple-element.102), channel_id=1, source_target_pairs={{0,16},{16,0},{32,48},{48,32},{1,17},{17,1},{33,49},{49,33},{2,18}... | collective-permute-start | bytes 786440 | tf_op jit(solution)/shard_map/ppermute | solution.py:32
  113.5 7.3 %collective-permute-start.27 = (bf16[512,128]{1,0:T(8,128)(2,1)S(1)}, bf16[512,128]{1,0:T(8,128)(2,1)S(1)}, u32[]{:S(2)}, u32[]{:S(2)}) collective-permute-start(bf16[512,128]{1,0:T(8,128)(2,1)S(1)} %get-tuple-element.105), channel_id=1, source_target_pairs={{0,32},{16,48},{32,0},{48,16},{1,33},{17,49},{33,1},{49,17},{2,34}... | collective-permute-start | bytes 393224 | tf_op jit(solution)/shard_map/ppermute | solution.py:32
  119.7 9.3 %collective-permute-start.20 = (bf16[512,256]{1,0:T(8,128)(2,1)S(1)}, bf16[512,256]{1,0:T(8,128)(2,1)S(1)}, u32[]{:S(2)}, u32[]{:S(2)}) collective-permute-start(bf16[512,256]{1,0:T(8,128)(2,1)S(1)} %get-tuple-element.89), channel_id=1, source_target_pairs={{0,16},{16,0},{32,48},{48,32},{1,17},{17,1},{33,49},{49,33},{2,18}... | collective-permute-start | bytes 786440 | tf_op jit(solution)/shard_map/ppermute | solution.py:32
  120.8 11.7 %collective-permute-start.28 = (bf16[512,128]{1,0:T(8,128)(2,1)S(1)}, bf16[512,128]{1,0:T(8,128)(2,1)S(1)}, u32[]{:S(2)}, u32[]{:S(2)}) collective-permute-start(bf16[512,128]{1,0:T(8,128)(2,1)S(1)} %shard_map.68), channel_id=1, source_target_pairs={{0,2},{2,0},{1,3},{3,1},{4,6},{6,4},{5,7},{7,5},{8,10},{10,8},{9,1... | collective-permute-start | bytes 393224 | tf_op jit(solution)/shard_map/ppermute | solution.py:28
  129.0 6.1 %collective-permute-start.21 = (bf16[512,128]{1,0:T(8,128)(2,1)S(1)}, bf16[512,128]{1,0:T(8,128)(2,1)S(1)}, u32[]{:S(2)}, u32[]{:S(2)}) collective-permute-start(bf16[512,128]{1,0:T(8,128)(2,1)S(1)} %get-tuple-element.91), channel_id=1, source_target_pairs={{0,32},{16,48},{32,0},{48,16},{1,33},{17,49},{33,1},{49,17},{2,34}... | collective-permute-start | bytes 393224 | tf_op jit(solution)/shard_map/ppermute | solution.py:32
